TPU v7x, 128 devices: a whole 4x4x4 slice. The times are simulated.
128 devices in a mesh: site: 64 (over x, z, y_lo, core), row: 2 (over y_hi).
Axes of the slice: x: 4, y: 4 (y_hi: 2, y_lo: 2; y = y_hi * 2 + y_lo), z: 4, core: 2. Of those that a mesh axis runs over, the one named last changes fastest.
Arguments:
- tensors: bfloat16 [128, 128, 128, 2, 128], P('site', 'row'), may hold values from -40 to 40
- neighbours: int32 [128, 3], replicated, may hold values from -1 to 127, as said below
- edge_ranks: int32 [128], replicated, may hold values from 64 to 128, as said below
- gate_matrix: float32 [4, 4], replicated, may hold values from -1.2 to 1.2
- probes: float32 [512, 128], replicated, may hold values from -6 to 6
Outputs:
- new_tensors: bfloat16 [128, 128, 128, 2, 128], P('site', 'row')
- messages: float32 [128, 3, 128], P('site')
- new_bonds: float32 [128, 128], P('site')
Inputs may be any that keep to these rules, and one draw needn't show every extreme that they name: neighbours[i, 0] = i - 1 and neighbours[i, 1] = i + 1, -1 past the ends; neighbours[i, 2] is the partner of site i under this layer's gates or -1; partners are mutual, and sites 4q and 4q + 1 pair only with sites 4q + 2 or 4q + 3. `edge_ranks`: the two sites of a gated pair carry the same rank.
All inputs are finite; a program needn't handle non-finite values.
Results may differ from a plain program's by a relative error of at most 0.0085.
Values may be sent and summed in bfloat16 or wider, within the bound.
No kernel may reach another device: no remote copies, remote signals or barrier semaphores. Data moves between devices by JAX's collectives and lax.ppermute only.
A program may use at most 192 MiB of HBM per device.

v0:
```python
import functools

import jax
import jax.numpy as jnp
from jax import lax
from jax.experimental import pallas as pl
from jax.experimental.pallas import tpu as pltpu
from jax.sharding import PartitionSpec as P

ROUNDS = 4
SWEEPS = 8
F32 = jnp.float32
BF16 = jnp.bfloat16
MB = 1 << 20
highest = lax.Precision.HIGHEST

CORE, ROW, MATE0, MATE1, FIRST, LAST, KEPT, RANK, GATED = range(9)


def smem():
    return pl.BlockSpec(memory_space=pltpu.SMEM)


def vmem():
    return pl.BlockSpec(memory_space=pltpu.VMEM)


def params(mib):
    return pltpu.CompilerParams(vmem_limit_bytes=mib * MB)


def cost(flops, moved):
    return pl.CostEstimate(flops=int(flops), bytes_accessed=int(moved), transcendentals=0)


def halves(value):
    high = value.astype(BF16)
    low = (value - high.astype(F32)).astype(BF16)
    return (high, low)


def dot_of(left, right, dims=((1,), (0,))):
    return lax.dot_general(left, right, (dims, ((), ())), preferred_element_type=F32)


def dot3(left, right, dims=((1,), (0,))):
    return dot_of(left[0], right[0], dims) + (
        dot_of(left[0], right[1], dims) + dot_of(left[1], right[0], dims)
    )


def dot_high(left, right, dims=((1,), (0,))):
    return lax.dot_general(left, right, (dims, ((), ())), preferred_element_type=F32, precision=highest)


def down(row):
    size = row.shape[-1]
    return jnp.transpose(jnp.broadcast_to(row, (size, size)))


def normalized(ref):
    rows = ref[...]
    return rows / jnp.sum(rows, axis=1, keepdims=True)


def incoming(info, own, mate, side):
    bond = own.shape[-1]
    flat = jnp.full((1, bond), 1.0 / bond, F32)
    zero = jnp.zeros((1, bond), F32)
    odd = info[CORE] == 1

    def row(rows, member, leg):
        return rows[3 * member + leg : 3 * member + leg + 1]

    def from_mate(place):
        return jnp.where(place == 0, row(mate, 0, 2), row(mate, 1, 2))

    mate0, mate1 = (info[MATE0], info[MATE1])
    up0 = row(mate, 1, 1) + jnp.where(mate0 == 1, row(mate, 1, 2), zero)
    first0 = jnp.where(odd, up0, jnp.where(info[FIRST] == 1, flat, row(side, 1, 1)))
    second0 = row(own, 1, 0)
    third0 = from_mate(mate0) + jnp.where(jnp.logical_and(odd, mate0 == 1), row(mate, 1, 1), zero)
    third0 = jnp.where(mate0 < 0, flat, third0)
    first1 = row(own, 0, 1)
    down1 = row(mate, 0, 0) + jnp.where(mate1 == 0, row(mate, 0, 2), zero)
    second1 = jnp.where(odd, jnp.where(info[LAST] == 1, flat, row(side, 0, 0)), down1)
    third1 = from_mate(mate1) + jnp.where(
        jnp.logical_and(jnp.logical_not(odd), mate1 == 0), row(mate, 0, 0), zero
    )
    third1 = jnp.where(mate1 < 0, flat, third1)
    return ((first0, second0, third0), (first1, second1, third1))


def split_kernel(x_ref, d_ref, s_ref, scratch):
    rows = x_ref.shape[1]
    bond = x_ref.shape[3]

    def body(index, carry):
        slot = scratch.at[index % 2]
        slot[...] = x_ref[0, index].astype(F32)
        even = slot[pl.ds(0, bond, 2), :]
        odd = slot[pl.ds(1, bond, 2), :]
        d_ref[0, index] = jnp.concatenate([even, odd], axis=1).astype(BF16)
        s_ref[0, index] = (even * even + odd * odd).astype(BF16)
        return carry

    lax.fori_loop(0, rows, body, 0, unroll=4)


def split_call(x):
    members, rows, wide, bond = x.shape
    block = 16
    return pl.pallas_call(
        split_kernel,
        grid=(members, rows // block),
        in_specs=[pl.BlockSpec((1, block, wide, bond), lambda m, i: (m, i, 0, 0))],
        out_specs=[
            pl.BlockSpec((1, block, bond, wide), lambda m, i: (m, i, 0, 0)),
            pl.BlockSpec((1, block, bond, bond), lambda m, i: (m, i, 0, 0)),
        ],
        out_shape=[
            jax.ShapeDtypeStruct((members, rows, bond, wide), BF16),
            jax.ShapeDtypeStruct((members, rows, bond, bond), BF16),
        ],
        scratch_shapes=[pltpu.VMEM((2, wide, bond), F32)],
        compiler_params=params(16),
        cost_estimate=cost(4 * x.size, 5 * x.size),
        name="split",
    )(x)


def round_kernel(info, own_ref, mate_ref, side_ref, s_ref, out_ref, first_ref, sums_ref):
    members, rows, bond = s_ref.shape[:3]
    weights = incoming(info, normalized(own_ref), normalized(mate_ref), normalized(side_ref))
    start = info[ROW] * rows
    out_ref[...] = jnp.ones(out_ref.shape, F32)
    for member in range(members):
        first, second, third = weights[member]
        third = third.astype(BF16).astype(F32)
        first_ref[...] = down(first)
        second_down = down(second)
        outer = second_down * third

        def body(index, total):
            block = s_ref[member, index].astype(F32)
            total = total + first_ref[pl.ds(start + index, 1), :] * block
            sums_ref[index] = jnp.sum((block * outer).reshape(bond // 8, 8, bond), axis=0)
            return total

        total = lax.fori_loop(0, rows, body, jnp.zeros((bond, bond), F32), unroll=4)
        ones = jnp.ones((8, bond), F32)
        half = dot_high(ones, jnp.sum(sums_ref[...], axis=1), ((1,), (1,)))[:1]
        empty = jnp.zeros_like(half)
        toward_first = jnp.where(
            info[ROW] == 0,
            jnp.concatenate([half, empty], axis=1),
            jnp.concatenate([empty, half], axis=1),
        )
        toward_second = dot_high(jnp.broadcast_to(third, (8, bond)), total, ((1,), (1,)))[:1]
        toward_third = jnp.sum(total * second_down, axis=0, keepdims=True)
        out_ref[pl.ds(3 * member, 1), :] = toward_first
        out_ref[pl.ds(3 * member + 1, 1), :] = toward_second
        out_ref[pl.ds(3 * member + 2, 1), :] = toward_third


def round_call(info, own, mate, side, squares):
    members, rows, bond = squares.shape[:3]
    return pl.pallas_call(
        round_kernel,
        in_specs=[smem(), vmem(), vmem(), vmem(), vmem()],
        out_specs=vmem(),
        out_shape=jax.ShapeDtypeStruct((8, bond), F32),
        scratch_shapes=[pltpu.VMEM((bond, bond), F32), pltpu.VMEM((rows, 8, bond), F32)],
        compiler_params=params(12),
        cost_estimate=cost(4 * squares.size, 2 * squares.size),
        name="message_round",
    )(info, own, mate, side, squares)


def gram_kernel(info, own_ref, mate_ref, side_ref, d_ref, keep_ref, send_ref, msg_ref, first_ref, second_ref, gram):
    member, step = (pl.program_id(0), pl.program_id(1))
    block, bond = d_ref.shape[1:3]
    rows = block * pl.num_programs(1)

    @pl.when(jnp.logical_and(member == 0, step == 0))
    def prepare():
        own = normalized(own_ref)
        weights = incoming(info, own, normalized(mate_ref), normalized(side_ref))
        for place in range(2):
            first_ref[place] = jnp.sqrt(down(weights[place][0]))
            second_ref[place] = jnp.sqrt(down(weights[place][1]))
            msg_ref[place] = own[3 * place : 3 * place + 3]

    start = info[ROW] * rows + step * block
    second = second_ref[member]
    parts = []
    for index in range(block):
        scale = first_ref[member, pl.ds(start + index, 1), :] * second
        piece = d_ref[0, index].astype(F32) * jnp.concatenate([scale, scale], axis=1)
        parts.append(piece.astype(BF16))
    weighted = jnp.concatenate(parts, axis=0)
    product = dot_of(weighted, weighted, ((0,), (0,)))

    @pl.when(step == 0)
    def begin():
        gram[...] = product

    @pl.when(step != 0)
    def add():
        gram[...] += product

    def put(ref):
        ref[0] = gram[:bond, :bond]
        ref[1] = gram[:bond, bond:]
        ref[2] = gram[bond:, bond:]

    last = step == pl.num_programs(1) - 1

    @pl.when(jnp.logical_and(last, member == info[KEPT]))
    def put_keep():
        put(keep_ref)

    @pl.when(jnp.logical_and(last, member != info[KEPT]))
    def put_send():
        put(send_ref)


def gram_call(info, own, mate, side, flat):
    members, rows, bond, wide = flat.shape
    block = 8
    upper = jax.ShapeDtypeStruct((3, bond, bond), F32)
    return pl.pallas_call(
        gram_kernel,
        grid=(members, rows // block),
        in_specs=[
            smem(),
            vmem(),
            vmem(),
            vmem(),
            pl.BlockSpec((1, block, bond, wide), lambda m, i: (m, i, 0, 0)),
        ],
        out_specs=[vmem(), vmem(), vmem()],
        out_shape=[upper, upper, jax.ShapeDtypeStruct((members, 3, bond), F32)],
        scratch_shapes=[
            pltpu.VMEM((members, bond, bond), F32),
            pltpu.VMEM((members, bond, bond), F32),
            pltpu.VMEM((wide, wide), F32),
        ],
        compiler_params=params(16),
        cost_estimate=cost(2 * wide * flat.size, 2 * flat.size),
        name="gram",
    )(info, own, mate, side, flat)


def eye_mask(size):
    down_index = lax.broadcasted_iota(jnp.int32, (size, size), 0)
    across_index = lax.broadcasted_iota(jnp.int32, (size, size), 1)
    return down_index == across_index


def root_pair(matrix):
    size = matrix.shape[0]
    diagonal = eye_mask(size)
    lift = jnp.where(diagonal, 1.5, 0.0).astype(F32)
    scale = jnp.sum(jnp.where(diagonal, matrix, 0.0), keepdims=True)
    current = matrix / scale
    poly = lift - 0.5 * current
    poly_parts = halves(poly)
    current = dot3(halves(current), poly_parts)
    partner = poly
    for _ in range(SWEEPS - 1):
        current_parts, partner_parts = (halves(current), halves(partner))
        poly_parts = halves(lift - 0.5 * dot3(partner_parts, current_parts))
        current = dot3(current_parts, poly_parts)
        partner = dot3(poly_parts, partner_parts)
    root_scale = jnp.sqrt(scale)
    return (current * root_scale, partner / root_scale)


def root_kernel(keep_ref, got_ref, upper_ref, inverse_ref):
    corner = keep_ref[0] + got_ref[0]
    above = keep_ref[1] + got_ref[1]
    below = keep_ref[2] + got_ref[2]
    matrix = jnp.concatenate(
        [
            jnp.concatenate([corner, above], axis=1),
            jnp.concatenate([jnp.transpose(above), below], axis=1),
        ],
        axis=0,
    )
    upper_ref[...], inverse_ref[...] = root_pair(matrix)


def root_call(keep, got):
    wide = 2 * keep.shape[1]
    full = jax.ShapeDtypeStruct((wide, wide), F32)
    return pl.pallas_call(
        root_kernel,
        in_specs=[vmem(), vmem()],
        out_specs=[vmem(), vmem()],
        out_shape=[full, full],
        compiler_params=params(16),
        cost_estimate=cost(66 * 2 * wide**3, 16 * wide * wide),
        name="root",
    )(keep, got)


def truncate_kernel(info, gate, own_ref, mate_ref, upper_ref, inverse_ref, other_ref, probes_ref, out_ref):
    wide, bond = (upper_ref.shape[0], probes_ref.shape[1])
    odd = info[CORE] == 1
    kept = info[KEPT]
    mate_place = jnp.maximum(jnp.where(kept == 0, info[MATE0], info[MATE1]), 0)
    own_msg = own_ref[pl.ds(3 * kept + 2, 1), :]
    mate_msg = mate_ref[pl.ds(3 * mate_place + 2, 1), :]
    own_msg = own_msg / jnp.sum(own_msg, axis=1, keepdims=True)
    mate_msg = mate_msg / jnp.sum(mate_msg, axis=1, keepdims=True)
    strength = bond * jnp.sqrt(own_msg * mate_msg)
    own_upper, other_upper = (upper_ref[...], other_ref[...])
    left = jnp.where(odd, other_upper, own_upper)
    right = jnp.where(odd, own_upper, other_upper)
    left_parts = halves(
        jnp.concatenate([left[:, :bond] * strength, left[:, bond:] * strength], axis=0)
    )
    right_parts = halves(jnp.concatenate([right[:, :bond], right[:, bond:]], axis=0))
    joined = dot3(left_parts, right_parts, ((1,), (1,)))
    joined_t = dot3(right_parts, left_parts, ((1,), (1,)))

    def quarter(value, down_half, across_half):
        return value[
            down_half * wide : (down_half + 1) * wide, across_half * wide : (across_half + 1) * wide
        ]

    def mixed(value, flipped):
        block_rows = []
        for out_down in range(2):
            blocks = []
            for out_across in range(2):
                out_first, out_second = (out_across, out_down) if flipped else (out_down, out_across)
                total = None
                for first in range(2):
                    for second in range(2):
                        piece = quarter(value, second, first) if flipped else quarter(value, first, second)
                        term = gate[2 * out_first + out_second, 2 * first + second] * piece
                        total = term if total is None else total + term
                blocks.append(total)
            block_rows.append(jnp.concatenate(blocks, axis=1))
        return jnp.concatenate(block_rows, axis=0)

    theta_parts = halves(mixed(joined, False))
    theta_t_parts = halves(mixed(joined_t, True))
    across = lax.broadcasted_iota(jnp.int32, (1, bond), 1)
    mask = (across < info[RANK]).astype(F32)
    probes = jnp.concatenate(
        [probes_ref[pl.ds(0, wide, 2), :], probes_ref[pl.ds(1, wide, 2), :]], axis=0
    )
    sampled_parts = halves(dot3(theta_parts, halves(probes * mask)))
    inner = dot3(sampled_parts, sampled_parts, ((0,), (0,)))
    inner = inner + jnp.where(eye_mask(bond), 1.0 - mask, 0.0)
    _, inner_inverse = root_pair(inner)
    basis = dot3(sampled_parts, halves(inner_inverse))
    coeffs_t = dot3(theta_t_parts, halves(basis))
    new_bond = jnp.sqrt(jnp.mean(coeffs_t * coeffs_t, axis=0, keepdims=True) + 1e-06)
    target = jnp.where(odd, coeffs_t / new_bond, basis)
    target = jnp.concatenate([target[:wide], target[wide:]], axis=1)
    change = dot3(halves(inverse_ref[...]), halves(target))
    gated = info[GATED] == 1
    identity = eye_mask(wide).astype(F32)
    out_ref[:wide] = jnp.where(gated, change, identity).astype(BF16)
    bond_parts = halves(jnp.where(gated, new_bond, 0.0))
    out_ref[wide:] = jnp.broadcast_to(jnp.concatenate(bond_parts, axis=1), (16, wide))


def truncate_call(info, gate, own, mate, upper, inverse, other, probes):
    wide = upper.shape[0]
    return pl.pallas_call(
        truncate_kernel,
        in_specs=[smem(), smem()] + [vmem()] * 6,
        out_specs=vmem(),
        out_shape=jax.ShapeDtypeStruct((wide + 16, wide), BF16),
        compiler_params=params(32),
        cost_estimate=cost(40 * 2 * wide**3, 24 * wide * wide),
        name="truncate",
    )(info, gate, own, mate, upper, inverse, other, probes)


def update_kernel(info, pack_ref, got_ref, d_ref, out_ref, bond_ref, scratch):
    member, step = (pl.program_id(0), pl.program_id(1))
    block, bond, wide = d_ref.shape[1:]
    kept = info[KEPT]

    @pl.when(jnp.logical_and(member == 0, step == 0))
    def bonds():
        tail = pack_ref[wide:].astype(F32)
        got = got_ref[wide:].astype(F32)
        mine = tail[:1, :bond] + tail[:1, bond:]
        other = got[:1, :bond] + got[:1, bond:]
        bond_ref[pl.ds(0, 1), :] = jnp.where(kept == 0, mine, other)
        bond_ref[pl.ds(1, 1), :] = jnp.where(kept == 0, other, mine)

    change = jnp.where(member == kept, pack_ref[:wide].astype(F32), got_ref[:wide].astype(F32)).astype(BF16)
    for index in range(block):
        result = dot_of(d_ref[0, index], change)
        slot = scratch.at[index % 2]
        slot[pl.ds(0, bond, 2), :] = result[:, :bond]
        slot[pl.ds(1, bond, 2), :] = result[:, bond:]
        out_ref[0, index] = slot[...].astype(BF16)


def update_call(info, pack, got, flat):
    members, rows, bond, wide = flat.shape
    block = 8
    return pl.pallas_call(
        update_kernel,
        grid=(members, rows // block),
        in_specs=[
            smem(),
            vmem(),
            vmem(),
            pl.BlockSpec((1, block, bond, wide), lambda m, i: (m, i, 0, 0)),
        ],
        out_specs=[pl.BlockSpec((1, block, wide, bond), lambda m, i: (m, i, 0, 0)), vmem()],
        out_shape=[
            jax.ShapeDtypeStruct((members, rows, wide, bond), BF16),
            jax.ShapeDtypeStruct((members, bond), F32),
        ],
        scratch_shapes=[pltpu.VMEM((2, wide, bond), F32)],
        compiler_params=params(16),
        cost_estimate=cost(2 * wide * flat.size, 4 * flat.size),
        name="update",
    )(info, pack, got, flat)


def scalars(neighbours, edge_ranks):
    device = lax.axis_index("site")
    row = lax.axis_index("row")
    core = device % 2
    base = device // 2 * 4
    block = lax.dynamic_slice(neighbours[:, 2], (base,), (4,))
    local = jnp.where(block < 0, -1, block - base)
    even0, even1 = (local[0], local[1])
    mate0 = jnp.where(core == 1, local[2], jnp.where(even0 < 0, -1, even0 - 2))
    mate1 = jnp.where(core == 1, local[3], jnp.where(even1 < 0, -1, even1 - 2))
    swap = jnp.logical_or(even0 == 3, even1 == 2).astype(jnp.int32)
    kept = jnp.where(core == 1, row ^ swap, row)
    rank = lax.dynamic_index_in_dim(edge_ranks, 2 * device + kept, keepdims=False)
    gated = jnp.where(kept == 0, mate0, mate1) >= 0
    first = device == 0
    last = device == lax.axis_size("site") - 1
    values = [core, row, mate0, mate1, first, last, kept, rank, gated]
    return jnp.stack([value.astype(jnp.int32) for value in values])


def shards(tensors, neighbours, edge_ranks, gate_matrix, probes):
    members, rows, bond, phys = tensors.shape[:4]
    sites = lax.axis_size("site")
    row_swap = [(0, 1), (1, 0)]
    core_swap = [(i, i ^ 1) for i in range(sites)]
    side_swap = [(i, i + 1) for i in range(1, sites - 1, 2)]
    side_swap += [(j, i) for i, j in side_swap]
    info = scalars(neighbours, edge_ranks)
    flat, squares = split_call(tensors.reshape(members, rows, bond * phys, bond))
    own = mate = side = jnp.ones((8, bond), F32)
    for _ in range(ROUNDS):
        part = round_call(info, own, mate, side, squares)
        own = part + lax.ppermute(part, "row", row_swap)
        side = lax.ppermute(own, "site", side_swap)
        mate = lax.ppermute(own, "site", core_swap)
    keep, send, messages = gram_call(info, own, mate, side, flat)
    got = lax.ppermute(send, "row", row_swap)
    upper, inverse = root_call(keep, got)
    other = lax.ppermute(upper, "site", core_swap)
    pack = truncate_call(info, gate_matrix, own, mate, upper, inverse, other, probes)
    got_pack = lax.ppermute(pack, "row", row_swap)
    updated, bonds = update_call(info, pack, got_pack, flat)
    return (updated.reshape(tensors.shape), messages, bonds)


def solution(mesh):
    return jax.shard_map(
        shards,
        mesh=mesh,
        in_specs=(P("site", "row", None, None, None), P(), P(), P(), P()),
        out_specs=(P("site", "row", None, None, None), P("site", None, None), P("site", None)),
        check_vma=False,
    )
```

profile of v0, /device:TPU:6, one launch (start us, length us, event | category | flops | bytes accessed | tf_op | source)
XLA Modules:
  0.0 135.5 jit_solution(2037667732020312272)
XLA Ops:
  7.1 3.4 %copy-done.3 = bf16[2,64,128,2,128]{4,3,2,1,0:T(2,128)(2,1)S(1)} copy-done((bf16[2,64,128,2,128]{4,3,2,1,0:T(2,128)(2,1)S(1)}, bf16[2,64,128,2,128]{4,3,2,1,0:T(2,128)(2,1)}, u32[]{:S(2)}) %copy-start.3) | copy-done | bytes 8388632
  10.5 3.0 %split.1 = (bf16[2,64,128,256]{3,2,1,0:T(8,128)(2,1)S(1)}, bf16[2,64,128,128]{3,2,1,0:T(8,128)(2,1)S(1)}) custom-call(bf16[2,64,256,128]{3,2,1,0:T(8,128)(2,1)S(1)} %bitcast.17), custom_call_target="tpu_custom_call" | custom-call | flops 16777216 | bytes 20971520 | tf_op jit(solution)/shard_map/split/pallas_call | solution.py:113
  13.5 1.9 %copy-done = bf16[2,64,128,128]{3,2,1,0:T(8,128)(2,1)} copy-done((bf16[2,64,128,128]{3,2,1,0:T(8,128)(2,1)}, bf16[2,64,128,128]{3,2,1,0:T(8,128)(2,1)S(1)}, u32[]{:S(2)}) %copy-start) | copy-done | bytes 4194328
  15.5 3.4 %copy-done.2 = bf16[2,64,128,256]{3,2,1,0:T(8,128)(2,1)} copy-done((bf16[2,64,128,256]{3,2,1,0:T(8,128)(2,1)}, bf16[2,64,128,256]{3,2,1,0:T(8,128)(2,1)S(1)}, u32[]{:S(2)}) %copy-start.2) | copy-done | bytes 8388632
  20.2 2.2 %copy-done.1 = bf16[2,64,128,128]{3,2,1,0:T(8,128)(2,1)S(1)} copy-done((bf16[2,64,128,128]{3,2,1,0:T(8,128)(2,1)S(1)}, bf16[2,64,128,128]{3,2,1,0:T(8,128)(2,1)}, u32[]{:S(2)}) %copy-start.1) | copy-done | bytes 4194328
  22.4 3.4 %message_round.4 = f32[8,128]{1,0:T(8,128)S(1)} custom-call(s32[9]{0:T(128)S(1)} %stack.48.info, f32[8,128]{1,0:T(8,128)S(1)} %broadcast_in_dim.8.own_ref.mate_ref.side_ref, f32[8,128]{1,0:T(8,128)S(1)} %broadcast_in_dim.8.own_ref.mate_ref.side_ref, f32[8,128]{1,0:T(8,128)S(1)} %broadcast_in_dim.8.own_ref.mate_ref.side_ref, ...), custom_call_target="tpu_custom_call" | custom-call | flops 8388608 | bytes 4194304 | tf_op jit(solution)/shard_map/message_round/pallas_call | solution.py:168
  25.8 3.2 %collective-permute-start = (f32[8,128]{1,0:T(8,128)S(1)}, f32[8,128]{1,0:T(8,128)S(1)}, u32[]{:S(2)}, u32[]{:S(2)}) collective-permute-start(f32[8,128]{1,0:T(8,128)S(1)} %message_round.4), channel_id=1, source_target_pairs={{0,1},{1,0},{2,3},{3,2},{4,5},{5,4},{6,7},{7,6},{8,9},{9,8},{10,11... | collective-permute-start | bytes 12296 | tf_op jit(solution)/shard_map/ppermute | solution.py:465
  29.0 1.9 %collective-permute-done = f32[8,128]{1,0:T(8,128)S(1)} collective-permute-done((f32[8,128]{1,0:T(8,128)S(1)}, f32[8,128]{1,0:T(8,128)S(1)}, u32[]{:S(2)}, u32[]{:S(2)}) %collective-permute-start) | collective-permute-done | bytes 4128 | tf_op jit(solution)/shard_map/ppermute | solution.py:465
  30.9 5.5 %collective-permute-start.2 = (f32[8,128]{1,0:T(8,128)S(1)}, f32[8,128]{1,0:T(8,128)S(1)}, u32[]{:S(2)}, u32[]{:S(2)}) collective-permute-start(f32[8,128]{1,0:T(8,128)S(1)} %add.37.own_ref), channel_id=1, source_target_pairs={{2,4},{6,8},{10,12},{14,16},{18,20},{22,24},{26,28},{30,32},{34,36... | collective-permute-start | bytes 12296 | tf_op jit(solution)/shard_map/ppermute | solution.py:466
  36.5 2.3 %collective-permute-done.2.side_ref = f32[8,128]{1,0:T(8,128)S(1)} collective-permute-done((f32[8,128]{1,0:T(8,128)S(1)}, f32[8,128]{1,0:T(8,128)S(1)}, u32[]{:S(2)}, u32[]{:S(2)}) %collective-permute-start.2) | collective-permute-done | bytes 4128 | tf_op jit(solution)/shard_map/ppermute | solution.py:466
  38.9 3.4 %message_round.5 = f32[8,128]{1,0:T(8,128)S(1)} custom-call(s32[9]{0:T(128)S(1)} %stack.48.info, f32[8,128]{1,0:T(8,128)S(1)} %add.37.own_ref, f32[8,128]{1,0:T(8,128)S(1)} %collective-permute-done.1.mate_ref, f32[8,128]{1,0:T(8,128)S(1)} %collective-permute-done.2.side_ref, bf16[2,64,128,128]{3,2,1,0:T(8,128)(2,1)S(1)} %copy-done.1), custom_call_target="tpu_custom_call" | custom-call | flops 8388608 | bytes 4194304 | tf_op jit(solution)/shard_map/message_round/pallas_call | solution.py:168
  42.3 3.2 %collective-permute-start.3 = (f32[8,128]{1,0:T(8,128)S(1)}, f32[8,128]{1,0:T(8,128)S(1)}, u32[]{:S(2)}, u32[]{:S(2)}) collective-permute-start(f32[8,128]{1,0:T(8,128)S(1)} %message_round.5), channel_id=1, source_target_pairs={{0,1},{1,0},{2,3},{3,2},{4,5},{5,4},{6,7},{7,6},{8,9},{9,8},{10,11... | collective-permute-start | bytes 12296 | tf_op jit(solution)/shard_map/ppermute | solution.py:465
  45.5 1.9 %collective-permute-done.3 = f32[8,128]{1,0:T(8,128)S(1)} collective-permute-done((f32[8,128]{1,0:T(8,128)S(1)}, f32[8,128]{1,0:T(8,128)S(1)}, u32[]{:S(2)}, u32[]{:S(2)}) %collective-permute-start.3) | collective-permute-done | bytes 4128 | tf_op jit(solution)/shard_map/ppermute | solution.py:465
  47.4 4.6 %collective-permute-start.5 = (f32[8,128]{1,0:T(8,128)S(1)}, f32[8,128]{1,0:T(8,128)S(1)}, u32[]{:S(2)}, u32[]{:S(2)}) collective-permute-start(f32[8,128]{1,0:T(8,128)S(1)} %add.38.own_ref), channel_id=1, source_target_pairs={{2,4},{6,8},{10,12},{14,16},{18,20},{22,24},{26,28},{30,32},{34,36... | collective-permute-start | bytes 12296 | tf_op jit(solution)/shard_map/ppermute | solution.py:466
  52.1 3.5 %collective-permute-done.5.side_ref = f32[8,128]{1,0:T(8,128)S(1)} collective-permute-done((f32[8,128]{1,0:T(8,128)S(1)}, f32[8,128]{1,0:T(8,128)S(1)}, u32[]{:S(2)}, u32[]{:S(2)}) %collective-permute-start.5) | collective-permute-done | bytes 4128 | tf_op jit(solution)/shard_map/ppermute | solution.py:466
  55.6 3.4 %message_round.6 = f32[8,128]{1,0:T(8,128)S(1)} custom-call(s32[9]{0:T(128)S(1)} %stack.48.info, f32[8,128]{1,0:T(8,128)S(1)} %add.38.own_ref, f32[8,128]{1,0:T(8,128)S(1)} %collective-permute-done.4.mate_ref, f32[8,128]{1,0:T(8,128)S(1)} %collective-permute-done.5.side_ref, bf16[2,64,128,128]{3,2,1,0:T(8,128)(2,1)S(1)} %copy-done.1), custom_call_target="tpu_custom_call" | custom-call | flops 8388608 | bytes 4194304 | tf_op jit(solution)/shard_map/message_round/pallas_call | solution.py:168
  59.1 3.2 %collective-permute-start.6 = (f32[8,128]{1,0:T(8,128)S(1)}, f32[8,128]{1,0:T(8,128)S(1)}, u32[]{:S(2)}, u32[]{:S(2)}) collective-permute-start(f32[8,128]{1,0:T(8,128)S(1)} %message_round.6), channel_id=1, source_target_pairs={{0,1},{1,0},{2,3},{3,2},{4,5},{5,4},{6,7},{7,6},{8,9},{9,8},{10,11... | collective-permute-start | bytes 12296 | tf_op jit(solution)/shard_map/ppermute | solution.py:465
  62.3 1.9 %collective-permute-done.6 = f32[8,128]{1,0:T(8,128)S(1)} collective-permute-done((f32[8,128]{1,0:T(8,128)S(1)}, f32[8,128]{1,0:T(8,128)S(1)}, u32[]{:S(2)}, u32[]{:S(2)}) %collective-permute-start.6) | collective-permute-done | bytes 4128 | tf_op jit(solution)/shard_map/ppermute | solution.py:465
  64.2 3.2 %collective-permute-start.8 = (f32[8,128]{1,0:T(8,128)S(1)}, f32[8,128]{1,0:T(8,128)S(1)}, u32[]{:S(2)}, u32[]{:S(2)}) collective-permute-start(f32[8,128]{1,0:T(8,128)S(1)} %add.39.own_ref), channel_id=1, source_target_pairs={{2,4},{6,8},{10,12},{14,16},{18,20},{22,24},{26,28},{30,32},{34,36... | collective-permute-start | bytes 12296 | tf_op jit(solution)/shard_map/ppermute | solution.py:466
  67.5 4.6 %collective-permute-done.8.side_ref = f32[8,128]{1,0:T(8,128)S(1)} collective-permute-done((f32[8,128]{1,0:T(8,128)S(1)}, f32[8,128]{1,0:T(8,128)S(1)}, u32[]{:S(2)}, u32[]{:S(2)}) %collective-permute-start.8) | collective-permute-done | bytes 4128 | tf_op jit(solution)/shard_map/ppermute | solution.py:466
  72.1 3.4 %message_round.7 = f32[8,128]{1,0:T(8,128)S(1)} custom-call(s32[9]{0:T(128)S(1)} %stack.48.info, f32[8,128]{1,0:T(8,128)S(1)} %add.39.own_ref, f32[8,128]{1,0:T(8,128)S(1)} %collective-permute-done.7.mate_ref, f32[8,128]{1,0:T(8,128)S(1)} %collective-permute-done.8.side_ref, bf16[2,64,128,128]{3,2,1,0:T(8,128)(2,1)S(1)} %copy-done.1), custom_call_target="tpu_custom_call" | custom-call | flops 8388608 | bytes 4194304 | tf_op jit(solution)/shard_map/message_round/pallas_call | solution.py:168
  75.6 3.2 %collective-permute-start.9 = (f32[8,128]{1,0:T(8,128)S(1)}, f32[8,128]{1,0:T(8,128)S(1)}, u32[]{:S(2)}, u32[]{:S(2)}) collective-permute-start(f32[8,128]{1,0:T(8,128)S(1)} %message_round.7), channel_id=1, source_target_pairs={{0,1},{1,0},{2,3},{3,2},{4,5},{5,4},{6,7},{7,6},{8,9},{9,8},{10,11... | collective-permute-start | bytes 12296 | tf_op jit(solution)/shard_map/ppermute | solution.py:465
  80.7 2.1 %collective-permute-start.11 = (f32[8,128]{1,0:T(8,128)S(1)}, f32[8,128]{1,0:T(8,128)S(1)}, u32[]{:S(2)}, u32[]{:S(2)}) collective-permute-start(f32[8,128]{1,0:T(8,128)S(1)} %add.40.own_ref), channel_id=1, source_target_pairs={{2,4},{6,8},{10,12},{14,16},{18,20},{22,24},{26,28},{30,32},{34,36... | collective-permute-start | bytes 12296 | tf_op jit(solution)/shard_map/ppermute | solution.py:466
  82.9 5.8 %collective-permute-done.11.side_ref = f32[8,128]{1,0:T(8,128)S(1)} collective-permute-done((f32[8,128]{1,0:T(8,128)S(1)}, f32[8,128]{1,0:T(8,128)S(1)}, u32[]{:S(2)}, u32[]{:S(2)}) %collective-permute-start.11) | collective-permute-done | bytes 4128 | tf_op jit(solution)/shard_map/ppermute | solution.py:466
  88.7 7.7 %gram.1 = (f32[3,128,128]{2,1,0:T(8,128)S(1)}, f32[3,128,128]{2,1,0:T(8,128)S(1)}, f32[2,3,128]{2,1,0:T(4,128)S(1)}) custom-call(s32[9]{0:T(128)S(1)} %stack.48.info, f32[8,128]{1,0:T(8,128)S(1)} %add.40.own_ref, f32[8,128]{1,0:T(8,128)S(1)} %collective-permute-done.10.mate_ref, f32[8,128]{1,0:T(8,128)S(1)} %collective-permute-done.11.side_ref, ...), custom_call_target="tpu_custom_call" | custom-call | flops 2147483648 | bytes 8388608 | tf_op jit(solution)/shard_map/gram/pallas_call | solution.py:232
  96.3 3.3 %collective-permute-start.12 = (f32[3,128,128]{2,1,0:T(8,128)S(1)}, f32[3,128,128]{2,1,0:T(8,128)S(1)}, u32[]{:S(2)}, u32[]{:S(2)}) collective-permute-start(f32[3,128,128]{2,1,0:T(8,128)S(1)} %get-tuple-element.15), channel_id=1, source_target_pairs={{0,1},{1,0},{2,3},{3,2},{4,5},{5,4},{6,7},{7,6},{8,9},{9,8},{10,11... | collective-permute-start | bytes 589832 | tf_op jit(solution)/shard_map/ppermute | solution.py:469
  99.6 4.0 %collective-permute-done.12.got_ref = f32[3,128,128]{2,1,0:T(8,128)S(1)} collective-permute-done((f32[3,128,128]{2,1,0:T(8,128)S(1)}, f32[3,128,128]{2,1,0:T(8,128)S(1)}, u32[]{:S(2)}, u32[]{:S(2)}) %collective-permute-start.12) | collective-permute-done | bytes 196640 | tf_op jit(solution)/shard_map/ppermute | solution.py:469
  103.6 5.0 %root.1 = (f32[256,256]{1,0:T(8,128)S(1)}, f32[256,256]{1,0:T(8,128)S(1)}) custom-call(f32[3,128,128]{2,1,0:T(8,128)S(1)} %get-tuple-element.14.keep_ref, f32[3,128,128]{2,1,0:T(8,128)S(1)} %collective-permute-done.12.got_ref), custom_call_target="tpu_custom_call" | custom-call | flops 2214592512 | bytes 1048576 | tf_op jit(solution)/shard_map/root/pallas_call | solution.py:297
  110.5 7.3 %truncate.1.pack_ref = bf16[272,256]{1,0:T(8,128)(2,1)S(1)} custom-call(s32[9]{0:T(128)S(1)} %stack.48.info, f32[4,4]{1,0:T(4,128)S(1)} %copy-done.5, f32[8,128]{1,0:T(8,128)S(1)} %add.40.own_ref, f32[8,128]{1,0:T(8,128)S(1)} %collective-permute-done.10.mate_ref, f32[256,256]{1,0:T(8,128)S(1)} %get-tuple-element.16.upper_ref, ...), custom_call_target="tpu_custom_call" | custom-call | flops 1342177280 | bytes 1572864 | tf_op jit(solution)/shard_map/truncate/pallas_call | solution.py:375
  117.8 3.3 %collective-permute-start.14 = (bf16[272,256]{1,0:T(8,128)(2,1)S(1)}, bf16[272,256]{1,0:T(8,128)(2,1)S(1)}, u32[]{:S(2)}, u32[]{:S(2)}) collective-permute-start(bf16[272,256]{1,0:T(8,128)(2,1)S(1)} %truncate.1.pack_ref), channel_id=1, source_target_pairs={{0,1},{1,0},{2,3},{3,2},{4,5},{5,4},{6,7},{7,6},{8,9},{9,8},{10,11... | collective-permute-start | bytes 417800 | tf_op jit(solution)/shard_map/ppermute | solution.py:473
  121.6 3.4 %collective-permute-done.14.got_ref = bf16[272,256]{1,0:T(8,128)(2,1)S(1)} collective-permute-done((bf16[272,256]{1,0:T(8,128)(2,1)S(1)}, bf16[272,256]{1,0:T(8,128)(2,1)S(1)}, u32[]{:S(2)}, u32[]{:S(2)}) %collective-permute-start.14) | collective-permute-done | bytes 139296 | tf_op jit(solution)/shard_map/ppermute | solution.py:473
  125.1 10.4 %update.1 = (bf16[2,64,256,128]{3,2,1,0:T(8,128)(2,1)}, f32[2,128]{1,0:T(2,128)}) custom-call(s32[9]{0:T(128)S(1)} %stack.48.info, bf16[272,256]{1,0:T(8,128)(2,1)S(1)} %truncate.1.pack_ref, bf16[272,256]{1,0:T(8,128)(2,1)S(1)} %collective-permute-done.14.got_ref, bf16[2,64,128,256]{3,2,1,0:T(8,128)(2,1)S(1)} %bitcast.16), custom_call_target="tpu_custom_call" | custom-call | flops 2147483648 | bytes 16777216 | tf_op jit(solution)/shard_map/update/pallas_call | solution.py:412
  (37 shorter events, 7.4 us)
Async XLA Ops:
  0.6 18.2 %copy-start.6 = (s32[128]{0:T(128)S(1)}, s32[128]{0:T(128)}, u32[]{:S(2)}) copy-start(s32[128]{0:T(128)} %param.7) | copy-start | bytes 1540
  7.1 3.4 %copy-start.3 = (bf16[2,64,128,2,128]{4,3,2,1,0:T(2,128)(2,1)S(1)}, bf16[2,64,128,2,128]{4,3,2,1,0:T(2,128)(2,1)}, u32[]{:S(2)}) copy-start(bf16[2,64,128,2,128]{4,3,2,1,0:T(2,128)(2,1)} %param.5) | copy-start | bytes 25165828
  13.5 2.0 %copy-start = (bf16[2,64,128,128]{3,2,1,0:T(8,128)(2,1)}, bf16[2,64,128,128]{3,2,1,0:T(8,128)(2,1)S(1)}, u32[]{:S(2)}) copy-start(bf16[2,64,128,128]{3,2,1,0:T(8,128)(2,1)S(1)} %get-tuple-element.12.s_ref) | copy-start | bytes 12582916
  15.5 3.4 %copy-start.2 = (bf16[2,64,128,256]{3,2,1,0:T(8,128)(2,1)}, bf16[2,64,128,256]{3,2,1,0:T(8,128)(2,1)S(1)}, u32[]{:S(2)}) copy-start(bf16[2,64,128,256]{3,2,1,0:T(8,128)(2,1)S(1)} %get-tuple-element.13.d_ref) | copy-start | bytes 25165828
  20.2 2.2 %copy-start.1 = (bf16[2,64,128,128]{3,2,1,0:T(8,128)(2,1)S(1)}, bf16[2,64,128,128]{3,2,1,0:T(8,128)(2,1)}, u32[]{:S(2)}) copy-start(bf16[2,64,128,128]{3,2,1,0:T(8,128)(2,1)} %copy-done) | copy-start | bytes 12582916
  22.4 66.3 %slice-start = ((s8[8388608]{0:T(1024)(128)(4,1)}), s8[4194304]{0:T(1024)(128)(4,1)S(1)}, s32[]{:S(2)}) async-start(s8[8388608]{0:T(1024)(128)(4,1)} %bitcast.15), calls=%async_computation | async-start | bytes 8388608
  25.8 5.1 %collective-permute-start = (f32[8,128]{1,0:T(8,128)S(1)}, f32[8,128]{1,0:T(8,128)S(1)}, u32[]{:S(2)}, u32[]{:S(2)}) collective-permute-start(f32[8,128]{1,0:T(8,128)S(1)} %message_round.4), channel_id=1, source_target_pairs={{0,1},{1,0},{2,3},{3,2},{4,5},{5,4},{6,7},{7,6},{8,9},{9,8},{10,11... | collective-permute-start | bytes 12296 | tf_op jit(solution)/shard_map/ppermute | solution.py:465
  30.9 7.9 %collective-permute-start.2 = (f32[8,128]{1,0:T(8,128)S(1)}, f32[8,128]{1,0:T(8,128)S(1)}, u32[]{:S(2)}, u32[]{:S(2)}) collective-permute-start(f32[8,128]{1,0:T(8,128)S(1)} %add.37.own_ref), channel_id=1, source_target_pairs={{2,4},{6,8},{10,12},{14,16},{18,20},{22,24},{26,28},{30,32},{34,36... | collective-permute-start | bytes 12296 | tf_op jit(solution)/shard_map/ppermute | solution.py:466
  36.4 2.4 %collective-permute-start.1 = (f32[8,128]{1,0:T(8,128)S(1)}, f32[8,128]{1,0:T(8,128)S(1)}, u32[]{:S(2)}, u32[]{:S(2)}) collective-permute-start(f32[8,128]{1,0:T(8,128)S(1)} %add.37.own_ref), channel_id=1, source_target_pairs={{0,2},{2,0},{4,6},{6,4},{8,10},{10,8},{12,14},{14,12},{16,18},{18,... | collective-permute-start | bytes 12296 | tf_op jit(solution)/shard_map/ppermute | solution.py:467
  42.3 5.1 %collective-permute-start.3 = (f32[8,128]{1,0:T(8,128)S(1)}, f32[8,128]{1,0:T(8,128)S(1)}, u32[]{:S(2)}, u32[]{:S(2)}) collective-permute-start(f32[8,128]{1,0:T(8,128)S(1)} %message_round.5), channel_id=1, source_target_pairs={{0,1},{1,0},{2,3},{3,2},{4,5},{5,4},{6,7},{7,6},{8,9},{9,8},{10,11... | collective-permute-start | bytes 12296 | tf_op jit(solution)/shard_map/ppermute | solution.py:465
  47.4 41.2 %slice-start.1 = ((s8[8388608]{0:T(1024)(128)(4,1)}), s8[4194304]{0:T(1024)(128)(4,1)S(1)}, s32[]{:S(2)}) async-start(s8[8388608]{0:T(1024)(128)(4,1)} %bitcast.15), calls=%async_computation.1 | async-start | bytes 8388608
  47.4 8.2 %collective-permute-start.5 = (f32[8,128]{1,0:T(8,128)S(1)}, f32[8,128]{1,0:T(8,128)S(1)}, u32[]{:S(2)}, u32[]{:S(2)}) collective-permute-start(f32[8,128]{1,0:T(8,128)S(1)} %add.38.own_ref), channel_id=1, source_target_pairs={{2,4},{6,8},{10,12},{14,16},{18,20},{22,24},{26,28},{30,32},{34,36... | collective-permute-start | bytes 12296 | tf_op jit(solution)/shard_map/ppermute | solution.py:466
  52.0 3.6 %collective-permute-start.4 = (f32[8,128]{1,0:T(8,128)S(1)}, f32[8,128]{1,0:T(8,128)S(1)}, u32[]{:S(2)}, u32[]{:S(2)}) collective-permute-start(f32[8,128]{1,0:T(8,128)S(1)} %add.38.own_ref), channel_id=1, source_target_pairs={{0,2},{2,0},{4,6},{6,4},{8,10},{10,8},{12,14},{14,12},{16,18},{18,... | collective-permute-start | bytes 12296 | tf_op jit(solution)/shard_map/ppermute | solution.py:467
  59.1 5.1 %collective-permute-start.6 = (f32[8,128]{1,0:T(8,128)S(1)}, f32[8,128]{1,0:T(8,128)S(1)}, u32[]{:S(2)}, u32[]{:S(2)}) collective-permute-start(f32[8,128]{1,0:T(8,128)S(1)} %message_round.6), channel_id=1, source_target_pairs={{0,1},{1,0},{2,3},{3,2},{4,5},{5,4},{6,7},{7,6},{8,9},{9,8},{10,11... | collective-permute-start | bytes 12296 | tf_op jit(solution)/shard_map/ppermute | solution.py:465
  64.2 7.9 %collective-permute-start.8 = (f32[8,128]{1,0:T(8,128)S(1)}, f32[8,128]{1,0:T(8,128)S(1)}, u32[]{:S(2)}, u32[]{:S(2)}) collective-permute-start(f32[8,128]{1,0:T(8,128)S(1)} %add.39.own_ref), channel_id=1, source_target_pairs={{2,4},{6,8},{10,12},{14,16},{18,20},{22,24},{26,28},{30,32},{34,36... | collective-permute-start | bytes 12296 | tf_op jit(solution)/shard_map/ppermute | solution.py:466
  67.4 4.7 %collective-permute-start.7 = (f32[8,128]{1,0:T(8,128)S(1)}, f32[8,128]{1,0:T(8,128)S(1)}, u32[]{:S(2)}, u32[]{:S(2)}) collective-permute-start(f32[8,128]{1,0:T(8,128)S(1)} %add.39.own_ref), channel_id=1, source_target_pairs={{0,2},{2,0},{4,6},{6,4},{8,10},{10,8},{12,14},{14,12},{16,18},{18,... | collective-permute-start | bytes 12296 | tf_op jit(solution)/shard_map/ppermute | solution.py:467
  75.6 34.9 %copy-start.4 = (f32[512,128]{1,0:T(8,128)S(1)}, f32[512,128]{1,0:T(8,128)}, u32[]{:S(2)}) copy-start(f32[512,128]{1,0:T(8,128)} %probes_ref.1) | copy-start | bytes 786436
  75.6 34.9 %copy-start.5 = (f32[4,4]{1,0:T(4,128)S(1)}, f32[4,4]{1,0:T(4,128)}, u32[]{:S(2)}) copy-start(f32[4,4]{1,0:T(4,128)} %gate.1) | copy-start | bytes 196
  75.6 5.1 %collective-permute-start.9 = (f32[8,128]{1,0:T(8,128)S(1)}, f32[8,128]{1,0:T(8,128)S(1)}, u32[]{:S(2)}, u32[]{:S(2)}) collective-permute-start(f32[8,128]{1,0:T(8,128)S(1)} %message_round.7), channel_id=1, source_target_pairs={{0,1},{1,0},{2,3},{3,2},{4,5},{5,4},{6,7},{7,6},{8,9},{9,8},{10,11... | collective-permute-start | bytes 12296 | tf_op jit(solution)/shard_map/ppermute | solution.py:465
  80.7 7.9 %collective-permute-start.11 = (f32[8,128]{1,0:T(8,128)S(1)}, f32[8,128]{1,0:T(8,128)S(1)}, u32[]{:S(2)}, u32[]{:S(2)}) collective-permute-start(f32[8,128]{1,0:T(8,128)S(1)} %add.40.own_ref), channel_id=1, source_target_pairs={{2,4},{6,8},{10,12},{14,16},{18,20},{22,24},{26,28},{30,32},{34,36... | collective-permute-start | bytes 12296 | tf_op jit(solution)/shard_map/ppermute | solution.py:466
  82.8 5.9 %collective-permute-start.10 = (f32[8,128]{1,0:T(8,128)S(1)}, f32[8,128]{1,0:T(8,128)S(1)}, u32[]{:S(2)}, u32[]{:S(2)}) collective-permute-start(f32[8,128]{1,0:T(8,128)S(1)} %add.40.own_ref), channel_id=1, source_target_pairs={{0,2},{2,0},{4,6},{6,4},{8,10},{10,8},{12,14},{14,12},{16,18},{18,... | collective-permute-start | bytes 12296 | tf_op jit(solution)/shard_map/ppermute | solution.py:467
  96.3 7.3 %collective-permute-start.12 = (f32[3,128,128]{2,1,0:T(8,128)S(1)}, f32[3,128,128]{2,1,0:T(8,128)S(1)}, u32[]{:S(2)}, u32[]{:S(2)}) collective-permute-start(f32[3,128,128]{2,1,0:T(8,128)S(1)} %get-tuple-element.15), channel_id=1, source_target_pairs={{0,1},{1,0},{2,3},{3,2},{4,5},{5,4},{6,7},{7,6},{8,9},{9,8},{10,11... | collective-permute-start | bytes 589832 | tf_op jit(solution)/shard_map/ppermute | solution.py:469
  108.6 1.8 %collective-permute-start.13 = (f32[256,256]{1,0:T(8,128)S(1)}, f32[256,256]{1,0:T(8,128)S(1)}, u32[]{:S(2)}, u32[]{:S(2)}) collective-permute-start(f32[256,256]{1,0:T(8,128)S(1)} %get-tuple-element.16.upper_ref), channel_id=1, source_target_pairs={{0,2},{2,0},{4,6},{6,4},{8,10},{10,8},{12,14},{14,12},{16,18},{18,... | collective-permute-start | bytes 786440 | tf_op jit(solution)/shard_map/ppermute | solution.py:471
  117.8 7.3 %collective-permute-start.14 = (bf16[272,256]{1,0:T(8,128)(2,1)S(1)}, bf16[272,256]{1,0:T(8,128)(2,1)S(1)}, u32[]{:S(2)}, u32[]{:S(2)}) collective-permute-start(bf16[272,256]{1,0:T(8,128)(2,1)S(1)} %truncate.1.pack_ref), channel_id=1, source_target_pairs={{0,1},{1,0},{2,3},{3,2},{4,5},{5,4},{6,7},{7,6},{8,9},{9,8},{10,11... | collective-permute-start | bytes 417800 | tf_op jit(solution)/shard_map/ppermute | solution.py:473
where the time goes:
time: 136 us; the launch traced here: 135 us
  Pallas kernels  47.2 us (35%)
  starting transfers between devices  35.4 us (26%)
  waiting for transfers between devices  32.8 us (24%)
  local copies, waits for them, and re-layouts  14.2 us (10%)
  between operations  5.81 us (4%)
    ppermute x4, waiting for transfers between devices, shards(): side = lax.ppermute(own, 'site', side_swap)  16.2 us
    ppermute x4, starting transfers between devices, shards(): side = lax.ppermute(own, 'site', side_swap)  15.4 us
    pallas_call x4, Pallas kernels, round_call(): pl.pallas_call(round_kernel, in_specs=[smem(), vmem(), vmem(), vmem(), vm...  13.8 us
    ppermute x4, starting transfers between devices, shards(): own = part + lax.ppermute(part, 'row', row_swap)  12.9 us
    unnamed x19, local copies, waits for them, and re-layouts  11.5 us
    pallas_call x1, Pallas kernels, update_call(): pl.pallas_call(update_kernel, grid=(members, rows // block), in_specs=[sm...  10.4 us
    pallas_call x1, Pallas kernels, gram_call(): pl.pallas_call(gram_kernel, grid=(members, rows // block), in_specs=[smem...  7.67 us
    ppermute x4, waiting for transfers between devices, shards(): own = part + lax.ppermute(part, 'row', row_swap)  7.67 us
  transfers between devices with their start and end apart: 15, of which 11 were waited for; matrix products, arithmetic and copies ran while one was open for 0% of the time, Pallas kernels for 0%

commit v1 on v0

v1 whole, which is shorter than its diff:
```python
import functools

import jax
import jax.numpy as jnp
from jax import lax
from jax.experimental import pallas as pl
from jax.experimental.pallas import tpu as pltpu
from jax.sharding import PartitionSpec as P

ROUNDS = 4
SWEEPS = 8
F32 = jnp.float32
BF16 = jnp.bfloat16
MB = 1 << 20
highest = lax.Precision.HIGHEST

CORE, ROW, MATE0, MATE1, FIRST, LAST, KEPT, RANK, GATED = range(9)


def smem():
    return pl.BlockSpec(memory_space=pltpu.SMEM)


def vmem():
    return pl.BlockSpec(memory_space=pltpu.VMEM)


def params(mib):
    return pltpu.CompilerParams(vmem_limit_bytes=mib * MB)


def cost(flops, moved):
    return pl.CostEstimate(flops=int(flops), bytes_accessed=int(moved), transcendentals=0)


def halves(value):
    high = value.astype(BF16)
    low = (value - high.astype(F32)).astype(BF16)
    return (high, low)


def dot_of(left, right, dims=((1,), (0,))):
    return lax.dot_general(left, right, (dims, ((), ())), preferred_element_type=F32)


def dot3(left, right, dims=((1,), (0,))):
    return dot_of(left[0], right[0], dims) + (
        dot_of(left[0], right[1], dims) + dot_of(left[1], right[0], dims)
    )


def dot_high(left, right, dims=((1,), (0,))):
    return lax.dot_general(left, right, (dims, ((), ())), preferred_element_type=F32, precision=highest)


def down(row):
    size = row.shape[-1]
    return jnp.transpose(jnp.broadcast_to(row, (size, size)))


def normalized(ref):
    rows = ref[...]
    return rows / jnp.sum(rows, axis=1, keepdims=True)


def incoming(info, own, mate, side):
    bond = own.shape[-1]
    flat = jnp.full((1, bond), 1.0 / bond, F32)
    zero = jnp.zeros((1, bond), F32)
    odd = info[CORE] == 1

    def row(rows, member, leg):
        return rows[3 * member + leg : 3 * member + leg + 1]

    def from_mate(place):
        return jnp.where(place == 0, row(mate, 0, 2), row(mate, 1, 2))

    mate0, mate1 = (info[MATE0], info[MATE1])
    up0 = row(mate, 1, 1) + jnp.where(mate0 == 1, row(mate, 1, 2), zero)
    first0 = jnp.where(odd, up0, jnp.where(info[FIRST] == 1, flat, row(side, 1, 1)))
    second0 = row(own, 1, 0)
    third0 = from_mate(mate0) + jnp.where(jnp.logical_and(odd, mate0 == 1), row(mate, 1, 1), zero)
    third0 = jnp.where(mate0 < 0, flat, third0)
    first1 = row(own, 0, 1)
    down1 = row(mate, 0, 0) + jnp.where(mate1 == 0, row(mate, 0, 2), zero)
    second1 = jnp.where(odd, jnp.where(info[LAST] == 1, flat, row(side, 0, 0)), down1)
    third1 = from_mate(mate1) + jnp.where(
        jnp.logical_and(jnp.logical_not(odd), mate1 == 0), row(mate, 0, 0), zero
    )
    third1 = jnp.where(mate1 < 0, flat, third1)
    return ((first0, second0, third0), (first1, second1, third1))


def hbm():
    return pl.BlockSpec(memory_space=pltpu.HBM)


def write_scalars(near, ranks, info):
    device, row = (lax.axis_index("site"), lax.axis_index("row"))
    core = lax.rem(device, 2)
    base = 2 * (device - core)
    even0, even1 = (near[2, base] - base, near[2, base + 1] - base)
    odd0, odd1 = (near[2, base + 2], near[2, base + 3])
    odd = core == 1
    info[MATE0] = jnp.where(odd, jnp.where(odd0 < 0, -1, odd0 - base), jnp.maximum(even0 - 2, -1))
    info[MATE1] = jnp.where(odd, jnp.where(odd1 < 0, -1, odd1 - base), jnp.maximum(even1 - 2, -1))
    crossed = jnp.logical_or(even0 == 3, even1 == 2)
    kept = jnp.where(jnp.logical_and(odd, crossed), 1 - row, row)
    site = 2 * device + kept
    info[CORE] = core
    info[ROW] = row
    info[FIRST] = (device == 0).astype(jnp.int32)
    info[LAST] = (device == lax.axis_size("site") - 1).astype(jnp.int32)
    info[KEPT] = kept
    info[RANK] = ranks[site]
    info[GATED] = (near[2, site] >= 0).astype(jnp.int32)


def open_kernel(x_hbm, x_ref, s_ref, out_ref, scratch, sums_ref, total_ref, sems):
    members, rows, wide, bond = x_hbm.shape
    steps = sems.shape[0]
    per = steps // members
    block = rows // per

    def fetch(step):
        place = (step // per, pl.ds(lax.rem(step, per) * block, block))
        return pltpu.make_async_copy(x_hbm.at[place], x_ref.at[place], sems.at[step])

    for step in range(steps):
        fetch(step).start()
    total_ref[...] = jnp.zeros(total_ref.shape, F32)

    def body(step, carry):
        fetch(step).wait()
        member, start = (step // per, lax.rem(step, per) * block)
        total = total_ref[member]
        for index in range(block):
            lane = scratch.at[index % scratch.shape[0]]
            lane[...] = x_ref[member, start + index].astype(F32)
            even = lane[pl.ds(0, bond, 2), :]
            odd = lane[pl.ds(1, bond, 2), :]
            square = even * even + odd * odd
            s_ref[member, start + index] = square.astype(BF16)
            sums_ref[member, start + index] = jnp.sum(square.reshape(bond // 8, 8, bond), axis=0)
            total = total + square
        total_ref[member] = total
        return carry

    lax.fori_loop(0, steps, body, 0)
    row = lax.axis_index("row")
    flat_weight = jnp.ones((1, bond), F32)
    out_ref[...] = jnp.ones(out_ref.shape, F32)
    for member in range(members):
        finish(row, out_ref, member, sums_ref[member], total_ref[member], flat_weight, None)


def open_call(x):
    members, rows, wide, bond = x.shape
    block = 8
    steps = members * rows // block
    return pl.pallas_call(
        open_kernel,
        in_specs=[hbm()],
        out_specs=[vmem(), vmem(), vmem()],
        out_shape=[
            jax.ShapeDtypeStruct(x.shape, BF16),
            jax.ShapeDtypeStruct((members, rows, bond, bond), BF16),
            jax.ShapeDtypeStruct((8, bond), F32),
        ],
        scratch_shapes=[
            pltpu.VMEM((4, wide, bond), F32),
            pltpu.VMEM((members, rows, 8, bond), F32),
            pltpu.VMEM((members, bond, bond), F32),
            pltpu.SemaphoreType.DMA((steps,)),
        ],
        compiler_params=params(38),
        cost_estimate=cost(4 * x.size, 5 * x.size),
        name="open",
    )(x)


def flatten_kernel(after, x_ref, *refs, member):
    flat_ref, scratch = refs[-2:]
    rows, bond = flat_ref.shape[:2]
    if member == 0:
        write_scalars(*refs[:3])

    def body(index, carry):
        lane = scratch.at[lax.rem(index, scratch.shape[0])]
        lane[...] = x_ref[member, index].astype(F32)
        parts = [lane[pl.ds(place, bond, 2), :] for place in range(2)]
        flat_ref[index] = jnp.concatenate(parts, axis=1).astype(BF16)
        return carry

    lax.fori_loop(0, rows, body, 0, unroll=8)


def flatten_call(after, x, member, *tables):
    members, rows, wide, bond = x.shape
    flat = jax.ShapeDtypeStruct((rows, bond, wide), BF16)
    info = jax.ShapeDtypeStruct((16,), jnp.int32)
    return pl.pallas_call(
        functools.partial(flatten_kernel, member=member),
        in_specs=[pl.BlockSpec(memory_space=pl.ANY), vmem()] + [smem()] * len(tables),
        out_specs=[smem(), vmem()] if tables else [vmem()],
        out_shape=[info, flat] if tables else [flat],
        scratch_shapes=[pltpu.VMEM((8, wide, bond), F32)],
        compiler_params=params(8),
        cost_estimate=cost(x.size, 2 * x.size),
        name="flatten",
    )(after, x, *tables)


def finish(row_index, out_ref, member, sums, total, third, second_down):
    bond = total.shape[0]
    half = dot_high(jnp.ones((8, bond), F32), jnp.sum(sums, axis=1), ((1,), (1,)))[:1]
    empty = jnp.zeros_like(half)
    toward_first = jnp.where(
        row_index == 0,
        jnp.concatenate([half, empty], axis=1),
        jnp.concatenate([empty, half], axis=1),
    )
    toward_second = dot_high(jnp.broadcast_to(third, (8, bond)), total, ((1,), (1,)))[:1]
    weighted = total if second_down is None else total * second_down
    toward_third = jnp.sum(weighted, axis=0, keepdims=True)
    for leg, row in enumerate((toward_first, toward_second, toward_third)):
        out_ref[pl.ds(3 * member + leg, 1), :] = row


def round_kernel(info, own_ref, mate_ref, side_ref, s_ref, after, out_ref, first_ref, sums_ref):
    members, rows, bond = s_ref.shape[:3]
    group = 4
    weights = incoming(info, normalized(own_ref), normalized(mate_ref), normalized(side_ref))
    start = info[ROW] * rows
    out_ref[...] = jnp.ones(out_ref.shape, F32)
    heads = []
    for member in range(members):
        first, second, third = weights[member]
        third = third.astype(BF16).astype(F32)
        first_ref[member] = down(first)
        second_down = down(second)
        heads.append((third, second_down, (second_down * third).astype(BF16)))
    totals = []
    for member in range(members):
        outer = heads[member][2]

        def body(step, total):
            joined = None
            for place in range(group):
                index = step * group + place
                block = s_ref[member, index]
                scale = jnp.broadcast_to(first_ref[member, pl.ds(start + index, 1), :], (16, bond))
                scale = jnp.concatenate([scale.astype(BF16)] * (bond // 16), axis=0)
                term = scale * block
                joined = term if joined is None else joined + term
                piece = block * outer
                piece = piece[:64] + piece[64:]
                piece = (piece[:32] + piece[32:]).astype(F32)
                sums_ref[member, index] = (piece[:8] + piece[8:16]) + (piece[16:24] + piece[24:])
            return total + joined.astype(F32)

        totals.append(lax.fori_loop(0, rows // group, body, jnp.zeros((bond, bond), F32), unroll=2))
    for member in range(members):
        third, second_down, _ = heads[member]
        finish(info[ROW], out_ref, member, sums_ref[member], totals[member], third, second_down)


def round_call(info, own, mate, side, squares, after):
    members, rows, bond = squares.shape[:3]
    return pl.pallas_call(
        round_kernel,
        in_specs=[smem(), vmem(), vmem(), vmem(), vmem(), pl.BlockSpec(memory_space=pl.ANY)],
        out_specs=vmem(),
        out_shape=jax.ShapeDtypeStruct((8, bond), F32),
        scratch_shapes=[
            pltpu.VMEM((members, bond, bond), F32),
            pltpu.VMEM((members, rows, 8, bond), F32),
        ],
        compiler_params=params(12),
        cost_estimate=cost(4 * squares.size, 2 * squares.size),
        name="message_round",
    )(info, own, mate, side, squares, after)


def gram_kernel(info, own_ref, mate_ref, side_ref, d0_ref, d1_ref, keep_ref, send_ref, msg_ref, first_ref, second_ref, gram):
    members = 2
    rows, bond, wide = d0_ref.shape
    block = 32
    own = normalized(own_ref)
    weights = incoming(info, own, normalized(mate_ref), normalized(side_ref))
    for member in range(members):
        first_ref[member] = jnp.sqrt(down(weights[member][0]))
        second_ref[member] = jnp.sqrt(down(weights[member][1]))
        for leg in range(3):
            msg_ref[leg, pl.ds(member, 1), :] = own[3 * member + leg : 3 * member + leg + 1]
    gram[...] = jnp.zeros(gram.shape, F32)
    for member, d_ref in enumerate((d0_ref, d1_ref)):

        def body(step, carry):
            start = step * block
            second = second_ref[member]
            parts = []
            for index in range(block):
                scale = first_ref[member, pl.ds(info[ROW] * rows + start + index, 1), :] * second
                piece = d_ref[start + index].astype(F32) * jnp.concatenate([scale, scale], axis=1)
                parts.append(piece.astype(BF16))
            weighted = jnp.concatenate(parts, axis=0)
            gram[member] += dot_of(weighted, weighted, ((0,), (0,)))
            return carry

        lax.fori_loop(0, rows // block, body, 0)

    def put(ref, member):
        ref[0] = gram[member, :bond, :bond]
        ref[1] = gram[member, :bond, bond:]
        ref[2] = gram[member, bond:, bond:]

    put(keep_ref, info[KEPT])
    put(send_ref, 1 - info[KEPT])


def gram_call(info, own, mate, side, flats):
    members = len(flats)
    rows, bond, wide = flats[0].shape
    upper = jax.ShapeDtypeStruct((3, bond, bond), F32)
    return pl.pallas_call(
        gram_kernel,
        in_specs=[smem()] + [vmem()] * 5,
        out_specs=[vmem(), vmem(), vmem()],
        out_shape=[upper, upper, jax.ShapeDtypeStruct((3, members, bond), F32)],
        scratch_shapes=[
            pltpu.VMEM((members, bond, bond), F32),
            pltpu.VMEM((members, bond, bond), F32),
            pltpu.VMEM((members, wide, wide), F32),
        ],
        compiler_params=params(24),
        cost_estimate=cost(4 * wide * flats[0].size, 4 * flats[0].size),
        name="gram",
    )(info, own, mate, side, *flats)


def eye_mask(size):
    down_index = lax.broadcasted_iota(jnp.int32, (size, size), 0)
    across_index = lax.broadcasted_iota(jnp.int32, (size, size), 1)
    return down_index == across_index


def root_pair(matrix):
    size = matrix.shape[0]
    diagonal = eye_mask(size)
    lift = jnp.where(diagonal, 1.5, 0.0).astype(F32)
    scale = jnp.sum(jnp.where(diagonal, matrix, 0.0), keepdims=True)
    current = matrix / scale
    poly = lift - 0.5 * current
    poly_parts = halves(poly)
    current = dot3(halves(current), poly_parts)
    partner = poly
    for _ in range(SWEEPS - 1):
        current_parts, partner_parts = (halves(current), halves(partner))
        poly_parts = halves(lift - 0.5 * dot3(partner_parts, current_parts))
        current = dot3(current_parts, poly_parts)
        partner = dot3(poly_parts, partner_parts)
    root_scale = jnp.sqrt(scale)
    return (current * root_scale, partner / root_scale)


def root_kernel(keep_ref, got_ref, upper_ref, inverse_ref):
    corner = keep_ref[0] + got_ref[0]
    above = keep_ref[1] + got_ref[1]
    below = keep_ref[2] + got_ref[2]
    matrix = jnp.concatenate(
        [
            jnp.concatenate([corner, above], axis=1),
            jnp.concatenate([jnp.transpose(above), below], axis=1),
        ],
        axis=0,
    )
    upper_ref[...], inverse_ref[...] = root_pair(matrix)


def root_call(keep, got):
    wide = 2 * keep.shape[1]
    full = jax.ShapeDtypeStruct((wide, wide), F32)
    return pl.pallas_call(
        root_kernel,
        in_specs=[vmem(), vmem()],
        out_specs=[vmem(), vmem()],
        out_shape=[full, full],
        compiler_params=params(16),
        cost_estimate=cost(66 * 2 * wide**3, 16 * wide * wide),
        name="root",
    )(keep, got)


def truncate_kernel(info, gate, own_ref, mate_ref, upper_ref, inverse_ref, other_ref, probes_ref, out_ref):
    wide, bond = (upper_ref.shape[0], probes_ref.shape[1])
    odd = info[CORE] == 1
    kept = info[KEPT]
    mate_place = jnp.maximum(jnp.where(kept == 0, info[MATE0], info[MATE1]), 0)
    own_msg = own_ref[pl.ds(3 * kept + 2, 1), :]
    mate_msg = mate_ref[pl.ds(3 * mate_place + 2, 1), :]
    own_msg = own_msg / jnp.sum(own_msg, axis=1, keepdims=True)
    mate_msg = mate_msg / jnp.sum(mate_msg, axis=1, keepdims=True)
    strength = bond * jnp.sqrt(own_msg * mate_msg)
    own_upper, other_upper = (upper_ref[...], other_ref[...])
    left = jnp.where(odd, other_upper, own_upper)
    right = jnp.where(odd, own_upper, other_upper)
    left_parts = halves(
        jnp.concatenate([left[:, :bond] * strength, left[:, bond:] * strength], axis=0)
    )
    right_parts = halves(jnp.concatenate([right[:, :bond], right[:, bond:]], axis=0))
    joined = dot3(left_parts, right_parts, ((1,), (1,)))
    joined_t = dot3(right_parts, left_parts, ((1,), (1,)))

    def quarter(value, down_half, across_half):
        return value[
            down_half * wide : (down_half + 1) * wide, across_half * wide : (across_half + 1) * wide
        ]

    def mixed(value, flipped):
        block_rows = []
        for out_down in range(2):
            blocks = []
            for out_across in range(2):
                out_first, out_second = (out_across, out_down) if flipped else (out_down, out_across)
                total = None
                for first in range(2):
                    for second in range(2):
                        piece = quarter(value, second, first) if flipped else quarter(value, first, second)
                        term = gate[2 * out_first + out_second, 2 * first + second] * piece
                        total = term if total is None else total + term
                blocks.append(total)
            block_rows.append(jnp.concatenate(blocks, axis=1))
        return jnp.concatenate(block_rows, axis=0)

    theta_parts = halves(mixed(joined, False))
    theta_t_parts = halves(mixed(joined_t, True))
    across = lax.broadcasted_iota(jnp.int32, (1, bond), 1)
    mask = (across < info[RANK]).astype(F32)
    probes = jnp.concatenate(
        [probes_ref[pl.ds(0, wide, 2), :], probes_ref[pl.ds(1, wide, 2), :]], axis=0
    )
    sampled_parts = halves(dot3(theta_parts, halves(probes * mask)))
    inner = dot3(sampled_parts, sampled_parts, ((0,), (0,)))
    inner = inner + jnp.where(eye_mask(bond), 1.0 - mask, 0.0)
    _, inner_inverse = root_pair(inner)
    basis = dot3(sampled_parts, halves(inner_inverse))
    coeffs_t = dot3(theta_t_parts, halves(basis))
    new_bond = jnp.sqrt(jnp.mean(coeffs_t * coeffs_t, axis=0, keepdims=True) + 1e-06)
    target = jnp.where(odd, coeffs_t / new_bond, basis)
    target = jnp.concatenate([target[:wide], target[wide:]], axis=1)
    change = dot3(halves(inverse_ref[...]), halves(target))
    gated = info[GATED] == 1
    identity = eye_mask(wide).astype(F32)
    out_ref[:wide] = jnp.where(gated, change, identity).astype(BF16)
    bond_parts = halves(jnp.where(gated, new_bond, 0.0))
    out_ref[wide:] = jnp.broadcast_to(jnp.concatenate(bond_parts, axis=1), (16, wide))


def truncate_call(info, gate, own, mate, upper, inverse, other, probes):
    wide = upper.shape[0]
    return pl.pallas_call(
        truncate_kernel,
        in_specs=[smem(), smem()] + [vmem()] * 6,
        out_specs=vmem(),
        out_shape=jax.ShapeDtypeStruct((wide + 16, wide), BF16),
        compiler_params=params(32),
        cost_estimate=cost(40 * 2 * wide**3, 24 * wide * wide),
        name="truncate",
    )(info, gate, own, mate, upper, inverse, other, probes)


def update_kernel(info, pack_ref, got_ref, d0_ref, d1_ref, out_hbm, bond_ref, held, scratch, sems):
    rows, bond, wide = d0_ref.shape
    slots, block = held.shape[:2]
    per = rows // block
    kept = info[KEPT]
    tail = pack_ref[wide:].astype(F32)
    got = got_ref[wide:].astype(F32)
    mine = tail[:1, :bond] + tail[:1, bond:]
    other = got[:1, :bond] + got[:1, bond:]
    bond_ref[pl.ds(0, 1), :] = jnp.where(kept == 0, mine, other)
    bond_ref[pl.ds(1, 1), :] = jnp.where(kept == 0, other, mine)

    def put(member, step):
        slot = lax.rem(member * per + step, slots)
        target = out_hbm.at[member, pl.ds(step * block, block)]
        return pltpu.make_async_copy(held.at[slot], target, sems.at[slot])

    for member, d_ref in enumerate((d0_ref, d1_ref)):
        change = jnp.where(member == kept, pack_ref[:wide].astype(F32), got_ref[:wide].astype(F32)).astype(BF16)

        def body(step, carry):
            start = step * block
            slot = lax.rem(member * per + step, slots)

            @pl.when(member * per + step >= slots)
            def free():
                put(member, step).wait()

            result = dot_of(d_ref[pl.ds(start, block)].reshape(block * bond, wide), change)
            for index in range(block):
                lane = scratch.at[index % scratch.shape[0]]
                piece = result[index * bond : (index + 1) * bond]
                lane[pl.ds(0, bond, 2), :] = piece[:, :bond]
                lane[pl.ds(1, bond, 2), :] = piece[:, bond:]
                held[slot, index] = lane[...].astype(BF16)
            put(member, step).start()
            return carry

        lax.fori_loop(0, per, body, 0)
    for step in range(per - slots, per):
        put(1, step).wait()


def update_call(info, pack, got, flats):
    members = len(flats)
    rows, bond, wide = flats[0].shape
    block, slots = (16, 4)
    return pl.pallas_call(
        update_kernel,
        in_specs=[smem()] + [vmem()] * 4,
        out_specs=[hbm(), vmem()],
        out_shape=[
            jax.ShapeDtypeStruct((members, rows, wide, bond), BF16),
            jax.ShapeDtypeStruct((members, bond), F32),
        ],
        scratch_shapes=[
            pltpu.VMEM((slots, block, wide, bond), BF16),
            pltpu.VMEM((4, wide, bond), F32),
            pltpu.SemaphoreType.DMA((slots,)),
        ],
        compiler_params=params(24),
        cost_estimate=cost(4 * wide * flats[0].size, 8 * flats[0].size),
        name="update",
    )(info, pack, got, *flats)


def shards(tensors, neighbours, edge_ranks, gate_matrix, probes):
    members, rows, bond, phys = tensors.shape[:4]
    sites = lax.axis_size("site")
    row_swap = [(0, 1), (1, 0)]
    core_swap = [(i, i ^ 1) for i in range(sites)]
    side_swap = [(i, i + 1) for i in range(1, sites - 1, 2)]
    side_swap += [(j, i) for i, j in side_swap]
    x = tensors.reshape(members, rows, bond * phys, bond)
    x, squares, part = open_call(x)
    for index in range(ROUNDS):
        if index > 0:
            part = round_call(info, own, mate, side, squares, flats[-1])
        if index == 0:
            info, *flats = flatten_call(part, x, index, neighbours.T, edge_ranks)
        elif index < members:
            flats += flatten_call(part, x, index)
        own = part + lax.ppermute(part, "row", row_swap)
        side = lax.ppermute(own, "site", side_swap)
        mate = lax.ppermute(own, "site", core_swap)
    keep, send, messages = gram_call(info, own, mate, side, flats)
    got = lax.ppermute(send, "row", row_swap)
    upper, inverse = root_call(keep, got)
    other = lax.ppermute(upper, "site", core_swap)
    pack = truncate_call(info, gate_matrix, own, mate, upper, inverse, other, probes)
    got_pack = lax.ppermute(pack, "row", row_swap)
    updated, bonds = update_call(info, pack, got_pack, flats)
    return (updated.reshape(tensors.shape), messages.transpose(1, 0, 2), bonds)


def solution(mesh):
    return jax.shard_map(
        shards,
        mesh=mesh,
        in_specs=(P("site", "row", None, None, None), P(), P(), P(), P()),
        out_specs=(P("site", "row", None, None, None), P("site", None, None), P("site", None)),
        check_vma=False,
    )
```

time: 136 us -> 105 us (0.77)
  local copies, waits for them, and re-layouts: 14.2 us -> 0.02 us
  Pallas kernels: 47.2 us -> 39.1 us
  between operations: 5.81 us -> 0.97 us
  waiting for transfers between devices: 32.8 us -> 30.4 us
    unnamed x19 -> x8, local copies, waits for them, and re-layouts: 11.5 us -> 0.02 us
    pallas_call x4 -> x3, Pallas kernels: 13.8 us -> 7.49 us  [round_call(): pl.pallas_call(round_kernel, in_specs=[smem(), vmem(), vmem(), vmem(), vm...]
    ppermute x4, waiting for transfers between devices: 16.2 us -> 12.9 us  [shards(): side = lax.ppermute(own, 'site', side_swap)]
    pallas_call x3 -> x5, Pallas kernels: 21.1 us -> 19.2 us  [the longest x1 6.98 us: update_call(): pl.pallas_call(update_kernel, in_specs=[smem()] + [vmem()] * 4, out_specs...]
  transfers between devices with their start and end apart: 15 -> 15, of which waited for: 11 -> 10; matrix products, arithmetic and copies ran while one was open for 0% -> 0% of each run, Pallas kernels for 0% -> 3%
where the time goes in v1:
time: 105 us
  Pallas kernels  39.1 us (37%)
  starting transfers between devices  34.8 us (33%)
  waiting for transfers between devices  30.4 us (29%)
    ppermute x4, starting transfers between devices, shards(): side = lax.ppermute(own, 'site', side_swap)  14.9 us
    ppermute x4, waiting for transfers between devices, shards(): side = lax.ppermute(own, 'site', side_swap)  12.9 us
    ppermute x4, starting transfers between devices, shards(): own = part + lax.ppermute(part, 'row', row_swap)  12.8 us
    ppermute x4, waiting for transfers between devices, shards(): own = part + lax.ppermute(part, 'row', row_swap)  7.84 us
    pallas_call x3, Pallas kernels, round_call(): pl.pallas_call(round_kernel, in_specs=[smem(), vmem(), vmem(), vmem(), vm...  7.49 us
    pallas_call x1, Pallas kernels, truncate_call(): pl.pallas_call(truncate_kernel, in_specs=[smem(), smem()] + [vmem()] * 6,...  7.31 us
    pallas_call x1, Pallas kernels, update_call(): pl.pallas_call(update_kernel, in_specs=[smem()] + [vmem()] * 4, out_specs...  6.98 us
    pallas_call x1, Pallas kernels, root_call(): pl.pallas_call(root_kernel, in_specs=[vmem(), vmem()], out_specs=[vmem(),...  5.05 us
  transfers between devices with their start and end apart: 15, of which 10 were waited for; matrix products, arithmetic and copies ran while one was open for 0% of the time, Pallas kernels for 3%

profile of v1, /device:TPU:6, one launch (start us, length us, event | category | flops | bytes accessed | tf_op | source)
XLA Modules:
  0.0 105.2 jit_solution(2840226367768885046)
XLA Ops:
  0.7 4.6 %open.1 = (bf16[2,64,256,128]{3,2,1,0:T(8,128)(2,1)S(1)}, bf16[2,64,128,128]{3,2,1,0:T(8,128)(2,1)S(1)}, f32[8,128]{1,0:T(8,128)S(1)}) custom-call(bf16[2,64,256,128]{3,2,1,0:T(8,128)(2,1)} %bitcast.5), custom_call_target="tpu_custom_call" | custom-call | flops 16777216 | bytes 20971520 | tf_op jit(solution)/shard_map/open/pallas_call | solution.py:161
  5.3 3.3 %collective-permute-start = (f32[8,128]{1,0:T(8,128)S(1)}, f32[8,128]{1,0:T(8,128)S(1)}, u32[]{:S(2)}, u32[]{:S(2)}) collective-permute-start(f32[8,128]{1,0:T(8,128)S(1)} %get-tuple-element.15.after), channel_id=1, source_target_pairs={{0,1},{1,0},{2,3},{3,2},{4,5},{5,4},{6,7},{7,6},{8,9},{9,8},{10,11... | collective-permute-start | bytes 12296 | tf_op jit(solution)/shard_map/ppermute | solution.py:555
  8.6 1.9 %collective-permute-done = f32[8,128]{1,0:T(8,128)S(1)} collective-permute-done((f32[8,128]{1,0:T(8,128)S(1)}, f32[8,128]{1,0:T(8,128)S(1)}, u32[]{:S(2)}, u32[]{:S(2)}) %collective-permute-start) | collective-permute-done | bytes 4128 | tf_op jit(solution)/shard_map/ppermute | solution.py:555
  10.5 5.5 %collective-permute-start.2 = (f32[8,128]{1,0:T(8,128)S(1)}, f32[8,128]{1,0:T(8,128)S(1)}, u32[]{:S(2)}, u32[]{:S(2)}) collective-permute-start(f32[8,128]{1,0:T(8,128)S(1)} %add.12.own_ref), channel_id=1, source_target_pairs={{2,4},{6,8},{10,12},{14,16},{18,20},{22,24},{26,28},{30,32},{34,36... | collective-permute-start | bytes 12296 | tf_op jit(solution)/shard_map/ppermute | solution.py:556
  16.1 2.3 %flatten.2 = (s32[16]{0:T(128)S(1)}, bf16[64,128,256]{2,1,0:T(8,128)(2,1)S(1)}) custom-call(f32[8,128]{1,0:T(8,128)S(1)} %get-tuple-element.15.after, bf16[2,64,256,128]{3,2,1,0:T(8,128)(2,1)S(1)} %get-tuple-element.16.x_ref, s32[3,128]{1,0:T(4,128)S(1)} %bitcast.4, s32[128]{0:T(128)S(1)} %copy-done.1), custom_call_target="tpu_custom_call" | custom-call | flops 4194304 | bytes 8388608 | tf_op jit(solution)/shard_map/flatten/pallas_call | solution.py:202
  18.5 2.5 %message_round.3.after = f32[8,128]{1,0:T(8,128)S(1)} custom-call(s32[16]{0:T(128)S(1)} %get-tuple-element.17.info, f32[8,128]{1,0:T(8,128)S(1)} %add.12.own_ref, f32[8,128]{1,0:T(8,128)S(1)} %collective-permute-done.1.mate_ref, f32[8,128]{1,0:T(8,128)S(1)} %collective-permute-done.2.side_ref, bf16[2,64,128,128]{3,2,1,0:T(8,128)(2,1)S(1)} %get-tuple-element.18.s_ref, ...), custom_call_target="tpu_custom_call" | custom-call | flops 8388608 | bytes 4194304 | tf_op jit(solution)/shard_map/message_round/pallas_call | solution.py:270
  21.0 3.2 %collective-permute-start.3 = (f32[8,128]{1,0:T(8,128)S(1)}, f32[8,128]{1,0:T(8,128)S(1)}, u32[]{:S(2)}, u32[]{:S(2)}) collective-permute-start(f32[8,128]{1,0:T(8,128)S(1)} %message_round.3.after), channel_id=1, source_target_pairs={{0,1},{1,0},{2,3},{3,2},{4,5},{5,4},{6,7},{7,6},{8,9},{9,8},{10,11... | collective-permute-start | bytes 12296 | tf_op jit(solution)/shard_map/ppermute | solution.py:555
  24.1 2.0 %collective-permute-done.3 = f32[8,128]{1,0:T(8,128)S(1)} collective-permute-done((f32[8,128]{1,0:T(8,128)S(1)}, f32[8,128]{1,0:T(8,128)S(1)}, u32[]{:S(2)}, u32[]{:S(2)}) %collective-permute-start.3) | collective-permute-done | bytes 4128 | tf_op jit(solution)/shard_map/ppermute | solution.py:555
  26.1 4.3 %collective-permute-start.5 = (f32[8,128]{1,0:T(8,128)S(1)}, f32[8,128]{1,0:T(8,128)S(1)}, u32[]{:S(2)}, u32[]{:S(2)}) collective-permute-start(f32[8,128]{1,0:T(8,128)S(1)} %add.13.own_ref), channel_id=1, source_target_pairs={{2,4},{6,8},{10,12},{14,16},{18,20},{22,24},{26,28},{30,32},{34,36... | collective-permute-start | bytes 12296 | tf_op jit(solution)/shard_map/ppermute | solution.py:556
  30.5 1.2 %flatten.3.after.d1_ref = bf16[64,128,256]{2,1,0:T(8,128)(2,1)S(1)} custom-call(f32[8,128]{1,0:T(8,128)S(1)} %message_round.3.after, bf16[2,64,256,128]{3,2,1,0:T(8,128)(2,1)S(1)} %get-tuple-element.16.x_ref), custom_call_target="tpu_custom_call" | custom-call | flops 4194304 | bytes 8388608 | tf_op jit(solution)/shard_map/flatten/pallas_call | solution.py:202
  31.7 2.3 %collective-permute-done.5.side_ref = f32[8,128]{1,0:T(8,128)S(1)} collective-permute-done((f32[8,128]{1,0:T(8,128)S(1)}, f32[8,128]{1,0:T(8,128)S(1)}, u32[]{:S(2)}, u32[]{:S(2)}) %collective-permute-start.5) | collective-permute-done | bytes 4128 | tf_op jit(solution)/shard_map/ppermute | solution.py:556
  34.0 2.5 %message_round.4 = f32[8,128]{1,0:T(8,128)S(1)} custom-call(s32[16]{0:T(128)S(1)} %get-tuple-element.17.info, f32[8,128]{1,0:T(8,128)S(1)} %add.13.own_ref, f32[8,128]{1,0:T(8,128)S(1)} %collective-permute-done.4.mate_ref, f32[8,128]{1,0:T(8,128)S(1)} %collective-permute-done.5.side_ref, bf16[2,64,128,128]{3,2,1,0:T(8,128)(2,1)S(1)} %get-tuple-element.18.s_ref, ...), custom_call_target="tpu_custom_call" | custom-call | flops 8388608 | bytes 4194304 | tf_op jit(solution)/shard_map/message_round/pallas_call | solution.py:270
  36.5 3.2 %collective-permute-start.6 = (f32[8,128]{1,0:T(8,128)S(1)}, f32[8,128]{1,0:T(8,128)S(1)}, u32[]{:S(2)}, u32[]{:S(2)}) collective-permute-start(f32[8,128]{1,0:T(8,128)S(1)} %message_round.4), channel_id=1, source_target_pairs={{0,1},{1,0},{2,3},{3,2},{4,5},{5,4},{6,7},{7,6},{8,9},{9,8},{10,11... | collective-permute-start | bytes 12296 | tf_op jit(solution)/shard_map/ppermute | solution.py:555
  39.7 2.0 %collective-permute-done.6 = f32[8,128]{1,0:T(8,128)S(1)} collective-permute-done((f32[8,128]{1,0:T(8,128)S(1)}, f32[8,128]{1,0:T(8,128)S(1)}, u32[]{:S(2)}, u32[]{:S(2)}) %collective-permute-start.6) | collective-permute-done | bytes 4128 | tf_op jit(solution)/shard_map/ppermute | solution.py:555
  41.7 3.1 %collective-permute-start.8 = (f32[8,128]{1,0:T(8,128)S(1)}, f32[8,128]{1,0:T(8,128)S(1)}, u32[]{:S(2)}, u32[]{:S(2)}) collective-permute-start(f32[8,128]{1,0:T(8,128)S(1)} %add.14.own_ref), channel_id=1, source_target_pairs={{2,4},{6,8},{10,12},{14,16},{18,20},{22,24},{26,28},{30,32},{34,36... | collective-permute-start | bytes 12296 | tf_op jit(solution)/shard_map/ppermute | solution.py:556
  44.8 0.1 collective-permute-start.7
  44.9 4.7 %collective-permute-done.8.side_ref = f32[8,128]{1,0:T(8,128)S(1)} collective-permute-done((f32[8,128]{1,0:T(8,128)S(1)}, f32[8,128]{1,0:T(8,128)S(1)}, u32[]{:S(2)}, u32[]{:S(2)}) %collective-permute-start.8) | collective-permute-done | bytes 4128 | tf_op jit(solution)/shard_map/ppermute | solution.py:556
  49.6 2.5 %message_round.5 = f32[8,128]{1,0:T(8,128)S(1)} custom-call(s32[16]{0:T(128)S(1)} %get-tuple-element.17.info, f32[8,128]{1,0:T(8,128)S(1)} %add.14.own_ref, f32[8,128]{1,0:T(8,128)S(1)} %collective-permute-done.7.mate_ref, f32[8,128]{1,0:T(8,128)S(1)} %collective-permute-done.8.side_ref, bf16[2,64,128,128]{3,2,1,0:T(8,128)(2,1)S(1)} %get-tuple-element.18.s_ref, ...), custom_call_target="tpu_custom_call" | custom-call | flops 8388608 | bytes 4194304 | tf_op jit(solution)/shard_map/message_round/pallas_call | solution.py:270
  52.1 3.2 %collective-permute-start.9 = (f32[8,128]{1,0:T(8,128)S(1)}, f32[8,128]{1,0:T(8,128)S(1)}, u32[]{:S(2)}, u32[]{:S(2)}) collective-permute-start(f32[8,128]{1,0:T(8,128)S(1)} %message_round.5), channel_id=1, source_target_pairs={{0,1},{1,0},{2,3},{3,2},{4,5},{5,4},{6,7},{7,6},{8,9},{9,8},{10,11... | collective-permute-start | bytes 12296 | tf_op jit(solution)/shard_map/ppermute | solution.py:555
  55.3 2.0 %collective-permute-done.9 = f32[8,128]{1,0:T(8,128)S(1)} collective-permute-done((f32[8,128]{1,0:T(8,128)S(1)}, f32[8,128]{1,0:T(8,128)S(1)}, u32[]{:S(2)}, u32[]{:S(2)}) %collective-permute-start.9) | collective-permute-done | bytes 4128 | tf_op jit(solution)/shard_map/ppermute | solution.py:555
  57.3 2.0 %collective-permute-start.11 = (f32[8,128]{1,0:T(8,128)S(1)}, f32[8,128]{1,0:T(8,128)S(1)}, u32[]{:S(2)}, u32[]{:S(2)}) collective-permute-start(f32[8,128]{1,0:T(8,128)S(1)} %add.15.own_ref), channel_id=1, source_target_pairs={{2,4},{6,8},{10,12},{14,16},{18,20},{22,24},{26,28},{30,32},{34,36... | collective-permute-start | bytes 12296 | tf_op jit(solution)/shard_map/ppermute | solution.py:556
  59.4 5.9 %collective-permute-done.11.side_ref = f32[8,128]{1,0:T(8,128)S(1)} collective-permute-done((f32[8,128]{1,0:T(8,128)S(1)}, f32[8,128]{1,0:T(8,128)S(1)}, u32[]{:S(2)}, u32[]{:S(2)}) %collective-permute-start.11) | collective-permute-done | bytes 4128 | tf_op jit(solution)/shard_map/ppermute | solution.py:556
  65.3 4.1 %gram.1 = (f32[3,128,128]{2,1,0:T(8,128)S(1)}, f32[3,128,128]{2,1,0:T(8,128)S(1)}, f32[3,2,128]{2,1,0:T(2,128)}) custom-call(s32[16]{0:T(128)S(1)} %get-tuple-element.17.info, f32[8,128]{1,0:T(8,128)S(1)} %add.15.own_ref, f32[8,128]{1,0:T(8,128)S(1)} %collective-permute-done.10.mate_ref, f32[8,128]{1,0:T(8,128)S(1)} %collective-permute-done.11.side_ref, ...), custom_call_target="tpu_custom_call" | custom-call | flops 2147483648 | bytes 8388608 | tf_op jit(solution)/shard_map/gram/pallas_call | solution.py:326
  69.4 3.2 %collective-permute-start.12 = (f32[3,128,128]{2,1,0:T(8,128)S(1)}, f32[3,128,128]{2,1,0:T(8,128)S(1)}, u32[]{:S(2)}, u32[]{:S(2)}) collective-permute-start(f32[3,128,128]{2,1,0:T(8,128)S(1)} %get-tuple-element.21), channel_id=1, source_target_pairs={{0,1},{1,0},{2,3},{3,2},{4,5},{5,4},{6,7},{7,6},{8,9},{9,8},{10,11... | collective-permute-start | bytes 589832 | tf_op jit(solution)/shard_map/ppermute | solution.py:559
  72.6 4.0 %collective-permute-done.12.got_ref = f32[3,128,128]{2,1,0:T(8,128)S(1)} collective-permute-done((f32[3,128,128]{2,1,0:T(8,128)S(1)}, f32[3,128,128]{2,1,0:T(8,128)S(1)}, u32[]{:S(2)}, u32[]{:S(2)}) %collective-permute-start.12) | collective-permute-done | bytes 196640 | tf_op jit(solution)/shard_map/ppermute | solution.py:559
  76.6 5.1 %root.1 = (f32[256,256]{1,0:T(8,128)S(1)}, f32[256,256]{1,0:T(8,128)S(1)}) custom-call(f32[3,128,128]{2,1,0:T(8,128)S(1)} %get-tuple-element.20.keep_ref, f32[3,128,128]{2,1,0:T(8,128)S(1)} %collective-permute-done.12.got_ref), custom_call_target="tpu_custom_call" | custom-call | flops 2214592512 | bytes 1048576 | tf_op jit(solution)/shard_map/root/pallas_call | solution.py:384
  81.7 0.3 collective-permute-start.13
  82.0 1.5 %collective-permute-done.13.other_ref = f32[256,256]{1,0:T(8,128)S(1)} collective-permute-done((f32[256,256]{1,0:T(8,128)S(1)}, f32[256,256]{1,0:T(8,128)S(1)}, u32[]{:S(2)}, u32[]{:S(2)}) %collective-permute-start.13) | collective-permute-done | bytes 262176 | tf_op jit(solution)/shard_map/ppermute | solution.py:561
  83.5 7.3 %truncate.1.pack_ref = bf16[272,256]{1,0:T(8,128)(2,1)S(1)} custom-call(s32[16]{0:T(128)S(1)} %get-tuple-element.17.info, f32[4,4]{1,0:T(4,128)S(1)} %copy-done.3, f32[8,128]{1,0:T(8,128)S(1)} %add.15.own_ref, f32[8,128]{1,0:T(8,128)S(1)} %collective-permute-done.10.mate_ref, f32[256,256]{1,0:T(8,128)S(1)} %get-tuple-element.22.upper_ref, ...), custom_call_target="tpu_custom_call" | custom-call | flops 1342177280 | bytes 1572864 | tf_op jit(solution)/shard_map/truncate/pallas_call | solution.py:462
  90.8 3.2 %collective-permute-start.14 = (bf16[272,256]{1,0:T(8,128)(2,1)S(1)}, bf16[272,256]{1,0:T(8,128)(2,1)S(1)}, u32[]{:S(2)}, u32[]{:S(2)}) collective-permute-start(bf16[272,256]{1,0:T(8,128)(2,1)S(1)} %truncate.1.pack_ref), channel_id=1, source_target_pairs={{0,1},{1,0},{2,3},{3,2},{4,5},{5,4},{6,7},{7,6},{8,9},{9,8},{10,11... | collective-permute-start | bytes 417800 | tf_op jit(solution)/shard_map/ppermute | solution.py:563
  94.0 4.1 %collective-permute-done.14.got_ref = bf16[272,256]{1,0:T(8,128)(2,1)S(1)} collective-permute-done((bf16[272,256]{1,0:T(8,128)(2,1)S(1)}, bf16[272,256]{1,0:T(8,128)(2,1)S(1)}, u32[]{:S(2)}, u32[]{:S(2)}) %collective-permute-start.14) | collective-permute-done | bytes 139296 | tf_op jit(solution)/shard_map/ppermute | solution.py:563
  98.1 7.0 %update.1 = (bf16[2,64,256,128]{3,2,1,0:T(8,128)(2,1)}, f32[2,128]{1,0:T(2,128)}) custom-call(s32[16]{0:T(128)S(1)} %get-tuple-element.17.info, bf16[272,256]{1,0:T(8,128)(2,1)S(1)} %truncate.1.pack_ref, bf16[272,256]{1,0:T(8,128)(2,1)S(1)} %collective-permute-done.14.got_ref, bf16[64,128,256]{2,1,0:T(8,128)(2,1)S(1)} %get-tuple-element.19.after.d0_ref, ...), custom_call_target="tpu_custom_call" | custom-call | flops 2147483648 | bytes 16777216 | tf_op jit(solution)/shard_map/update/pallas_call | solution.py:520
  (20 shorter events, 0.3 us)
Async XLA Ops:
  0.6 15.5 %copy-start.1 = (s32[128]{0:T(128)S(1)}, s32[128]{0:T(128)}, u32[]{:S(2)}) copy-start(s32[128]{0:T(128)} %refs_1_.1) | copy-start | bytes 1540
  0.6 15.5 %copy-start = (s32[128,3]{0,1:T(4,128)S(1)}, s32[128,3]{0,1:T(4,128)}, u32[]{:S(2)}) copy-start(s32[128,3]{0,1:T(4,128)} %param.6) | copy-start | bytes 4612
  5.3 5.2 %collective-permute-start = (f32[8,128]{1,0:T(8,128)S(1)}, f32[8,128]{1,0:T(8,128)S(1)}, u32[]{:S(2)}, u32[]{:S(2)}) collective-permute-start(f32[8,128]{1,0:T(8,128)S(1)} %get-tuple-element.15.after), channel_id=1, source_target_pairs={{0,1},{1,0},{2,3},{3,2},{4,5},{5,4},{6,7},{7,6},{8,9},{9,8},{10,11... | collective-permute-start | bytes 12296 | tf_op jit(solution)/shard_map/ppermute | solution.py:555
  10.5 8.0 %collective-permute-start.2 = (f32[8,128]{1,0:T(8,128)S(1)}, f32[8,128]{1,0:T(8,128)S(1)}, u32[]{:S(2)}, u32[]{:S(2)}) collective-permute-start(f32[8,128]{1,0:T(8,128)S(1)} %add.12.own_ref), channel_id=1, source_target_pairs={{2,4},{6,8},{10,12},{14,16},{18,20},{22,24},{26,28},{30,32},{34,36... | collective-permute-start | bytes 12296 | tf_op jit(solution)/shard_map/ppermute | solution.py:556
  16.0 2.5 %collective-permute-start.1 = (f32[8,128]{1,0:T(8,128)S(1)}, f32[8,128]{1,0:T(8,128)S(1)}, u32[]{:S(2)}, u32[]{:S(2)}) collective-permute-start(f32[8,128]{1,0:T(8,128)S(1)} %add.12.own_ref), channel_id=1, source_target_pairs={{0,2},{2,0},{4,6},{6,4},{8,10},{10,8},{12,14},{14,12},{16,18},{18,... | collective-permute-start | bytes 12296 | tf_op jit(solution)/shard_map/ppermute | solution.py:557
  21.0 5.1 %collective-permute-start.3 = (f32[8,128]{1,0:T(8,128)S(1)}, f32[8,128]{1,0:T(8,128)S(1)}, u32[]{:S(2)}, u32[]{:S(2)}) collective-permute-start(f32[8,128]{1,0:T(8,128)S(1)} %message_round.3.after), channel_id=1, source_target_pairs={{0,1},{1,0},{2,3},{3,2},{4,5},{5,4},{6,7},{7,6},{8,9},{9,8},{10,11... | collective-permute-start | bytes 12296 | tf_op jit(solution)/shard_map/ppermute | solution.py:555
  26.1 7.9 %collective-permute-start.5 = (f32[8,128]{1,0:T(8,128)S(1)}, f32[8,128]{1,0:T(8,128)S(1)}, u32[]{:S(2)}, u32[]{:S(2)}) collective-permute-start(f32[8,128]{1,0:T(8,128)S(1)} %add.13.own_ref), channel_id=1, source_target_pairs={{2,4},{6,8},{10,12},{14,16},{18,20},{22,24},{26,28},{30,32},{34,36... | collective-permute-start | bytes 12296 | tf_op jit(solution)/shard_map/ppermute | solution.py:556
  30.4 3.6 %collective-permute-start.4 = (f32[8,128]{1,0:T(8,128)S(1)}, f32[8,128]{1,0:T(8,128)S(1)}, u32[]{:S(2)}, u32[]{:S(2)}) collective-permute-start(f32[8,128]{1,0:T(8,128)S(1)} %add.13.own_ref), channel_id=1, source_target_pairs={{0,2},{2,0},{4,6},{6,4},{8,10},{10,8},{12,14},{14,12},{16,18},{18,... | collective-permute-start | bytes 12296 | tf_op jit(solution)/shard_map/ppermute | solution.py:557
  36.5 5.1 %collective-permute-start.6 = (f32[8,128]{1,0:T(8,128)S(1)}, f32[8,128]{1,0:T(8,128)S(1)}, u32[]{:S(2)}, u32[]{:S(2)}) collective-permute-start(f32[8,128]{1,0:T(8,128)S(1)} %message_round.4), channel_id=1, source_target_pairs={{0,1},{1,0},{2,3},{3,2},{4,5},{5,4},{6,7},{7,6},{8,9},{9,8},{10,11... | collective-permute-start | bytes 12296 | tf_op jit(solution)/shard_map/ppermute | solution.py:555
  41.7 7.9 %collective-permute-start.8 = (f32[8,128]{1,0:T(8,128)S(1)}, f32[8,128]{1,0:T(8,128)S(1)}, u32[]{:S(2)}, u32[]{:S(2)}) collective-permute-start(f32[8,128]{1,0:T(8,128)S(1)} %add.14.own_ref), channel_id=1, source_target_pairs={{2,4},{6,8},{10,12},{14,16},{18,20},{22,24},{26,28},{30,32},{34,36... | collective-permute-start | bytes 12296 | tf_op jit(solution)/shard_map/ppermute | solution.py:556
  44.8 4.8 %collective-permute-start.7 = (f32[8,128]{1,0:T(8,128)S(1)}, f32[8,128]{1,0:T(8,128)S(1)}, u32[]{:S(2)}, u32[]{:S(2)}) collective-permute-start(f32[8,128]{1,0:T(8,128)S(1)} %add.14.own_ref), channel_id=1, source_target_pairs={{0,2},{2,0},{4,6},{6,4},{8,10},{10,8},{12,14},{14,12},{16,18},{18,... | collective-permute-start | bytes 12296 | tf_op jit(solution)/shard_map/ppermute | solution.py:557
  52.1 31.4 %copy-start.2 = (f32[512,128]{1,0:T(8,128)S(1)}, f32[512,128]{1,0:T(8,128)}, u32[]{:S(2)}) copy-start(f32[512,128]{1,0:T(8,128)} %probes_ref.1) | copy-start | bytes 786436
  52.1 31.4 %copy-start.3 = (f32[4,4]{1,0:T(4,128)S(1)}, f32[4,4]{1,0:T(4,128)}, u32[]{:S(2)}) copy-start(f32[4,4]{1,0:T(4,128)} %gate.1) | copy-start | bytes 196
  52.1 5.2 %collective-permute-start.9 = (f32[8,128]{1,0:T(8,128)S(1)}, f32[8,128]{1,0:T(8,128)S(1)}, u32[]{:S(2)}, u32[]{:S(2)}) collective-permute-start(f32[8,128]{1,0:T(8,128)S(1)} %message_round.5), channel_id=1, source_target_pairs={{0,1},{1,0},{2,3},{3,2},{4,5},{5,4},{6,7},{7,6},{8,9},{9,8},{10,11... | collective-permute-start | bytes 12296 | tf_op jit(solution)/shard_map/ppermute | solution.py:555
  57.3 8.0 %collective-permute-start.11 = (f32[8,128]{1,0:T(8,128)S(1)}, f32[8,128]{1,0:T(8,128)S(1)}, u32[]{:S(2)}, u32[]{:S(2)}) collective-permute-start(f32[8,128]{1,0:T(8,128)S(1)} %add.15.own_ref), channel_id=1, source_target_pairs={{2,4},{6,8},{10,12},{14,16},{18,20},{22,24},{26,28},{30,32},{34,36... | collective-permute-start | bytes 12296 | tf_op jit(solution)/shard_map/ppermute | solution.py:556
  59.3 6.0 %collective-permute-start.10 = (f32[8,128]{1,0:T(8,128)S(1)}, f32[8,128]{1,0:T(8,128)S(1)}, u32[]{:S(2)}, u32[]{:S(2)}) collective-permute-start(f32[8,128]{1,0:T(8,128)S(1)} %add.15.own_ref), channel_id=1, source_target_pairs={{0,2},{2,0},{4,6},{6,4},{8,10},{10,8},{12,14},{14,12},{16,18},{18,... | collective-permute-start | bytes 12296 | tf_op jit(solution)/shard_map/ppermute | solution.py:557
  69.4 7.3 %collective-permute-start.12 = (f32[3,128,128]{2,1,0:T(8,128)S(1)}, f32[3,128,128]{2,1,0:T(8,128)S(1)}, u32[]{:S(2)}, u32[]{:S(2)}) collective-permute-start(f32[3,128,128]{2,1,0:T(8,128)S(1)} %get-tuple-element.21), channel_id=1, source_target_pairs={{0,1},{1,0},{2,3},{3,2},{4,5},{5,4},{6,7},{7,6},{8,9},{9,8},{10,11... | collective-permute-start | bytes 589832 | tf_op jit(solution)/shard_map/ppermute | solution.py:559
  81.7 1.8 %collective-permute-start.13 = (f32[256,256]{1,0:T(8,128)S(1)}, f32[256,256]{1,0:T(8,128)S(1)}, u32[]{:S(2)}, u32[]{:S(2)}) collective-permute-start(f32[256,256]{1,0:T(8,128)S(1)} %get-tuple-element.22.upper_ref), channel_id=1, source_target_pairs={{0,2},{2,0},{4,6},{6,4},{8,10},{10,8},{12,14},{14,12},{16,18},{18,... | collective-permute-start | bytes 786440 | tf_op jit(solution)/shard_map/ppermute | solution.py:561
  90.8 7.3 %collective-permute-start.14 = (bf16[272,256]{1,0:T(8,128)(2,1)S(1)}, bf16[272,256]{1,0:T(8,128)(2,1)S(1)}, u32[]{:S(2)}, u32[]{:S(2)}) collective-permute-start(bf16[272,256]{1,0:T(8,128)(2,1)S(1)} %truncate.1.pack_ref), channel_id=1, source_target_pairs={{0,1},{1,0},{2,3},{3,2},{4,5},{5,4},{6,7},{7,6},{8,9},{9,8},{10,11... | collective-permute-start | bytes 417800 | tf_op jit(solution)/shard_map/ppermute | solution.py:563

commit v2 on v1

v2 whole, which is shorter than its diff:
```python
import functools

import jax
import jax.numpy as jnp
from jax import lax
from jax.experimental import pallas as pl
from jax.experimental.pallas import tpu as pltpu
from jax.sharding import PartitionSpec as P

ROUNDS = 4
SWEEPS = 8
F32 = jnp.float32
BF16 = jnp.bfloat16
MB = 1 << 20
highest = lax.Precision.HIGHEST

CORE, ROW, MATE0, MATE1, FIRST, LAST, KEPT, RANK, GATED = range(9)


def smem():
    return pl.BlockSpec(memory_space=pltpu.SMEM)


def vmem():
    return pl.BlockSpec(memory_space=pltpu.VMEM)


def params(mib):
    return pltpu.CompilerParams(vmem_limit_bytes=mib * MB)


def cost(flops, moved):
    return pl.CostEstimate(flops=int(flops), bytes_accessed=int(moved), transcendentals=0)


def halves(value):
    high = value.astype(BF16)
    low = (value - high.astype(F32)).astype(BF16)
    return (high, low)


def dot_of(left, right, dims=((1,), (0,))):
    return lax.dot_general(left, right, (dims, ((), ())), preferred_element_type=F32)


def dot3(left, right, dims=((1,), (0,))):
    return dot_of(left[0], right[0], dims) + (
        dot_of(left[0], right[1], dims) + dot_of(left[1], right[0], dims)
    )


def dot_high(left, right, dims=((1,), (0,))):
    return lax.dot_general(left, right, (dims, ((), ())), preferred_element_type=F32, precision=highest)


def down(row):
    size = row.shape[-1]
    return jnp.transpose(jnp.broadcast_to(row, (size, size)))


def normalized(ref):
    rows = ref[...]
    return rows / jnp.sum(rows, axis=1, keepdims=True)


def pick(rows, member, leg):
    return rows[3 * member + leg : 3 * member + leg + 1]


def level(rows):
    return jnp.full((1, rows.shape[-1]), 1.0 / rows.shape[-1], F32)


def from_mate(mate, place):
    return jnp.where(place == 0, pick(mate, 0, 2), pick(mate, 1, 2))


def inner_incoming(info, own, mate):
    odd = info[CORE] == 1
    place = jnp.where(odd, info[MATE0], info[MATE1])
    joined = place == info[CORE]
    chain = jnp.where(odd, pick(mate, 1, 1), pick(mate, 0, 0))
    gated = jnp.where(odd, pick(mate, 1, 2), pick(mate, 0, 2))
    near = chain + jnp.where(joined, gated, 0.0)
    home = jnp.where(odd, pick(own, 1, 0), pick(own, 0, 1))
    third = from_mate(mate, place) + jnp.where(joined, chain, 0.0)
    return (
        jnp.where(odd, near, home),
        jnp.where(odd, home, near),
        jnp.where(place < 0, level(own), third),
    )


def outer_known(info, own, mate):
    odd = info[CORE] == 1
    place = jnp.where(odd, info[MATE1], info[MATE0])
    home = jnp.where(odd, pick(own, 0, 1), pick(own, 1, 0))
    return (home, jnp.where(place < 0, level(own), from_mate(mate, place)))


def outer_far(info, side):
    far = jnp.where(info[CORE] == 1, pick(side, 0, 0), pick(side, 1, 1))
    return jnp.where(info[FIRST] + info[LAST] > 0, level(side), far)


def outer_incoming(info, own, mate, side):
    odd = info[CORE] == 1
    home, third = outer_known(info, own, mate)
    far = outer_far(info, side)
    return (jnp.where(odd, home, far), jnp.where(odd, far, home), third)


def hbm():
    return pl.BlockSpec(memory_space=pltpu.HBM)


def anywhere():
    return pl.BlockSpec(memory_space=pl.ANY)


def write_scalars(near, ranks, info):
    device, row = (lax.axis_index("site"), lax.axis_index("row"))
    core = lax.rem(device, 2)
    base = 2 * (device - core)
    even0, even1 = (near[2, base] - base, near[2, base + 1] - base)
    odd0, odd1 = (near[2, base + 2], near[2, base + 3])
    odd = core == 1
    info[MATE0] = jnp.where(odd, jnp.where(odd0 < 0, -1, odd0 - base), jnp.maximum(even0 - 2, -1))
    info[MATE1] = jnp.where(odd, jnp.where(odd1 < 0, -1, odd1 - base), jnp.maximum(even1 - 2, -1))
    crossed = jnp.logical_or(even0 == 3, even1 == 2)
    kept = jnp.where(jnp.logical_and(odd, crossed), 1 - row, row)
    site = 2 * device + kept
    info[CORE] = core
    info[ROW] = row
    info[FIRST] = (device == 0).astype(jnp.int32)
    info[LAST] = (device == lax.axis_size("site") - 1).astype(jnp.int32)
    info[KEPT] = kept
    info[RANK] = ranks[site]
    info[GATED] = (near[2, site] >= 0).astype(jnp.int32)


def open_kernel(x_hbm, x_ref, s_ref, out_ref, scratch, sums_ref, total_ref, sems):
    members, rows, wide, bond = x_hbm.shape
    steps = sems.shape[0]
    per = steps // members
    block = rows // per

    def fetch(step):
        place = (step // per, pl.ds(lax.rem(step, per) * block, block))
        return pltpu.make_async_copy(x_hbm.at[place], x_ref.at[place], sems.at[step])

    for step in range(steps):
        fetch(step).start()
    total_ref[...] = jnp.zeros(total_ref.shape, F32)

    def body(step, carry):
        fetch(step).wait()
        member, start = (step // per, lax.rem(step, per) * block)
        total = total_ref[member]
        for index in range(block):
            lane = scratch.at[index % scratch.shape[0]]
            lane[...] = x_ref[member, start + index].astype(F32)
            even = lane[pl.ds(0, bond, 2), :]
            odd = lane[pl.ds(1, bond, 2), :]
            square = even * even + odd * odd
            s_ref[member, start + index] = square.astype(BF16)
            sums_ref[member, start + index] = jnp.sum(square.reshape(bond // 8, 8, bond), axis=0)
            total = total + square
        total_ref[member] = total
        return carry

    lax.fori_loop(0, steps, body, 0)
    row = lax.axis_index("row")
    flat_weight = jnp.ones((1, bond), F32)
    out_ref[...] = jnp.ones(out_ref.shape, F32)
    for member in range(members):
        finish(row, out_ref, member, sums_ref[member], total_ref[member], flat_weight, None)


def open_call(x):
    members, rows, wide, bond = x.shape
    block = 8
    steps = members * rows // block
    return pl.pallas_call(
        open_kernel,
        in_specs=[hbm()],
        out_specs=[vmem(), vmem(), vmem()],
        out_shape=[
            jax.ShapeDtypeStruct(x.shape, BF16),
            jax.ShapeDtypeStruct((members, rows, bond, bond), BF16),
            jax.ShapeDtypeStruct((8, bond), F32),
        ],
        scratch_shapes=[
            pltpu.VMEM((4, wide, bond), F32),
            pltpu.VMEM((members, rows, 8, bond), F32),
            pltpu.VMEM((members, bond, bond), F32),
            pltpu.SemaphoreType.DMA((steps,)),
        ],
        compiler_params=params(38),
        cost_estimate=cost(4 * x.size, 5 * x.size),
        name="open",
    )(x)


def flatten_kernel(after, x_ref, *refs, member):
    flat_ref, scratch = refs[-2:]
    rows, bond = flat_ref.shape[1:3]
    if member == 0:
        write_scalars(*refs[:3])

    def body(index, carry):
        lane = scratch.at[lax.rem(index, scratch.shape[0])]
        lane[...] = x_ref[member, index].astype(F32)
        parts = [lane[pl.ds(place, bond, 2), :] for place in range(2)]
        flat_ref[member, index] = jnp.concatenate(parts, axis=1).astype(BF16)
        return carry

    lax.fori_loop(0, rows, body, 0, unroll=8)


def flatten_call(after, x, member, *more):
    members, rows, wide, bond = x.shape
    flat = jax.ShapeDtypeStruct((members, rows, bond, wide), BF16)
    info = jax.ShapeDtypeStruct((16,), jnp.int32)
    first = member == 0
    return pl.pallas_call(
        functools.partial(flatten_kernel, member=member),
        in_specs=[anywhere(), vmem()] + ([smem(), smem()] if first else [vmem()]),
        out_specs=[smem(), vmem()] if first else vmem(),
        out_shape=[info, flat] if first else flat,
        input_output_aliases={} if first else {2: 0},
        scratch_shapes=[pltpu.VMEM((8, wide, bond), F32)],
        compiler_params=params(8),
        cost_estimate=cost(x.size, 2 * x.size),
        name="flatten",
    )(after, x, *more)


def halved(row_index, row):
    half = row.shape[1] // 2
    return jnp.where(row_index == 0, row[:, :half], row[:, half:])


def placed(row_index, half):
    empty = jnp.zeros_like(half)
    return jnp.where(
        row_index == 0,
        jnp.concatenate([half, empty], axis=1),
        jnp.concatenate([empty, half], axis=1),
    )


def by_row(row, matrix):
    return dot_high(jnp.broadcast_to(row, (8, row.shape[1])), matrix)[:1]


def by_column(row, matrix):
    return dot_high(jnp.broadcast_to(row, (8, row.shape[1])), matrix, ((1,), (1,)))[:1]


def put_leg(out_ref, member, leg, row):
    out_ref[pl.ds(3 * member + leg, 1), :] = row


def finish(row_index, out_ref, member, sums, total, third, second_down):
    bond = total.shape[0]
    half = by_column(jnp.ones((1, bond), F32), jnp.sum(sums, axis=1))
    weighted = total if second_down is None else total * second_down
    put_leg(out_ref, member, 0, placed(row_index, half))
    put_leg(out_ref, member, 1, by_column(third, total))
    put_leg(out_ref, member, 2, jnp.sum(weighted, axis=0, keepdims=True))


GROUP = 4


def scaled_sum(s_ref, member, step, first_ref, start):
    bond = s_ref.shape[2]
    joined = None
    for place in range(GROUP):
        index = step * GROUP + place
        scale = jnp.broadcast_to(first_ref[pl.ds(start + index, 1), :], (16, bond)).astype(BF16)
        term = jnp.concatenate([scale] * (bond // 16), axis=0) * s_ref[member, index]
        joined = term if joined is None else joined + term
    return joined.astype(F32)


def contract_inner(info, weights, s_ref, out_ref, first_ref, sums_ref):
    rows, bond = s_ref.shape[1:3]
    member = 1 - info[CORE]
    start = info[ROW] * rows
    first, second, third = weights
    third = third.astype(BF16).astype(F32)
    first_ref[...] = down(first)
    second_down = down(second)
    outer = (second_down * third).astype(BF16)

    def body(step, total):
        for place in range(GROUP):
            index = step * GROUP + place
            piece = s_ref[member, index] * outer
            piece = piece[:64] + piece[64:]
            piece = (piece[:32] + piece[32:]).astype(F32)
            sums_ref[index] = (piece[:8] + piece[8:16]) + (piece[16:24] + piece[24:])
        return total + scaled_sum(s_ref, member, step, first_ref, start)

    total = lax.fori_loop(0, rows // GROUP, body, jnp.zeros((bond, bond), F32), unroll=2)
    finish(info[ROW], out_ref, member, sums_ref[...], total, third, second_down)


def contract_outer(info, home, third, s_ref, out_ref, mixed_ref, other_ref, first_ref):
    rows, bond = s_ref.shape[1:3]
    member = info[CORE]
    odd = info[CORE] == 1
    start = info[ROW] * rows
    third_rows = jnp.broadcast_to(third.astype(BF16), (8, bond))

    def mix(step, carry):
        pair = s_ref[member, pl.ds(2 * step, 2)].reshape(2 * bond, bond)
        product = dot_of(third_rows, pair, ((1,), (1,)))
        mixed_ref[pl.ds(2 * step, 1), :] = product[:1, :bond]
        mixed_ref[pl.ds(2 * step + 1, 1), :] = product[:1, bond:]
        return carry

    lax.fori_loop(0, rows // 2, mix, 0, unroll=8)

    @pl.when(odd)
    def over_first():
        first_ref[...] = down(home)

        def body(step, total):
            return total + scaled_sum(s_ref, member, step, first_ref, start)

        zero = jnp.zeros((bond, bond), F32)
        other_ref[...] = lax.fori_loop(0, rows // GROUP, body, zero, unroll=2)
        put_leg(out_ref, member, 1, by_row(halved(info[ROW], home), mixed_ref[...]))

    @pl.when(jnp.logical_not(odd))
    def over_second():
        second_rows = jnp.concatenate(halves(home) + (jnp.zeros((6, bond), BF16),), axis=0)

        def body(step, carry):
            pair = jnp.concatenate([s_ref[member, 2 * step], s_ref[member, 2 * step + 1]], axis=1)
            product = dot_of(second_rows, pair)
            product = product[:1] + product[1:2]
            other_ref[pl.ds(2 * step, 1), :] = product[:, :bond]
            other_ref[pl.ds(2 * step + 1, 1), :] = product[:, bond:]
            return carry

        lax.fori_loop(0, rows // 2, body, 0, unroll=8)
        put_leg(out_ref, member, 0, placed(info[ROW], by_column(home, mixed_ref[...])))


def inner_kernel(info, own_ref, mate_ref, s_ref, after, out_ref, mixed_ref, other_ref, first_ref, sums_ref):
    own, mate = (normalized(own_ref), normalized(mate_ref))
    out_ref[...] = jnp.ones(out_ref.shape, F32)
    contract_inner(info, inner_incoming(info, own, mate), s_ref, out_ref, first_ref, sums_ref)
    home, third = outer_known(info, own, mate)
    contract_outer(info, home, third, s_ref, out_ref, mixed_ref, other_ref, first_ref)


def outer_kernel(info, side_ref, part_ref, mixed_ref, other_ref, out_ref):
    rows = mixed_ref.shape[0]
    far = outer_far(info, normalized(side_ref))
    out_ref[...] = part_ref[...]

    @pl.when(info[CORE] == 1)
    def as_second():
        put_leg(out_ref, 1, 0, placed(info[ROW], by_column(far, mixed_ref[...])))
        put_leg(out_ref, 1, 2, by_row(far, other_ref[...]))

    @pl.when(info[CORE] == 0)
    def as_first():
        half = halved(info[ROW], far)
        put_leg(out_ref, 0, 1, by_row(half, mixed_ref[...]))
        put_leg(out_ref, 0, 2, by_row(half, other_ref[:rows]))


def inner_call(info, own, mate, squares, after):
    rows, bond = squares.shape[1:3]
    return pl.pallas_call(
        inner_kernel,
        in_specs=[smem(), vmem(), vmem(), vmem(), anywhere()],
        out_specs=[vmem(), vmem(), vmem()],
        out_shape=[
            jax.ShapeDtypeStruct((8, bond), F32),
            jax.ShapeDtypeStruct((rows, bond), F32),
            jax.ShapeDtypeStruct((bond, bond), F32),
        ],
        scratch_shapes=[pltpu.VMEM((bond, bond), F32), pltpu.VMEM((rows, 8, bond), F32)],
        compiler_params=params(8),
        cost_estimate=cost(4 * squares.size, 2 * squares.size),
        name="inner_round",
    )(info, own, mate, squares, after)


def outer_call(info, side, part, mixed, other):
    return pl.pallas_call(
        outer_kernel,
        in_specs=[smem(), vmem(), vmem(), vmem(), vmem()],
        out_specs=vmem(),
        out_shape=jax.ShapeDtypeStruct(part.shape, F32),
        compiler_params=params(8),
        cost_estimate=cost(8 * mixed.size, 8 * mixed.size),
        name="outer_round",
    )(info, side, part, mixed, other)


def add_gram(info, member, weights, d_ref, out_ref, first_ref, gram):
    rows, bond = d_ref.shape[1:3]
    block = 32
    start = info[ROW] * rows
    first_ref[...] = jnp.sqrt(down(weights[0]))
    second = jnp.sqrt(down(weights[1]))
    gram[...] = jnp.zeros(gram.shape, F32)

    def body(step, carry):
        parts = []
        for place in range(block):
            index = step * block + place
            scale = first_ref[pl.ds(start + index, 1), :] * second
            piece = d_ref[member, index].astype(F32) * jnp.concatenate([scale, scale], axis=1)
            parts.append(piece.astype(BF16))
        weighted = jnp.concatenate(parts, axis=0)
        gram[...] += dot_of(weighted, weighted, ((0,), (0,)))
        return carry

    lax.fori_loop(0, rows // block, body, 0)
    out_ref[0] = gram[:bond, :bond]
    out_ref[1] = gram[:bond, bond:]
    out_ref[2] = gram[bond:, bond:]


def gram_weights(info, member, own_ref, mate_ref, side_ref):
    own, mate, side = (normalized(own_ref), normalized(mate_ref), normalized(side_ref))
    inner = inner_incoming(info, own, mate)
    outer = outer_incoming(info, own, mate, side)
    return [jnp.where(member == info[CORE], outer[leg], inner[leg]) for leg in range(2)]


def send_kernel(info, own_ref, mate_ref, side_ref, d_ref, out_ref, msg_ref, first_ref, gram):
    member = 1 - info[KEPT]
    weights = gram_weights(info, member, own_ref, mate_ref, side_ref)
    own = normalized(own_ref)
    for place in range(2):
        for leg in range(3):
            msg_ref[leg, pl.ds(place, 1), :] = pick(own, place, leg)
    add_gram(info, member, weights, d_ref, out_ref, first_ref, gram)


def keep_kernel(info, own_ref, mate_ref, side_ref, d_ref, after, out_ref, first_ref, gram):
    member = info[KEPT]
    weights = gram_weights(info, member, own_ref, mate_ref, side_ref)
    add_gram(info, member, weights, d_ref, out_ref, first_ref, gram)


def gram_call(kernel, name, extra_specs, out_specs, out_shape, flat, operands):
    rows, bond, wide = flat.shape[1:]
    return pl.pallas_call(
        kernel,
        in_specs=[smem()] + [vmem()] * 4 + extra_specs,
        out_specs=out_specs,
        out_shape=out_shape,
        scratch_shapes=[pltpu.VMEM((bond, bond), F32), pltpu.VMEM((wide, wide), F32)],
        compiler_params=params(20),
        cost_estimate=cost(wide * flat.size, flat.size),
        name=name,
    )(*operands)


def send_call(info, own, mate, side, flat):
    members, _, bond, _ = flat.shape
    shapes = [
        jax.ShapeDtypeStruct((3, bond, bond), F32),
        jax.ShapeDtypeStruct((3, members, bond), F32),
    ]
    operands = (info, own, mate, side, flat)
    return gram_call(send_kernel, "gram_to_send", [], [vmem(), vmem()], shapes, flat, operands)


def keep_call(info, own, mate, side, flat, after):
    bond = flat.shape[2]
    shape = jax.ShapeDtypeStruct((3, bond, bond), F32)
    operands = (info, own, mate, side, flat, after)
    return gram_call(keep_kernel, "gram_to_keep", [anywhere()], vmem(), shape, flat, operands)


def eye_mask(size):
    down_index = lax.broadcasted_iota(jnp.int32, (size, size), 0)
    across_index = lax.broadcasted_iota(jnp.int32, (size, size), 1)
    return down_index == across_index


def root_pair(matrix):
    size = matrix.shape[0]
    diagonal = eye_mask(size)
    lift = jnp.where(diagonal, 1.5, 0.0).astype(F32)
    scale = jnp.sum(jnp.where(diagonal, matrix, 0.0), keepdims=True)
    current = matrix / scale
    poly = lift - 0.5 * current
    poly_parts = halves(poly)
    current = dot3(halves(current), poly_parts)
    partner = poly
    for _ in range(SWEEPS - 1):
        current_parts, partner_parts = (halves(current), halves(partner))
        poly_parts = halves(lift - 0.5 * dot3(partner_parts, current_parts))
        current = dot3(current_parts, poly_parts)
        partner = dot3(poly_parts, partner_parts)
    root_scale = jnp.sqrt(scale)
    return (current * root_scale, partner / root_scale)


def root_kernel(keep_ref, got_ref, upper_ref, inverse_ref):
    corner = keep_ref[0] + got_ref[0]
    above = keep_ref[1] + got_ref[1]
    below = keep_ref[2] + got_ref[2]
    matrix = jnp.concatenate(
        [
            jnp.concatenate([corner, above], axis=1),
            jnp.concatenate([jnp.transpose(above), below], axis=1),
        ],
        axis=0,
    )
    upper_ref[...], inverse_ref[...] = root_pair(matrix)


def root_call(keep, got):
    wide = 2 * keep.shape[1]
    full = jax.ShapeDtypeStruct((wide, wide), F32)
    return pl.pallas_call(
        root_kernel,
        in_specs=[vmem(), vmem()],
        out_specs=[vmem(), vmem()],
        out_shape=[full, full],
        compiler_params=params(16),
        cost_estimate=cost(66 * 2 * wide**3, 16 * wide * wide),
        name="root",
    )(keep, got)


def truncate_kernel(info, gate, own_ref, mate_ref, upper_ref, inverse_ref, other_ref, probes_ref, out_ref):
    wide, bond = (upper_ref.shape[0], probes_ref.shape[1])
    odd = info[CORE] == 1
    kept = info[KEPT]
    mate_place = jnp.maximum(jnp.where(kept == 0, info[MATE0], info[MATE1]), 0)
    own_msg = own_ref[pl.ds(3 * kept + 2, 1), :]
    mate_msg = mate_ref[pl.ds(3 * mate_place + 2, 1), :]
    own_msg = own_msg / jnp.sum(own_msg, axis=1, keepdims=True)
    mate_msg = mate_msg / jnp.sum(mate_msg, axis=1, keepdims=True)
    strength = bond * jnp.sqrt(own_msg * mate_msg)
    own_upper, other_upper = (upper_ref[...], other_ref[...])
    left = jnp.where(odd, other_upper, own_upper)
    right = jnp.where(odd, own_upper, other_upper)
    left_parts, right_parts = (halves(left), halves(right))

    def block(value, down_half, across_half):
        return value[
            down_half * bond : (down_half + 1) * bond, across_half * bond : (across_half + 1) * bond
        ]

    def combined(value, entry):
        block_rows = []
        for out_down in range(2):
            blocks = []
            for out_across in range(2):
                total = None
                for first in range(2):
                    for second in range(2):
                        term = entry(out_down, out_across, first, second) * block(value, first, second)
                        total = term if total is None else total + term
                blocks.append(total * strength_down)
            block_rows.append(jnp.concatenate(blocks, axis=1))
        return jnp.concatenate(block_rows, axis=0)

    across = lax.broadcasted_iota(jnp.int32, (1, bond), 1)
    mask = (across < info[RANK]).astype(F32)
    strength_down = down(strength)
    probes = jnp.concatenate(
        [probes_ref[pl.ds(0, wide, 2), :] * mask, probes_ref[pl.ds(1, wide, 2), :] * mask], axis=1
    )
    probed = combined(
        dot3(right_parts, halves(probes)),
        lambda s, s_out, t, t_out: gate[2 * s_out + t_out, 2 * s + t],
    )
    sampled = dot3(left_parts, halves(probed))
    sampled_parts = halves(jnp.concatenate([sampled[:, :bond], sampled[:, bond:]], axis=0))
    inner = dot3(sampled_parts, sampled_parts, ((0,), (0,)))
    inner = inner + jnp.where(eye_mask(bond), 1.0 - mask, 0.0)
    _, inner_inverse = root_pair(inner)
    basis = dot3(sampled_parts, halves(inner_inverse))
    basis = jnp.concatenate([basis[:wide], basis[wide:]], axis=1)
    based = combined(
        dot3(left_parts, halves(basis)),
        lambda t, t_out, s, s_out: gate[2 * s_out + t_out, 2 * s + t],
    )
    coeffs = dot3(right_parts, halves(based))
    squares = jnp.sum(coeffs * coeffs, axis=0, keepdims=True)
    new_bond = jnp.sqrt((squares[:, :bond] + squares[:, bond:]) / (2 * wide) + 1e-06)
    target = jnp.where(odd, coeffs / jnp.concatenate([new_bond, new_bond], axis=1), basis)
    change = dot3(halves(inverse_ref[...]), halves(target))
    gated = info[GATED] == 1
    identity = eye_mask(wide).astype(F32)
    out_ref[:wide] = jnp.where(gated, change, identity).astype(BF16)
    bond_parts = halves(jnp.where(gated, new_bond, 0.0))
    out_ref[wide:] = jnp.broadcast_to(jnp.concatenate(bond_parts, axis=1), (16, wide))


def truncate_call(info, gate, own, mate, upper, inverse, other, probes):
    wide = upper.shape[0]
    return pl.pallas_call(
        truncate_kernel,
        in_specs=[smem(), smem()] + [vmem()] * 6,
        out_specs=vmem(),
        out_shape=jax.ShapeDtypeStruct((wide + 16, wide), BF16),
        compiler_params=params(32),
        cost_estimate=cost(40 * 2 * wide**3, 24 * wide * wide),
        name="truncate",
    )(info, gate, own, mate, upper, inverse, other, probes)


def update_member(member, pack_ref, d_ref, out_hbm, held, scratch, sems):
    rows, bond, wide = d_ref.shape[1:]
    slots, block = held.shape[:2]
    steps = rows // block

    def put(step):
        slot = lax.rem(step, slots)
        target = out_hbm.at[member, pl.ds(step * block, block)]
        return pltpu.make_async_copy(held.at[slot], target, sems.at[slot])

    def body(step, carry):
        start = step * block
        slot = lax.rem(step, slots)

        @pl.when(step >= slots)
        def free():
            put(step).wait()

        rows_in = d_ref[member, pl.ds(start, block)].reshape(block * bond, wide)
        result = dot_of(rows_in, pack_ref[:wide])
        for index in range(block):
            lane = scratch.at[index % scratch.shape[0]]
            piece = result[index * bond : (index + 1) * bond]
            lane[pl.ds(0, bond, 2), :] = piece[:, :bond]
            lane[pl.ds(1, bond, 2), :] = piece[:, bond:]
            held[slot, index] = lane[...].astype(BF16)
        put(step).start()
        return carry

    lax.fori_loop(0, steps, body, 0)
    for step in range(steps - slots, steps):
        put(step).wait()


def own_kernel(info, pack_ref, d_ref, after, out_hbm, held, scratch, sems):
    update_member(info[KEPT], pack_ref, d_ref, out_hbm, held, scratch, sems)


def other_kernel(info, pack_ref, got_ref, d_ref, begun_hbm, out_hbm, bond_ref, held, scratch, sems):
    bond, wide = d_ref.shape[2:]
    kept = info[KEPT]
    tail = pack_ref[wide:].astype(F32)
    got = got_ref[wide:].astype(F32)
    mine = tail[:1, :bond] + tail[:1, bond:]
    other = got[:1, :bond] + got[:1, bond:]
    bond_ref[pl.ds(0, 1), :] = jnp.where(kept == 0, mine, other)
    bond_ref[pl.ds(1, 1), :] = jnp.where(kept == 0, other, mine)
    update_member(1 - kept, got_ref, d_ref, out_hbm, held, scratch, sems)


def update_call(kernel, name, in_specs, aliases, with_bonds, flat, operands):
    members, rows, bond, wide = flat.shape
    block, slots = (16, 4)
    tensor = jax.ShapeDtypeStruct((members, rows, wide, bond), BF16)
    bonds = jax.ShapeDtypeStruct((members, bond), F32)
    return pl.pallas_call(
        kernel,
        in_specs=in_specs,
        out_specs=[hbm(), vmem()] if with_bonds else hbm(),
        out_shape=[tensor, bonds] if with_bonds else tensor,
        input_output_aliases=aliases,
        scratch_shapes=[
            pltpu.VMEM((slots, block, wide, bond), BF16),
            pltpu.VMEM((4, wide, bond), F32),
            pltpu.SemaphoreType.DMA((slots,)),
        ],
        compiler_params=params(24),
        cost_estimate=cost(wide * flat.size, 2 * flat.size),
        name=name,
    )(*operands)


def own_call(info, pack, flat, after):
    specs = [smem(), vmem(), vmem(), anywhere()]
    return update_call(own_kernel, "update_own", specs, {}, False, flat, (info, pack, flat, after))


def other_call(info, pack, got, flat, begun):
    specs = [smem(), vmem(), vmem(), vmem(), hbm()]
    operands = (info, pack, got, flat, begun)
    return update_call(other_kernel, "update_other", specs, {4: 0}, True, flat, operands)


def shards(tensors, neighbours, edge_ranks, gate_matrix, probes):
    members, rows, bond, phys = tensors.shape[:4]
    sites = lax.axis_size("site")
    row_swap = [(0, 1), (1, 0)]
    core_swap = [(i, i ^ 1) for i in range(sites)]
    side_swap = [(i, i + 1) for i in range(1, sites - 1, 2)]
    side_swap += [(j, i) for i, j in side_swap]
    x = tensors.reshape(members, rows, bond * phys, bond)
    x, squares, part = open_call(x)
    info, flat = flatten_call(part, x, 0, neighbours.T, edge_ranks)
    for index in range(ROUNDS):
        if index > 0:
            begun = inner_call(info, own, mate, squares, flat)
            part = outer_call(info, side, *begun)
        if index == 1:
            flat = flatten_call(part, x, 1, flat)
        own = part + lax.ppermute(part, "row", row_swap)
        side = lax.ppermute(own, "site", side_swap)
        mate = lax.ppermute(own, "site", core_swap)
    send, messages = send_call(info, own, mate, side, flat)
    got = lax.ppermute(send, "row", row_swap)
    keep = keep_call(info, own, mate, side, flat, send)
    upper, inverse = root_call(keep, got)
    other = lax.ppermute(upper, "site", core_swap)
    pack = truncate_call(info, gate_matrix, own, mate, upper, inverse, other, probes)
    got_pack = lax.ppermute(pack, "row", row_swap)
    begun = own_call(info, pack, flat, pack)
    updated, bonds = other_call(info, pack, got_pack, flat, begun)
    return (updated.reshape(tensors.shape), messages.transpose(1, 0, 2), bonds)


def solution(mesh):
    return jax.shard_map(
        shards,
        mesh=mesh,
        in_specs=(P("site", "row", None, None, None), P(), P(), P(), P()),
        out_specs=(P("site", "row", None, None, None), P("site", None, None), P("site", None)),
        check_vma=False,
    )
```

time: 105 us -> 100 us (0.952)
  waiting for transfers between devices: 30.4 us -> 17.8 us
  Pallas kernels: 39.1 us -> 45.7 us
    pallas_call x5 -> x10, Pallas kernels: 18.5 us -> 26.8 us  [the longest x3 11.1 us: inner_call(): pl.pallas_call(inner_kernel, in_specs=[smem(), vmem(), vmem(), vmem(), an...]
    ppermute x4, waiting for transfers between devices: 12.9 us -> 5.58 us  [shards(): side = lax.ppermute(own, 'site', side_swap)]
    ppermute x1, waiting for transfers between devices: 4.07 us -> 0.31 us  [shards(): got_pack = lax.ppermute(pack, 'row', row_swap)]
    ppermute x1, waiting for transfers between devices: 4.03 us -> 1.84 us  [shards(): got = lax.ppermute(send, 'row', row_swap)]
    ppermute x4, starting transfers between devices: 14.9 us -> 16.8 us  [shards(): side = lax.ppermute(own, 'site', side_swap)]
    pallas_call x1, Pallas kernels: 7.31 us -> 5.71 us  [truncate_call(): pl.pallas_call(truncate_kernel, in_specs=[smem(), smem()] + [vmem()] * 6,...]
  transfers between devices with their start and end apart: 15 -> 15, of which waited for: 10 -> 10; matrix products, arithmetic and copies ran while one was open for 0% -> 0% of each run, Pallas kernels for 3% -> 21%
where the time goes in v2:
time: 100 us; the launch traced here: 99.8 us
  Pallas kernels  45.7 us (46%)
  starting transfers between devices  35.3 us (35%)
  waiting for transfers between devices  17.8 us (18%)
    ppermute x4, starting transfers between devices, shards(): side = lax.ppermute(own, 'site', side_swap)  16.8 us
    ppermute x4, starting transfers between devices, shards(): own = part + lax.ppermute(part, 'row', row_swap)  12 us
    pallas_call x3, Pallas kernels, inner_call(): pl.pallas_call(inner_kernel, in_specs=[smem(), vmem(), vmem(), vmem(), an...  11.1 us
    ppermute x4, waiting for transfers between devices, shards(): own = part + lax.ppermute(part, 'row', row_swap)  8.55 us
    pallas_call x2, Pallas kernels, update_call(): pl.pallas_call(kernel, in_specs=in_specs, out_specs=[hbm(), vmem()] if wi...  8.38 us
    pallas_call x1, Pallas kernels, truncate_call(): pl.pallas_call(truncate_kernel, in_specs=[smem(), smem()] + [vmem()] * 6,...  5.71 us
    ppermute x4, waiting for transfers between devices, shards(): side = lax.ppermute(own, 'site', side_swap)  5.58 us
    pallas_call x1, Pallas kernels, root_call(): pl.pallas_call(root_kernel, in_specs=[vmem(), vmem()], out_specs=[vmem(),...  5.05 us
  transfers between devices with their start and end apart: 15, of which 10 were waited for; matrix products, arithmetic and copies ran while one was open for 0% of the time, Pallas kernels for 21%

profile of v2, /device:TPU:6, one launch (start us, length us, event | category | flops | bytes accessed | tf_op | source)
XLA Modules:
  0.0 99.8 jit_solution(415158552561110217)
XLA Ops:
  0.7 4.6 %open.1 = (bf16[2,64,256,128]{3,2,1,0:T(8,128)(2,1)S(1)}, bf16[2,64,128,128]{3,2,1,0:T(8,128)(2,1)S(1)}, f32[8,128]{1,0:T(8,128)S(1)}) custom-call(bf16[2,64,256,128]{3,2,1,0:T(8,128)(2,1)} %bitcast.6), custom_call_target="tpu_custom_call" | custom-call | flops 16777216 | bytes 20971520 | tf_op jit(solution)/shard_map/open/pallas_call | solution.py:184
  5.3 3.3 %collective-permute-start = (f32[8,128]{1,0:T(8,128)S(1)}, f32[8,128]{1,0:T(8,128)S(1)}, u32[]{:S(2)}, u32[]{:S(2)}) collective-permute-start(f32[8,128]{1,0:T(8,128)S(1)} %get-tuple-element.23.after), channel_id=1, source_target_pairs={{0,1},{1,0},{2,3},{3,2},{4,5},{5,4},{6,7},{7,6},{8,9},{9,8},{10,11... | collective-permute-start | bytes 12296 | tf_op jit(solution)/shard_map/ppermute | solution.py:720
  8.6 1.9 %collective-permute-done = f32[8,128]{1,0:T(8,128)S(1)} collective-permute-done((f32[8,128]{1,0:T(8,128)S(1)}, f32[8,128]{1,0:T(8,128)S(1)}, u32[]{:S(2)}, u32[]{:S(2)}) %collective-permute-start) | collective-permute-done | bytes 4128 | tf_op jit(solution)/shard_map/ppermute | solution.py:720
  10.5 7.3 %collective-permute-start.1 = (f32[8,128]{1,0:T(8,128)S(1)}, f32[8,128]{1,0:T(8,128)S(1)}, u32[]{:S(2)}, u32[]{:S(2)}) collective-permute-start(f32[8,128]{1,0:T(8,128)S(1)} %add.12.own_ref), channel_id=1, source_target_pairs={{2,4},{6,8},{10,12},{14,16},{18,20},{22,24},{26,28},{30,32},{34,36... | collective-permute-start | bytes 12296 | tf_op jit(solution)/shard_map/ppermute | solution.py:721
  17.9 2.3 %flatten.2 = (s32[16]{0:T(128)S(1)}, bf16[2,64,128,256]{3,2,1,0:T(8,128)(2,1)S(1)}) custom-call(f32[8,128]{1,0:T(8,128)S(1)} %get-tuple-element.23.after, bf16[2,64,256,128]{3,2,1,0:T(8,128)(2,1)S(1)} %get-tuple-element.24.x_ref, s32[3,128]{1,0:T(4,128)S(1)} %bitcast.4, s32[128]{0:T(128)S(1)} %copy-done.1), custom_call_target="tpu_custom_call" | custom-call | flops 4194304 | bytes 8388608 | tf_op jit(solution)/shard_map/flatten/pallas_call | solution.py:226
  20.2 3.7 %inner_round.3 = (f32[8,128]{1,0:T(8,128)S(1)}, f32[64,128]{1,0:T(8,128)S(1)}, f32[128,128]{1,0:T(8,128)S(1)}) custom-call(s32[16]{0:T(128)S(1)} %get-tuple-element.25.info, f32[8,128]{1,0:T(8,128)S(1)} %add.12.own_ref, f32[8,128]{1,0:T(8,128)S(1)} %collective-permute-done.2.mate_ref, bf16[2,64,128,128]{3,2,1,0:T(8,128)(2,1)S(1)} %get-tuple-element.26.s_ref, ...), custom_call_target="tpu_custom_call" | custom-call | flops 8388608 | bytes 4194304 | tf_op jit(solution)/shard_map/inner_round/pallas_call | solution.py:381
  23.9 0.9 outer_round.3.after
  24.8 2.9 %collective-permute-start.3 = (f32[8,128]{1,0:T(8,128)S(1)}, f32[8,128]{1,0:T(8,128)S(1)}, u32[]{:S(2)}, u32[]{:S(2)}) collective-permute-start(f32[8,128]{1,0:T(8,128)S(1)} %outer_round.3.after), channel_id=1, source_target_pairs={{0,1},{1,0},{2,3},{3,2},{4,5},{5,4},{6,7},{7,6},{8,9},{9,8},{10,11... | collective-permute-start | bytes 12296 | tf_op jit(solution)/shard_map/ppermute | solution.py:720
  27.7 2.2 %collective-permute-done.3 = f32[8,128]{1,0:T(8,128)S(1)} collective-permute-done((f32[8,128]{1,0:T(8,128)S(1)}, f32[8,128]{1,0:T(8,128)S(1)}, u32[]{:S(2)}, u32[]{:S(2)}) %collective-permute-start.3) | collective-permute-done | bytes 4128 | tf_op jit(solution)/shard_map/ppermute | solution.py:720
  29.9 2.5 %collective-permute-start.4 = (f32[8,128]{1,0:T(8,128)S(1)}, f32[8,128]{1,0:T(8,128)S(1)}, u32[]{:S(2)}, u32[]{:S(2)}) collective-permute-start(f32[8,128]{1,0:T(8,128)S(1)} %add.13.own_ref), channel_id=1, source_target_pairs={{2,4},{6,8},{10,12},{14,16},{18,20},{22,24},{26,28},{30,32},{34,36... | collective-permute-start | bytes 12296 | tf_op jit(solution)/shard_map/ppermute | solution.py:721
  32.4 1.2 %flatten.3.after.d_ref = bf16[2,64,128,256]{3,2,1,0:T(8,128)(2,1)S(1)} custom-call(f32[8,128]{1,0:T(8,128)S(1)} %outer_round.3.after, bf16[2,64,256,128]{3,2,1,0:T(8,128)(2,1)S(1)} %get-tuple-element.24.x_ref, bf16[2,64,128,256]{3,2,1,0:T(8,128)(2,1)S(1)} %get-tuple-element.27.after.refs_0_), custom_call_target="tpu_custom_call", output_to_operand_aliasing={{}: (2, {})} | custom-call | flops 4194304 | bytes 8388608 | tf_op jit(solution)/shard_map/flatten/pallas_call | solution.py:226
  33.6 3.7 %inner_round.4 = (f32[8,128]{1,0:T(8,128)S(1)}, f32[64,128]{1,0:T(8,128)S(1)}, f32[128,128]{1,0:T(8,128)S(1)}) custom-call(s32[16]{0:T(128)S(1)} %get-tuple-element.25.info, f32[8,128]{1,0:T(8,128)S(1)} %add.13.own_ref, f32[8,128]{1,0:T(8,128)S(1)} %collective-permute-done.5.mate_ref, bf16[2,64,128,128]{3,2,1,0:T(8,128)(2,1)S(1)} %get-tuple-element.26.s_ref, ...), custom_call_target="tpu_custom_call" | custom-call | flops 8388608 | bytes 4194304 | tf_op jit(solution)/shard_map/inner_round/pallas_call | solution.py:381
  37.8 0.8 outer_round.4
  38.7 2.9 %collective-permute-start.6 = (f32[8,128]{1,0:T(8,128)S(1)}, f32[8,128]{1,0:T(8,128)S(1)}, u32[]{:S(2)}, u32[]{:S(2)}) collective-permute-start(f32[8,128]{1,0:T(8,128)S(1)} %outer_round.4), channel_id=1, source_target_pairs={{0,1},{1,0},{2,3},{3,2},{4,5},{5,4},{6,7},{7,6},{8,9},{9,8},{10,11... | collective-permute-start | bytes 12296 | tf_op jit(solution)/shard_map/ppermute | solution.py:720
  41.6 2.2 %collective-permute-done.6 = f32[8,128]{1,0:T(8,128)S(1)} collective-permute-done((f32[8,128]{1,0:T(8,128)S(1)}, f32[8,128]{1,0:T(8,128)S(1)}, u32[]{:S(2)}, u32[]{:S(2)}) %collective-permute-start.6) | collective-permute-done | bytes 4128 | tf_op jit(solution)/shard_map/ppermute | solution.py:720
  43.8 4.0 %collective-permute-start.7 = (f32[8,128]{1,0:T(8,128)S(1)}, f32[8,128]{1,0:T(8,128)S(1)}, u32[]{:S(2)}, u32[]{:S(2)}) collective-permute-start(f32[8,128]{1,0:T(8,128)S(1)} %add.14.own_ref), channel_id=1, source_target_pairs={{2,4},{6,8},{10,12},{14,16},{18,20},{22,24},{26,28},{30,32},{34,36... | collective-permute-start | bytes 12296 | tf_op jit(solution)/shard_map/ppermute | solution.py:721
  47.9 3.7 %inner_round.5 = (f32[8,128]{1,0:T(8,128)S(1)}, f32[64,128]{1,0:T(8,128)S(1)}, f32[128,128]{1,0:T(8,128)S(1)}) custom-call(s32[16]{0:T(128)S(1)} %get-tuple-element.25.info, f32[8,128]{1,0:T(8,128)S(1)} %add.14.own_ref, f32[8,128]{1,0:T(8,128)S(1)} %collective-permute-done.8.mate_ref, bf16[2,64,128,128]{3,2,1,0:T(8,128)(2,1)S(1)} %get-tuple-element.26.s_ref, ...), custom_call_target="tpu_custom_call" | custom-call | flops 8388608 | bytes 4194304 | tf_op jit(solution)/shard_map/inner_round/pallas_call | solution.py:381
  51.7 0.8 outer_round.5
  52.6 2.9 %collective-permute-start.9 = (f32[8,128]{1,0:T(8,128)S(1)}, f32[8,128]{1,0:T(8,128)S(1)}, u32[]{:S(2)}, u32[]{:S(2)}) collective-permute-start(f32[8,128]{1,0:T(8,128)S(1)} %outer_round.5), channel_id=1, source_target_pairs={{0,1},{1,0},{2,3},{3,2},{4,5},{5,4},{6,7},{7,6},{8,9},{9,8},{10,11... | collective-permute-start | bytes 12296 | tf_op jit(solution)/shard_map/ppermute | solution.py:720
  55.5 2.2 %collective-permute-done.9 = f32[8,128]{1,0:T(8,128)S(1)} collective-permute-done((f32[8,128]{1,0:T(8,128)S(1)}, f32[8,128]{1,0:T(8,128)S(1)}, u32[]{:S(2)}, u32[]{:S(2)}) %collective-permute-start.9) | collective-permute-done | bytes 4128 | tf_op jit(solution)/shard_map/ppermute | solution.py:720
  57.7 2.9 %collective-permute-start.11 = (f32[8,128]{1,0:T(8,128)S(1)}, f32[8,128]{1,0:T(8,128)S(1)}, u32[]{:S(2)}, u32[]{:S(2)}) collective-permute-start(f32[8,128]{1,0:T(8,128)S(1)} %add.15.own_ref), channel_id=1, source_target_pairs={{2,4},{6,8},{10,12},{14,16},{18,20},{22,24},{26,28},{30,32},{34,36... | collective-permute-start | bytes 12296 | tf_op jit(solution)/shard_map/ppermute | solution.py:721
  60.8 4.9 %collective-permute-done.11.side_ref = f32[8,128]{1,0:T(8,128)S(1)} collective-permute-done((f32[8,128]{1,0:T(8,128)S(1)}, f32[8,128]{1,0:T(8,128)S(1)}, u32[]{:S(2)}, u32[]{:S(2)}) %collective-permute-start.11) | collective-permute-done | bytes 4128 | tf_op jit(solution)/shard_map/ppermute | solution.py:721
  65.6 2.4 %gram_to_send.1 = (f32[3,128,128]{2,1,0:T(8,128)S(1)}, f32[3,2,128]{2,1,0:T(2,128)}) custom-call(s32[16]{0:T(128)S(1)} %get-tuple-element.25.info, f32[8,128]{1,0:T(8,128)S(1)} %add.15.own_ref, f32[8,128]{1,0:T(8,128)S(1)} %collective-permute-done.10.mate_ref, f32[8,128]{1,0:T(8,128)S(1)} %collective-permute-done.11.side_ref, ...), custom_call_target="tpu_custom_call" | custom-call | flops 1073741824 | bytes 4194304 | tf_op jit(solution)/shard_map/gram_to_send/pallas_call | solution.py:459
  68.1 3.1 %collective-permute-start.12 = (f32[3,128,128]{2,1,0:T(8,128)S(1)}, f32[3,128,128]{2,1,0:T(8,128)S(1)}, u32[]{:S(2)}, u32[]{:S(2)}) collective-permute-start(f32[3,128,128]{2,1,0:T(8,128)S(1)} %get-tuple-element.37.after), channel_id=1, source_target_pairs={{0,1},{1,0},{2,3},{3,2},{4,5},{5,4},{6,7},{7,6},{8,9},{9,8},{10,11... | collective-permute-start | bytes 589832 | tf_op jit(solution)/shard_map/ppermute | solution.py:724
  71.1 2.3 %gram_to_keep.1.keep_ref = f32[3,128,128]{2,1,0:T(8,128)S(1)} custom-call(s32[16]{0:T(128)S(1)} %get-tuple-element.25.info, f32[8,128]{1,0:T(8,128)S(1)} %add.15.own_ref, f32[8,128]{1,0:T(8,128)S(1)} %collective-permute-done.10.mate_ref, f32[8,128]{1,0:T(8,128)S(1)} %collective-permute-done.11.side_ref, bf16[2,64,128,256]{3,2,1,0:T(8,128)(2,1)S(1)} %flatten.3.after.d_ref, ...), custom_call_target="tpu_custom_call" | custom-call | flops 1073741824 | bytes 4194304 | tf_op jit(solution)/shard_map/gram_to_keep/pallas_call | solution.py:459
  73.5 1.8 %collective-permute-done.12.got_ref = f32[3,128,128]{2,1,0:T(8,128)S(1)} collective-permute-done((f32[3,128,128]{2,1,0:T(8,128)S(1)}, f32[3,128,128]{2,1,0:T(8,128)S(1)}, u32[]{:S(2)}, u32[]{:S(2)}) %collective-permute-start.12) | collective-permute-done | bytes 196640 | tf_op jit(solution)/shard_map/ppermute | solution.py:724
  75.3 5.1 %root.1 = (f32[256,256]{1,0:T(8,128)S(1)}, f32[256,256]{1,0:T(8,128)S(1)}) custom-call(f32[3,128,128]{2,1,0:T(8,128)S(1)} %gram_to_keep.1.keep_ref, f32[3,128,128]{2,1,0:T(8,128)S(1)} %collective-permute-done.12.got_ref), custom_call_target="tpu_custom_call" | custom-call | flops 2214592512 | bytes 1048576 | tf_op jit(solution)/shard_map/root/pallas_call | solution.py:530
  80.6 1.5 %collective-permute-done.13.other_ref = f32[256,256]{1,0:T(8,128)S(1)} collective-permute-done((f32[256,256]{1,0:T(8,128)S(1)}, f32[256,256]{1,0:T(8,128)S(1)}, u32[]{:S(2)}, u32[]{:S(2)}) %collective-permute-start.13) | collective-permute-done | bytes 262176 | tf_op jit(solution)/shard_map/ppermute | solution.py:727
  82.2 5.7 %truncate.1.pack_ref.after = bf16[272,256]{1,0:T(8,128)(2,1)S(1)} custom-call(s32[16]{0:T(128)S(1)} %get-tuple-element.25.info, f32[4,4]{1,0:T(4,128)S(1)} %copy-done.3, f32[8,128]{1,0:T(8,128)S(1)} %add.15.own_ref, f32[8,128]{1,0:T(8,128)S(1)} %collective-permute-done.10.mate_ref, f32[256,256]{1,0:T(8,128)S(1)} %get-tuple-element.38.upper_ref, ...), custom_call_target="tpu_custom_call" | custom-call | flops 1342177280 | bytes 1572864 | tf_op jit(solution)/shard_map/truncate/pallas_call | solution.py:610
  87.9 3.1 %collective-permute-start.14 = (bf16[272,256]{1,0:T(8,128)(2,1)S(1)}, bf16[272,256]{1,0:T(8,128)(2,1)S(1)}, u32[]{:S(2)}, u32[]{:S(2)}) collective-permute-start(bf16[272,256]{1,0:T(8,128)(2,1)S(1)} %truncate.1.pack_ref.after), channel_id=1, source_target_pairs={{0,1},{1,0},{2,3},{3,2},{4,5},{5,4},{6,7},{7,6},{8,9},{9,8},{10,11... | collective-permute-start | bytes 417800 | tf_op jit(solution)/shard_map/ppermute | solution.py:729
  91.0 3.9 %update_own.1.begun_hbm = bf16[2,64,256,128]{3,2,1,0:T(8,128)(2,1)} custom-call(s32[16]{0:T(128)S(1)} %get-tuple-element.25.info, bf16[272,256]{1,0:T(8,128)(2,1)S(1)} %truncate.1.pack_ref.after, bf16[2,64,128,256]{3,2,1,0:T(8,128)(2,1)S(1)} %flatten.3.after.d_ref, bf16[272,256]{1,0:T(8,128)(2,1)S(1)} %truncate.1.pack_ref.after), custom_call_target="tpu_custom_call" | custom-call | flops 1073741824 | bytes 8388608 | tf_op jit(solution)/shard_map/update_own/pallas_call | solution.py:676
  95.2 4.5 %update_other.1 = (bf16[2,64,256,128]{3,2,1,0:T(8,128)(2,1)}, f32[2,128]{1,0:T(2,128)}) custom-call(s32[16]{0:T(128)S(1)} %get-tuple-element.25.info, bf16[272,256]{1,0:T(8,128)(2,1)S(1)} %truncate.1.pack_ref.after, bf16[272,256]{1,0:T(8,128)(2,1)S(1)} %collective-permute-done.14.got_ref, ...), custom_call_target="tpu_custom_call", output_to_operand_aliasing={{0}: (4, {})} | custom-call | flops 1073741824 | bytes 8388608 | tf_op jit(solution)/shard_map/update_other/pallas_call | solution.py:676
  (25 shorter events, 1.4 us)
Async XLA Ops:
  0.6 17.2 %copy-start.1 = (s32[128]{0:T(128)S(1)}, s32[128]{0:T(128)}, u32[]{:S(2)}) copy-start(s32[128]{0:T(128)} %refs_1_.1) | copy-start | bytes 1540
  0.6 17.2 %copy-start = (s32[128,3]{0,1:T(4,128)S(1)}, s32[128,3]{0,1:T(4,128)}, u32[]{:S(2)}) copy-start(s32[128,3]{0,1:T(4,128)} %param.6) | copy-start | bytes 4612
  5.3 5.2 %collective-permute-start = (f32[8,128]{1,0:T(8,128)S(1)}, f32[8,128]{1,0:T(8,128)S(1)}, u32[]{:S(2)}, u32[]{:S(2)}) collective-permute-start(f32[8,128]{1,0:T(8,128)S(1)} %get-tuple-element.23.after), channel_id=1, source_target_pairs={{0,1},{1,0},{2,3},{3,2},{4,5},{5,4},{6,7},{7,6},{8,9},{9,8},{10,11... | collective-permute-start | bytes 12296 | tf_op jit(solution)/shard_map/ppermute | solution.py:720
  10.5 9.7 %collective-permute-start.2 = (f32[8,128]{1,0:T(8,128)S(1)}, f32[8,128]{1,0:T(8,128)S(1)}, u32[]{:S(2)}, u32[]{:S(2)}) collective-permute-start(f32[8,128]{1,0:T(8,128)S(1)} %add.12.own_ref), channel_id=1, source_target_pairs={{0,2},{2,0},{4,6},{6,4},{8,10},{10,8},{12,14},{14,12},{16,18},{18,... | collective-permute-start | bytes 12296 | tf_op jit(solution)/shard_map/ppermute | solution.py:722
  10.5 13.4 %collective-permute-start.1 = (f32[8,128]{1,0:T(8,128)S(1)}, f32[8,128]{1,0:T(8,128)S(1)}, u32[]{:S(2)}, u32[]{:S(2)}) collective-permute-start(f32[8,128]{1,0:T(8,128)S(1)} %add.12.own_ref), channel_id=1, source_target_pairs={{2,4},{6,8},{10,12},{14,16},{18,20},{22,24},{26,28},{30,32},{34,36... | collective-permute-start | bytes 12296 | tf_op jit(solution)/shard_map/ppermute | solution.py:721
  24.8 5.1 %collective-permute-start.3 = (f32[8,128]{1,0:T(8,128)S(1)}, f32[8,128]{1,0:T(8,128)S(1)}, u32[]{:S(2)}, u32[]{:S(2)}) collective-permute-start(f32[8,128]{1,0:T(8,128)S(1)} %outer_round.3.after), channel_id=1, source_target_pairs={{0,1},{1,0},{2,3},{3,2},{4,5},{5,4},{6,7},{7,6},{8,9},{9,8},{10,11... | collective-permute-start | bytes 12296 | tf_op jit(solution)/shard_map/ppermute | solution.py:720
  29.9 3.7 %collective-permute-start.5 = (f32[8,128]{1,0:T(8,128)S(1)}, f32[8,128]{1,0:T(8,128)S(1)}, u32[]{:S(2)}, u32[]{:S(2)}) collective-permute-start(f32[8,128]{1,0:T(8,128)S(1)} %add.13.own_ref), channel_id=1, source_target_pairs={{0,2},{2,0},{4,6},{6,4},{8,10},{10,8},{12,14},{14,12},{16,18},{18,... | collective-permute-start | bytes 12296 | tf_op jit(solution)/shard_map/ppermute | solution.py:722
  29.9 7.9 %collective-permute-start.4 = (f32[8,128]{1,0:T(8,128)S(1)}, f32[8,128]{1,0:T(8,128)S(1)}, u32[]{:S(2)}, u32[]{:S(2)}) collective-permute-start(f32[8,128]{1,0:T(8,128)S(1)} %add.13.own_ref), channel_id=1, source_target_pairs={{2,4},{6,8},{10,12},{14,16},{18,20},{22,24},{26,28},{30,32},{34,36... | collective-permute-start | bytes 12296 | tf_op jit(solution)/shard_map/ppermute | solution.py:721
  38.7 5.1 %collective-permute-start.6 = (f32[8,128]{1,0:T(8,128)S(1)}, f32[8,128]{1,0:T(8,128)S(1)}, u32[]{:S(2)}, u32[]{:S(2)}) collective-permute-start(f32[8,128]{1,0:T(8,128)S(1)} %outer_round.4), channel_id=1, source_target_pairs={{0,1},{1,0},{2,3},{3,2},{4,5},{5,4},{6,7},{7,6},{8,9},{9,8},{10,11... | collective-permute-start | bytes 12296 | tf_op jit(solution)/shard_map/ppermute | solution.py:720
  43.8 4.1 %collective-permute-start.8 = (f32[8,128]{1,0:T(8,128)S(1)}, f32[8,128]{1,0:T(8,128)S(1)}, u32[]{:S(2)}, u32[]{:S(2)}) collective-permute-start(f32[8,128]{1,0:T(8,128)S(1)} %add.14.own_ref), channel_id=1, source_target_pairs={{0,2},{2,0},{4,6},{6,4},{8,10},{10,8},{12,14},{14,12},{16,18},{18,... | collective-permute-start | bytes 12296 | tf_op jit(solution)/shard_map/ppermute | solution.py:722
  43.8 7.9 %collective-permute-start.7 = (f32[8,128]{1,0:T(8,128)S(1)}, f32[8,128]{1,0:T(8,128)S(1)}, u32[]{:S(2)}, u32[]{:S(2)}) collective-permute-start(f32[8,128]{1,0:T(8,128)S(1)} %add.14.own_ref), channel_id=1, source_target_pairs={{2,4},{6,8},{10,12},{14,16},{18,20},{22,24},{26,28},{30,32},{34,36... | collective-permute-start | bytes 12296 | tf_op jit(solution)/shard_map/ppermute | solution.py:721
  52.6 5.1 %collective-permute-start.9 = (f32[8,128]{1,0:T(8,128)S(1)}, f32[8,128]{1,0:T(8,128)S(1)}, u32[]{:S(2)}, u32[]{:S(2)}) collective-permute-start(f32[8,128]{1,0:T(8,128)S(1)} %outer_round.5), channel_id=1, source_target_pairs={{0,1},{1,0},{2,3},{3,2},{4,5},{5,4},{6,7},{7,6},{8,9},{9,8},{10,11... | collective-permute-start | bytes 12296 | tf_op jit(solution)/shard_map/ppermute | solution.py:720
  57.7 7.9 %collective-permute-start.11 = (f32[8,128]{1,0:T(8,128)S(1)}, f32[8,128]{1,0:T(8,128)S(1)}, u32[]{:S(2)}, u32[]{:S(2)}) collective-permute-start(f32[8,128]{1,0:T(8,128)S(1)} %add.15.own_ref), channel_id=1, source_target_pairs={{2,4},{6,8},{10,12},{14,16},{18,20},{22,24},{26,28},{30,32},{34,36... | collective-permute-start | bytes 12296 | tf_op jit(solution)/shard_map/ppermute | solution.py:721
  60.7 5.0 %collective-permute-start.10 = (f32[8,128]{1,0:T(8,128)S(1)}, f32[8,128]{1,0:T(8,128)S(1)}, u32[]{:S(2)}, u32[]{:S(2)}) collective-permute-start(f32[8,128]{1,0:T(8,128)S(1)} %add.15.own_ref), channel_id=1, source_target_pairs={{0,2},{2,0},{4,6},{6,4},{8,10},{10,8},{12,14},{14,12},{16,18},{18,... | collective-permute-start | bytes 12296 | tf_op jit(solution)/shard_map/ppermute | solution.py:722
  68.0 14.1 %copy-start.2 = (f32[512,128]{1,0:T(8,128)S(1)}, f32[512,128]{1,0:T(8,128)}, u32[]{:S(2)}) copy-start(f32[512,128]{1,0:T(8,128)} %probes_ref.1) | copy-start | bytes 786436
  68.0 14.1 %copy-start.3 = (f32[4,4]{1,0:T(4,128)S(1)}, f32[4,4]{1,0:T(4,128)}, u32[]{:S(2)}) copy-start(f32[4,4]{1,0:T(4,128)} %gate.1) | copy-start | bytes 196
  68.1 7.3 %collective-permute-start.12 = (f32[3,128,128]{2,1,0:T(8,128)S(1)}, f32[3,128,128]{2,1,0:T(8,128)S(1)}, u32[]{:S(2)}, u32[]{:S(2)}) collective-permute-start(f32[3,128,128]{2,1,0:T(8,128)S(1)} %get-tuple-element.37.after), channel_id=1, source_target_pairs={{0,1},{1,0},{2,3},{3,2},{4,5},{5,4},{6,7},{7,6},{8,9},{9,8},{10,11... | collective-permute-start | bytes 589832 | tf_op jit(solution)/shard_map/ppermute | solution.py:724
  80.4 1.8 %collective-permute-start.13 = (f32[256,256]{1,0:T(8,128)S(1)}, f32[256,256]{1,0:T(8,128)S(1)}, u32[]{:S(2)}, u32[]{:S(2)}) collective-permute-start(f32[256,256]{1,0:T(8,128)S(1)} %get-tuple-element.38.upper_ref), channel_id=1, source_target_pairs={{0,2},{2,0},{4,6},{6,4},{8,10},{10,8},{12,14},{14,12},{16,18},{18,... | collective-permute-start | bytes 786440 | tf_op jit(solution)/shard_map/ppermute | solution.py:727
  87.9 7.3 %collective-permute-start.14 = (bf16[272,256]{1,0:T(8,128)(2,1)S(1)}, bf16[272,256]{1,0:T(8,128)(2,1)S(1)}, u32[]{:S(2)}, u32[]{:S(2)}) collective-permute-start(bf16[272,256]{1,0:T(8,128)(2,1)S(1)} %truncate.1.pack_ref.after), channel_id=1, source_target_pairs={{0,1},{1,0},{2,3},{3,2},{4,5},{5,4},{6,7},{7,6},{8,9},{9,8},{10,11... | collective-permute-start | bytes 417800 | tf_op jit(solution)/shard_map/ppermute | solution.py:729

commit v3 on v2

--- a/solution.py
+++ b/solution.py
@@ -76,9 +76,9 @@
 
 
 def inner_incoming(info, own, mate):
-    odd = info[CORE] == 1
-    place = jnp.where(odd, info[MATE0], info[MATE1])
-    joined = place == info[CORE]
+    odd = info[0, CORE] == 1
+    place = jnp.where(odd, info[0, MATE0], info[0, MATE1])
+    joined = place == info[0, CORE]
     chain = jnp.where(odd, pick(mate, 1, 1), pick(mate, 0, 0))
     gated = jnp.where(odd, pick(mate, 1, 2), pick(mate, 0, 2))
     near = chain + jnp.where(joined, gated, 0.0)
@@ -92,19 +92,19 @@
 
 
 def outer_known(info, own, mate):
-    odd = info[CORE] == 1
-    place = jnp.where(odd, info[MATE1], info[MATE0])
+    odd = info[0, CORE] == 1
+    place = jnp.where(odd, info[0, MATE1], info[0, MATE0])
     home = jnp.where(odd, pick(own, 0, 1), pick(own, 1, 0))
     return (home, jnp.where(place < 0, level(own), from_mate(mate, place)))
 
 
 def outer_far(info, side):
-    far = jnp.where(info[CORE] == 1, pick(side, 0, 0), pick(side, 1, 1))
-    return jnp.where(info[FIRST] + info[LAST] > 0, level(side), far)
+    far = jnp.where(info[0, CORE] == 1, pick(side, 0, 0), pick(side, 1, 1))
+    return jnp.where(info[0, FIRST] + info[0, LAST] > 0, level(side), far)
 
 
 def outer_incoming(info, own, mate, side):
-    odd = info[CORE] == 1
+    odd = info[0, CORE] == 1
     home, third = outer_known(info, own, mate)
     far = outer_far(info, side)
     return (jnp.where(odd, home, far), jnp.where(odd, far, home), third)
@@ -118,25 +118,44 @@
     return pl.BlockSpec(memory_space=pl.ANY)
 
 
-def write_scalars(near, ranks, info):
+def scalars_kernel(after, near, ranks, out_ref):
     device, row = (lax.axis_index("site"), lax.axis_index("row"))
     core = lax.rem(device, 2)
     base = 2 * (device - core)
     even0, even1 = (near[2, base] - base, near[2, base + 1] - base)
     odd0, odd1 = (near[2, base + 2], near[2, base + 3])
     odd = core == 1
-    info[MATE0] = jnp.where(odd, jnp.where(odd0 < 0, -1, odd0 - base), jnp.maximum(even0 - 2, -1))
-    info[MATE1] = jnp.where(odd, jnp.where(odd1 < 0, -1, odd1 - base), jnp.maximum(even1 - 2, -1))
     crossed = jnp.logical_or(even0 == 3, even1 == 2)
     kept = jnp.where(jnp.logical_and(odd, crossed), 1 - row, row)
     site = 2 * device + kept
-    info[CORE] = core
-    info[ROW] = row
-    info[FIRST] = (device == 0).astype(jnp.int32)
-    info[LAST] = (device == lax.axis_size("site") - 1).astype(jnp.int32)
-    info[KEPT] = kept
-    info[RANK] = ranks[site]
-    info[GATED] = (near[2, site] >= 0).astype(jnp.int32)
+    values = {
+        CORE: core,
+        ROW: row,
+        MATE0: jnp.where(odd, jnp.where(odd0 < 0, -1, odd0 - base), jnp.maximum(even0 - 2, -1)),
+        MATE1: jnp.where(odd, jnp.where(odd1 < 0, -1, odd1 - base), jnp.maximum(even1 - 2, -1)),
+        FIRST: (device == 0).astype(jnp.int32),
+        LAST: (device == lax.axis_size("site") - 1).astype(jnp.int32),
+        KEPT: kept,
+        RANK: ranks[site],
+        GATED: (near[2, site] >= 0).astype(jnp.int32),
+    }
+    lanes = lax.broadcasted_iota(jnp.int32, out_ref.shape, 1)
+    total = jnp.zeros(out_ref.shape, jnp.int32)
+    for place, value in values.items():
+        total = jnp.where(lanes == place, value, total)
+    out_ref[...] = total
+
+
+def scalars_call(after, near, ranks):
+    return pl.pallas_call(
+        scalars_kernel,
+        in_specs=[anywhere(), smem(), smem()],
+        out_specs=vmem(),
+        out_shape=jax.ShapeDtypeStruct((8, 128), jnp.int32),
+        compiler_params=params(4),
+        cost_estimate=cost(1024, 1 << 20),
+        name="scalars",
+    )(after, near, ranks)
 
 
 def open_kernel(x_hbm, x_ref, s_ref, out_ref, scratch, sums_ref, total_ref, sems):
@@ -202,38 +221,32 @@
     )(x)
 
 
-def flatten_kernel(after, x_ref, *refs, member):
-    flat_ref, scratch = refs[-2:]
-    rows, bond = flat_ref.shape[1:3]
-    if member == 0:
-        write_scalars(*refs[:3])
-
-    def body(index, carry):
-        lane = scratch.at[lax.rem(index, scratch.shape[0])]
-        lane[...] = x_ref[member, index].astype(F32)
-        parts = [lane[pl.ds(place, bond, 2), :] for place in range(2)]
-        flat_ref[member, index] = jnp.concatenate(parts, axis=1).astype(BF16)
-        return carry
-
-    lax.fori_loop(0, rows, body, 0, unroll=8)
-
-
-def flatten_call(after, x, member, *more):
+def flatten_kernel(after, x_ref, flat_ref, scratch):
+    members, rows, bond = flat_ref.shape[:3]
+    for member in range(members):
+
+        def body(index, carry):
+            lane = scratch.at[lax.rem(index, scratch.shape[0])]
+            lane[...] = x_ref[member, index].astype(F32)
+            parts = [lane[pl.ds(place, bond, 2), :] for place in range(2)]
+            flat_ref[member, index] = jnp.concatenate(parts, axis=1).astype(BF16)
+            return carry
+
+        lax.fori_loop(0, rows, body, 0, unroll=8)
+
+
+def flatten_call(after, x):
     members, rows, wide, bond = x.shape
-    flat = jax.ShapeDtypeStruct((members, rows, bond, wide), BF16)
-    info = jax.ShapeDtypeStruct((16,), jnp.int32)
-    first = member == 0
-    return pl.pallas_call(
-        functools.partial(flatten_kernel, member=member),
-        in_specs=[anywhere(), vmem()] + ([smem(), smem()] if first else [vmem()]),
-        out_specs=[smem(), vmem()] if first else vmem(),
-        out_shape=[info, flat] if first else flat,
-        input_output_aliases={} if first else {2: 0},
+    return pl.pallas_call(
+        flatten_kernel,
+        in_specs=[anywhere(), vmem()],
+        out_specs=vmem(),
+        out_shape=jax.ShapeDtypeStruct((members, rows, bond, wide), BF16),
         scratch_shapes=[pltpu.VMEM((8, wide, bond), F32)],
         compiler_params=params(8),
-        cost_estimate=cost(x.size, 2 * x.size),
+        cost_estimate=cost(2 * x.size, 4 * x.size),
         name="flatten",
-    )(after, x, *more)
+    )(after, x)
 
 
 def halved(row_index, row):
@@ -287,8 +300,8 @@
 
 def contract_inner(info, weights, s_ref, out_ref, first_ref, sums_ref):
     rows, bond = s_ref.shape[1:3]
-    member = 1 - info[CORE]
-    start = info[ROW] * rows
+    member = 1 - info[0, CORE]
+    start = info[0, ROW] * rows
     first, second, third = weights
     third = third.astype(BF16).astype(F32)
     first_ref[...] = down(first)
@@ -305,14 +318,14 @@
         return total + scaled_sum(s_ref, member, step, first_ref, start)
 
     total = lax.fori_loop(0, rows // GROUP, body, jnp.zeros((bond, bond), F32), unroll=2)
-    finish(info[ROW], out_ref, member, sums_ref[...], total, third, second_down)
+    finish(info[0, ROW], out_ref, member, sums_ref[...], total, third, second_down)
 
 
 def contract_outer(info, home, third, s_ref, out_ref, mixed_ref, other_ref, first_ref):
     rows, bond = s_ref.shape[1:3]
-    member = info[CORE]
-    odd = info[CORE] == 1
-    start = info[ROW] * rows
+    member = info[0, CORE]
+    odd = info[0, CORE] == 1
+    start = info[0, ROW] * rows
     third_rows = jnp.broadcast_to(third.astype(BF16), (8, bond))
 
     def mix(step, carry):
@@ -333,7 +346,7 @@
 
         zero = jnp.zeros((bond, bond), F32)
         other_ref[...] = lax.fori_loop(0, rows // GROUP, body, zero, unroll=2)
-        put_leg(out_ref, member, 1, by_row(halved(info[ROW], home), mixed_ref[...]))
+        put_leg(out_ref, member, 1, by_row(halved(info[0, ROW], home), mixed_ref[...]))
 
     @pl.when(jnp.logical_not(odd))
     def over_second():
@@ -348,10 +361,10 @@
             return carry
 
         lax.fori_loop(0, rows // 2, body, 0, unroll=8)
-        put_leg(out_ref, member, 0, placed(info[ROW], by_column(home, mixed_ref[...])))
-
-
-def inner_kernel(info, own_ref, mate_ref, s_ref, after, out_ref, mixed_ref, other_ref, first_ref, sums_ref):
+        put_leg(out_ref, member, 0, placed(info[0, ROW], by_column(home, mixed_ref[...])))
+
+
+def inner_kernel(info, own_ref, mate_ref, s_ref, out_ref, mixed_ref, other_ref, first_ref, sums_ref):
     own, mate = (normalized(own_ref), normalized(mate_ref))
     out_ref[...] = jnp.ones(out_ref.shape, F32)
     contract_inner(info, inner_incoming(info, own, mate), s_ref, out_ref, first_ref, sums_ref)
@@ -364,23 +377,23 @@
     far = outer_far(info, normalized(side_ref))
     out_ref[...] = part_ref[...]
 
-    @pl.when(info[CORE] == 1)
+    @pl.when(info[0, CORE] == 1)
     def as_second():
-        put_leg(out_ref, 1, 0, placed(info[ROW], by_column(far, mixed_ref[...])))
+        put_leg(out_ref, 1, 0, placed(info[0, ROW], by_column(far, mixed_ref[...])))
         put_leg(out_ref, 1, 2, by_row(far, other_ref[...]))
 
-    @pl.when(info[CORE] == 0)
+    @pl.when(info[0, CORE] == 0)
     def as_first():
-        half = halved(info[ROW], far)
+        half = halved(info[0, ROW], far)
         put_leg(out_ref, 0, 1, by_row(half, mixed_ref[...]))
         put_leg(out_ref, 0, 2, by_row(half, other_ref[:rows]))
 
 
-def inner_call(info, own, mate, squares, after):
+def inner_call(info, own, mate, squares):
     rows, bond = squares.shape[1:3]
     return pl.pallas_call(
         inner_kernel,
-        in_specs=[smem(), vmem(), vmem(), vmem(), anywhere()],
+        in_specs=[vmem(), vmem(), vmem(), vmem()],
         out_specs=[vmem(), vmem(), vmem()],
         out_shape=[
             jax.ShapeDtypeStruct((8, bond), F32),
@@ -391,13 +404,13 @@
         compiler_params=params(8),
         cost_estimate=cost(4 * squares.size, 2 * squares.size),
         name="inner_round",
-    )(info, own, mate, squares, after)
+    )(info, own, mate, squares)
 
 
 def outer_call(info, side, part, mixed, other):
     return pl.pallas_call(
         outer_kernel,
-        in_specs=[smem(), vmem(), vmem(), vmem(), vmem()],
+        in_specs=[vmem(), vmem(), vmem(), vmem(), vmem()],
         out_specs=vmem(),
         out_shape=jax.ShapeDtypeStruct(part.shape, F32),
         compiler_params=params(8),
@@ -409,7 +422,7 @@
 def add_gram(info, member, weights, d_ref, out_ref, first_ref, gram):
     rows, bond = d_ref.shape[1:3]
     block = 32
-    start = info[ROW] * rows
+    start = info[0, ROW] * rows
     first_ref[...] = jnp.sqrt(down(weights[0]))
     second = jnp.sqrt(down(weights[1]))
     gram[...] = jnp.zeros(gram.shape, F32)
@@ -435,11 +448,17 @@
     own, mate, side = (normalized(own_ref), normalized(mate_ref), normalized(side_ref))
     inner = inner_incoming(info, own, mate)
     outer = outer_incoming(info, own, mate, side)
-    return [jnp.where(member == info[CORE], outer[leg], inner[leg]) for leg in range(2)]
-
-
-def send_kernel(info, own_ref, mate_ref, side_ref, d_ref, out_ref, msg_ref, first_ref, gram):
-    member = 1 - info[KEPT]
+    return [jnp.where(member == info[0, CORE], outer[leg], inner[leg]) for leg in range(2)]
+
+
+def send_kernel(info, own_ref, mate_ref, side_ref, d_ref, out_ref, first_ref, gram):
+    member = 1 - info[0, KEPT]
+    weights = gram_weights(info, member, own_ref, mate_ref, side_ref)
+    add_gram(info, member, weights, d_ref, out_ref, first_ref, gram)
+
+
+def keep_kernel(info, own_ref, mate_ref, side_ref, d_ref, after, out_ref, msg_ref, first_ref, gram):
+    member = info[0, KEPT]
     weights = gram_weights(info, member, own_ref, mate_ref, side_ref)
     own = normalized(own_ref)
     for place in range(2):
@@ -448,17 +467,11 @@
     add_gram(info, member, weights, d_ref, out_ref, first_ref, gram)
 
 
-def keep_kernel(info, own_ref, mate_ref, side_ref, d_ref, after, out_ref, first_ref, gram):
-    member = info[KEPT]
-    weights = gram_weights(info, member, own_ref, mate_ref, side_ref)
-    add_gram(info, member, weights, d_ref, out_ref, first_ref, gram)
-
-
 def gram_call(kernel, name, extra_specs, out_specs, out_shape, flat, operands):
     rows, bond, wide = flat.shape[1:]
     return pl.pallas_call(
         kernel,
-        in_specs=[smem()] + [vmem()] * 4 + extra_specs,
+        in_specs=[vmem()] + [vmem()] * 4 + extra_specs,
         out_specs=out_specs,
         out_shape=out_shape,
         scratch_shapes=[pltpu.VMEM((bond, bond), F32), pltpu.VMEM((wide, wide), F32)],
@@ -469,20 +482,20 @@
 
 
 def send_call(info, own, mate, side, flat):
+    bond = flat.shape[2]
+    shape = jax.ShapeDtypeStruct((3, bond, bond), F32)
+    operands = (info, own, mate, side, flat)
+    return gram_call(send_kernel, "gram_to_send", [], vmem(), shape, flat, operands)
+
+
+def keep_call(info, own, mate, side, flat, after):
     members, _, bond, _ = flat.shape
     shapes = [
         jax.ShapeDtypeStruct((3, bond, bond), F32),
         jax.ShapeDtypeStruct((3, members, bond), F32),
     ]
-    operands = (info, own, mate, side, flat)
-    return gram_call(send_kernel, "gram_to_send", [], [vmem(), vmem()], shapes, flat, operands)
-
-
-def keep_call(info, own, mate, side, flat, after):
-    bond = flat.shape[2]
-    shape = jax.ShapeDtypeStruct((3, bond, bond), F32)
     operands = (info, own, mate, side, flat, after)
-    return gram_call(keep_kernel, "gram_to_keep", [anywhere()], vmem(), shape, flat, operands)
+    return gram_call(keep_kernel, "gram_to_keep", [anywhere()], [vmem(), vmem()], shapes, flat, operands)
 
 
 def eye_mask(size):
@@ -540,9 +553,9 @@
 
 def truncate_kernel(info, gate, own_ref, mate_ref, upper_ref, inverse_ref, other_ref, probes_ref, out_ref):
     wide, bond = (upper_ref.shape[0], probes_ref.shape[1])
-    odd = info[CORE] == 1
-    kept = info[KEPT]
-    mate_place = jnp.maximum(jnp.where(kept == 0, info[MATE0], info[MATE1]), 0)
+    odd = info[0, CORE] == 1
+    kept = info[0, KEPT]
+    mate_place = jnp.maximum(jnp.where(kept == 0, info[0, MATE0], info[0, MATE1]), 0)
     own_msg = own_ref[pl.ds(3 * kept + 2, 1), :]
     mate_msg = mate_ref[pl.ds(3 * mate_place + 2, 1), :]
     own_msg = own_msg / jnp.sum(own_msg, axis=1, keepdims=True)
@@ -573,7 +586,7 @@
         return jnp.concatenate(block_rows, axis=0)
 
     across = lax.broadcasted_iota(jnp.int32, (1, bond), 1)
-    mask = (across < info[RANK]).astype(F32)
+    mask = (across < info[0, RANK]).astype(F32)
     strength_down = down(strength)
     probes = jnp.concatenate(
         [probes_ref[pl.ds(0, wide, 2), :] * mask, probes_ref[pl.ds(1, wide, 2), :] * mask], axis=1
@@ -598,7 +611,7 @@
     new_bond = jnp.sqrt((squares[:, :bond] + squares[:, bond:]) / (2 * wide) + 1e-06)
     target = jnp.where(odd, coeffs / jnp.concatenate([new_bond, new_bond], axis=1), basis)
     change = dot3(halves(inverse_ref[...]), halves(target))
-    gated = info[GATED] == 1
+    gated = info[0, GATED] == 1
     identity = eye_mask(wide).astype(F32)
     out_ref[:wide] = jnp.where(gated, change, identity).astype(BF16)
     bond_parts = halves(jnp.where(gated, new_bond, 0.0))
@@ -609,7 +622,7 @@
     wide = upper.shape[0]
     return pl.pallas_call(
         truncate_kernel,
-        in_specs=[smem(), smem()] + [vmem()] * 6,
+        in_specs=[vmem()] * 8,
         out_specs=vmem(),
         out_shape=jax.ShapeDtypeStruct((wide + 16, wide), BF16),
         compiler_params=params(32),
@@ -653,19 +666,22 @@
 
 
 def own_kernel(info, pack_ref, d_ref, after, out_hbm, held, scratch, sems):
-    update_member(info[KEPT], pack_ref, d_ref, out_hbm, held, scratch, sems)
-
-
-def other_kernel(info, pack_ref, got_ref, d_ref, begun_hbm, out_hbm, bond_ref, held, scratch, sems):
+    update_member(info[0, KEPT], pack_ref, d_ref, out_hbm, held, scratch, sems)
+
+
+def other_kernel(info, pack_ref, got_ref, d_ref, begun_hbm, out_hbm, bond_hbm, held, scratch, sems, bond_ref, bond_sem):
     bond, wide = d_ref.shape[2:]
-    kept = info[KEPT]
+    kept = info[0, KEPT]
     tail = pack_ref[wide:].astype(F32)
     got = got_ref[wide:].astype(F32)
     mine = tail[:1, :bond] + tail[:1, bond:]
     other = got[:1, :bond] + got[:1, bond:]
     bond_ref[pl.ds(0, 1), :] = jnp.where(kept == 0, mine, other)
     bond_ref[pl.ds(1, 1), :] = jnp.where(kept == 0, other, mine)
+    bond_copy = pltpu.make_async_copy(bond_ref, bond_hbm, bond_sem)
+    bond_copy.start()
     update_member(1 - kept, got_ref, d_ref, out_hbm, held, scratch, sems)
+    bond_copy.wait()
 
 
 def update_call(kernel, name, in_specs, aliases, with_bonds, flat, operands):
@@ -676,14 +692,15 @@
     return pl.pallas_call(
         kernel,
         in_specs=in_specs,
-        out_specs=[hbm(), vmem()] if with_bonds else hbm(),
+        out_specs=[hbm(), hbm()] if with_bonds else hbm(),
         out_shape=[tensor, bonds] if with_bonds else tensor,
         input_output_aliases=aliases,
         scratch_shapes=[
             pltpu.VMEM((slots, block, wide, bond), BF16),
             pltpu.VMEM((4, wide, bond), F32),
             pltpu.SemaphoreType.DMA((slots,)),
-        ],
+        ]
+        + ([pltpu.VMEM((members, bond), F32), pltpu.SemaphoreType.DMA(())] if with_bonds else []),
         compiler_params=params(24),
         cost_estimate=cost(wide * flat.size, 2 * flat.size),
         name=name,
@@ -691,12 +708,12 @@
 
 
 def own_call(info, pack, flat, after):
-    specs = [smem(), vmem(), vmem(), anywhere()]
+    specs = [vmem(), vmem(), vmem(), anywhere()]
     return update_call(own_kernel, "update_own", specs, {}, False, flat, (info, pack, flat, after))
 
 
 def other_call(info, pack, got, flat, begun):
-    specs = [smem(), vmem(), vmem(), vmem(), hbm()]
+    specs = [vmem(), vmem(), vmem(), vmem(), hbm()]
     operands = (info, pack, got, flat, begun)
     return update_call(other_kernel, "update_other", specs, {4: 0}, True, flat, operands)
 
@@ -710,19 +727,18 @@
     side_swap += [(j, i) for i, j in side_swap]
     x = tensors.reshape(members, rows, bond * phys, bond)
     x, squares, part = open_call(x)
-    info, flat = flatten_call(part, x, 0, neighbours.T, edge_ranks)
+    info = scalars_call(part, neighbours.T, edge_ranks)
     for index in range(ROUNDS):
         if index > 0:
-            begun = inner_call(info, own, mate, squares, flat)
+            begun = inner_call(info, own, mate, squares)
             part = outer_call(info, side, *begun)
-        if index == 1:
-            flat = flatten_call(part, x, 1, flat)
         own = part + lax.ppermute(part, "row", row_swap)
         side = lax.ppermute(own, "site", side_swap)
         mate = lax.ppermute(own, "site", core_swap)
-    send, messages = send_call(info, own, mate, side, flat)
+    flat = flatten_call(own, x)
+    send = send_call(info, own, mate, side, flat)
     got = lax.ppermute(send, "row", row_swap)
-    keep = keep_call(info, own, mate, side, flat, send)
+    keep, messages = keep_call(info, own, mate, side, flat, send)
     upper, inverse = root_call(keep, got)
     other = lax.ppermute(upper, "site", core_swap)
     pack = truncate_call(info, gate_matrix, own, mate, upper, inverse, other, probes)

time: 100 us -> 94.6 us (0.946)
  Pallas kernels: 45.7 us -> 39.5 us
  waiting for transfers between devices: 17.8 us -> 20.3 us
  starting transfers between devices: 35.3 us -> 33.6 us
    pallas_call x13, Pallas kernels: 36 us -> 29.8 us  [the longest x3 9.62 us: inner_call(): pl.pallas_call(inner_kernel, in_specs=[vmem(), vmem(), vmem(), vmem()], o...]
    ppermute x4, starting transfers between devices: 16.8 us -> 15.2 us  [shards(): side = lax.ppermute(own, 'site', side_swap)]
    ppermute x4, waiting for transfers between devices: 5.58 us -> 7 us  [shards(): side = lax.ppermute(own, 'site', side_swap)]
  transfers between devices with their start and end apart: 15 -> 15, of which waited for: 10 -> 10; matrix products, arithmetic and copies ran while one was open for 0% -> 0% of each run, Pallas kernels for 21% -> 19%
where the time goes in v3:
time: 94.6 us; the launch traced here: 94.3 us
  Pallas kernels  39.5 us (42%)
  starting transfers between devices  33.6 us (36%)
  waiting for transfers between devices  20.3 us (21%)
  between operations  0.98 us (1%)
    ppermute x4, starting transfers between devices, shards(): side = lax.ppermute(own, 'site', side_swap)  15.2 us
    ppermute x4, starting transfers between devices, shards(): own = part + lax.ppermute(part, 'row', row_swap)  12 us
    pallas_call x3, Pallas kernels, inner_call(): pl.pallas_call(inner_kernel, in_specs=[vmem(), vmem(), vmem(), vmem()], o...  9.62 us
    ppermute x4, waiting for transfers between devices, shards(): own = part + lax.ppermute(part, 'row', row_swap)  8.55 us
    ppermute x4, waiting for transfers between devices, shards(): side = lax.ppermute(own, 'site', side_swap)  7 us
    pallas_call x2, Pallas kernels, update_call(): pl.pallas_call(kernel, in_specs=in_specs, out_specs=[hbm(), hbm()] if wit...  6.95 us
    pallas_call x1, Pallas kernels, truncate_call(): pl.pallas_call(truncate_kernel, in_specs=[vmem()] * 8, out_specs=vmem(),...  5.27 us
    pallas_call x1, Pallas kernels, root_call(): pl.pallas_call(root_kernel, in_specs=[vmem(), vmem()], out_specs=[vmem(),...  5.05 us
  transfers between devices with their start and end apart: 15, of which 10 were waited for; matrix products, arithmetic and copies ran while one was open for 0% of the time, Pallas kernels for 19%

profile of v3, /device:TPU:6, one launch (start us, length us, event | category | flops | bytes accessed | tf_op | source)
XLA Modules:
  0.0 94.3 jit_solution(18180625483507301629)
XLA Ops:
  0.7 4.6 %open.1 = (bf16[2,64,256,128]{3,2,1,0:T(8,128)(2,1)S(1)}, bf16[2,64,128,128]{3,2,1,0:T(8,128)(2,1)S(1)}, f32[8,128]{1,0:T(8,128)S(1)}) custom-call(bf16[2,64,256,128]{3,2,1,0:T(8,128)(2,1)} %bitcast.6), custom_call_target="tpu_custom_call" | custom-call | flops 16777216 | bytes 20971520 | tf_op jit(solution)/shard_map/open/pallas_call | solution.py:203
  5.3 3.3 %collective-permute-start = (f32[8,128]{1,0:T(8,128)S(1)}, f32[8,128]{1,0:T(8,128)S(1)}, u32[]{:S(2)}, u32[]{:S(2)}) collective-permute-start(f32[8,128]{1,0:T(8,128)S(1)} %get-tuple-element.21.after), channel_id=1, source_target_pairs={{0,1},{1,0},{2,3},{3,2},{4,5},{5,4},{6,7},{7,6},{8,9},{9,8},{10,11... | collective-permute-start | bytes 12296 | tf_op jit(solution)/shard_map/ppermute | solution.py:735
  8.6 1.9 %collective-permute-done = f32[8,128]{1,0:T(8,128)S(1)} collective-permute-done((f32[8,128]{1,0:T(8,128)S(1)}, f32[8,128]{1,0:T(8,128)S(1)}, u32[]{:S(2)}, u32[]{:S(2)}) %collective-permute-start) | collective-permute-done | bytes 4128 | tf_op jit(solution)/shard_map/ppermute | solution.py:735
  10.5 7.3 %collective-permute-start.1 = (f32[8,128]{1,0:T(8,128)S(1)}, f32[8,128]{1,0:T(8,128)S(1)}, u32[]{:S(2)}, u32[]{:S(2)}) collective-permute-start(f32[8,128]{1,0:T(8,128)S(1)} %add.12.own_ref), channel_id=1, source_target_pairs={{2,4},{6,8},{10,12},{14,16},{18,20},{22,24},{26,28},{30,32},{34,36... | collective-permute-start | bytes 12296 | tf_op jit(solution)/shard_map/ppermute | solution.py:736
  17.9 0.6 scalars.1.info
  18.5 3.2 %inner_round.3 = (f32[8,128]{1,0:T(8,128)S(1)}, f32[64,128]{1,0:T(8,128)S(1)}, f32[128,128]{1,0:T(8,128)S(1)}) custom-call(s32[8,128]{1,0:T(8,128)S(1)} %scalars.1.info, f32[8,128]{1,0:T(8,128)S(1)} %add.12.own_ref, f32[8,128]{1,0:T(8,128)S(1)} %collective-permute-done.2.mate_ref, bf16[2,64,128,128]{3,2,1,0:T(8,128)(2,1)S(1)} %get-tuple-element.22.s_ref), custom_call_target="tpu_custom_call" | custom-call | flops 8388608 | bytes 4194304 | tf_op jit(solution)/shard_map/inner_round/pallas_call | solution.py:394
  22.1 2.9 %collective-permute-start.3 = (f32[8,128]{1,0:T(8,128)S(1)}, f32[8,128]{1,0:T(8,128)S(1)}, u32[]{:S(2)}, u32[]{:S(2)}) collective-permute-start(f32[8,128]{1,0:T(8,128)S(1)} %outer_round.3), channel_id=1, source_target_pairs={{0,1},{1,0},{2,3},{3,2},{4,5},{5,4},{6,7},{7,6},{8,9},{9,8},{10,11... | collective-permute-start | bytes 12296 | tf_op jit(solution)/shard_map/ppermute | solution.py:735
  25.0 2.2 %collective-permute-done.3 = f32[8,128]{1,0:T(8,128)S(1)} collective-permute-done((f32[8,128]{1,0:T(8,128)S(1)}, f32[8,128]{1,0:T(8,128)S(1)}, u32[]{:S(2)}, u32[]{:S(2)}) %collective-permute-start.3) | collective-permute-done | bytes 4128 | tf_op jit(solution)/shard_map/ppermute | solution.py:735
  27.2 3.0 %collective-permute-start.4 = (f32[8,128]{1,0:T(8,128)S(1)}, f32[8,128]{1,0:T(8,128)S(1)}, u32[]{:S(2)}, u32[]{:S(2)}) collective-permute-start(f32[8,128]{1,0:T(8,128)S(1)} %add.13.own_ref), channel_id=1, source_target_pairs={{2,4},{6,8},{10,12},{14,16},{18,20},{22,24},{26,28},{30,32},{34,36... | collective-permute-start | bytes 12296 | tf_op jit(solution)/shard_map/ppermute | solution.py:736
  30.3 3.2 %inner_round.4 = (f32[8,128]{1,0:T(8,128)S(1)}, f32[64,128]{1,0:T(8,128)S(1)}, f32[128,128]{1,0:T(8,128)S(1)}) custom-call(s32[8,128]{1,0:T(8,128)S(1)} %scalars.1.info, f32[8,128]{1,0:T(8,128)S(1)} %add.13.own_ref, f32[8,128]{1,0:T(8,128)S(1)} %collective-permute-done.5.mate_ref, bf16[2,64,128,128]{3,2,1,0:T(8,128)(2,1)S(1)} %get-tuple-element.22.s_ref), custom_call_target="tpu_custom_call" | custom-call | flops 8388608 | bytes 4194304 | tf_op jit(solution)/shard_map/inner_round/pallas_call | solution.py:394
  33.5 1.7 %collective-permute-done.4.side_ref = f32[8,128]{1,0:T(8,128)S(1)} collective-permute-done((f32[8,128]{1,0:T(8,128)S(1)}, f32[8,128]{1,0:T(8,128)S(1)}, u32[]{:S(2)}, u32[]{:S(2)}) %collective-permute-start.4) | collective-permute-done | bytes 4128 | tf_op jit(solution)/shard_map/ppermute | solution.py:736
  35.5 2.9 %collective-permute-start.6 = (f32[8,128]{1,0:T(8,128)S(1)}, f32[8,128]{1,0:T(8,128)S(1)}, u32[]{:S(2)}, u32[]{:S(2)}) collective-permute-start(f32[8,128]{1,0:T(8,128)S(1)} %outer_round.4), channel_id=1, source_target_pairs={{0,1},{1,0},{2,3},{3,2},{4,5},{5,4},{6,7},{7,6},{8,9},{9,8},{10,11... | collective-permute-start | bytes 12296 | tf_op jit(solution)/shard_map/ppermute | solution.py:735
  38.5 2.2 %collective-permute-done.6 = f32[8,128]{1,0:T(8,128)S(1)} collective-permute-done((f32[8,128]{1,0:T(8,128)S(1)}, f32[8,128]{1,0:T(8,128)S(1)}, u32[]{:S(2)}, u32[]{:S(2)}) %collective-permute-start.6) | collective-permute-done | bytes 4128 | tf_op jit(solution)/shard_map/ppermute | solution.py:735
  40.7 2.4 %collective-permute-start.7 = (f32[8,128]{1,0:T(8,128)S(1)}, f32[8,128]{1,0:T(8,128)S(1)}, u32[]{:S(2)}, u32[]{:S(2)}) collective-permute-start(f32[8,128]{1,0:T(8,128)S(1)} %add.14.own_ref), channel_id=1, source_target_pairs={{2,4},{6,8},{10,12},{14,16},{18,20},{22,24},{26,28},{30,32},{34,36... | collective-permute-start | bytes 12296 | tf_op jit(solution)/shard_map/ppermute | solution.py:736
  43.1 3.2 %inner_round.5 = (f32[8,128]{1,0:T(8,128)S(1)}, f32[64,128]{1,0:T(8,128)S(1)}, f32[128,128]{1,0:T(8,128)S(1)}) custom-call(s32[8,128]{1,0:T(8,128)S(1)} %scalars.1.info, f32[8,128]{1,0:T(8,128)S(1)} %add.14.own_ref, f32[8,128]{1,0:T(8,128)S(1)} %collective-permute-done.8.mate_ref, bf16[2,64,128,128]{3,2,1,0:T(8,128)(2,1)S(1)} %get-tuple-element.22.s_ref), custom_call_target="tpu_custom_call" | custom-call | flops 8388608 | bytes 4194304 | tf_op jit(solution)/shard_map/inner_round/pallas_call | solution.py:394
  46.3 2.3 %collective-permute-done.7.side_ref = f32[8,128]{1,0:T(8,128)S(1)} collective-permute-done((f32[8,128]{1,0:T(8,128)S(1)}, f32[8,128]{1,0:T(8,128)S(1)}, u32[]{:S(2)}, u32[]{:S(2)}) %collective-permute-start.7) | collective-permute-done | bytes 4128 | tf_op jit(solution)/shard_map/ppermute | solution.py:736
  49.0 2.9 %collective-permute-start.9 = (f32[8,128]{1,0:T(8,128)S(1)}, f32[8,128]{1,0:T(8,128)S(1)}, u32[]{:S(2)}, u32[]{:S(2)}) collective-permute-start(f32[8,128]{1,0:T(8,128)S(1)} %outer_round.5), channel_id=1, source_target_pairs={{0,1},{1,0},{2,3},{3,2},{4,5},{5,4},{6,7},{7,6},{8,9},{9,8},{10,11... | collective-permute-start | bytes 12296 | tf_op jit(solution)/shard_map/ppermute | solution.py:735
  51.9 2.2 %collective-permute-done.9 = f32[8,128]{1,0:T(8,128)S(1)} collective-permute-done((f32[8,128]{1,0:T(8,128)S(1)}, f32[8,128]{1,0:T(8,128)S(1)}, u32[]{:S(2)}, u32[]{:S(2)}) %collective-permute-start.9) | collective-permute-done | bytes 4128 | tf_op jit(solution)/shard_map/ppermute | solution.py:735
  54.1 2.4 %collective-permute-start.11 = (f32[8,128]{1,0:T(8,128)S(1)}, f32[8,128]{1,0:T(8,128)S(1)}, u32[]{:S(2)}, u32[]{:S(2)}) collective-permute-start(f32[8,128]{1,0:T(8,128)S(1)} %add.15.after.own_ref), channel_id=1, source_target_pairs={{2,4},{6,8},{10,12},{14,16},{18,20},{22,24},{26,28},{30,32},{34,36... | collective-permute-start | bytes 12296 | tf_op jit(solution)/shard_map/ppermute | solution.py:736
  56.7 2.4 %flatten.1.d_ref = bf16[2,64,128,256]{3,2,1,0:T(8,128)(2,1)S(1)} custom-call(f32[8,128]{1,0:T(8,128)S(1)} %add.15.after.own_ref, bf16[2,64,256,128]{3,2,1,0:T(8,128)(2,1)S(1)} %get-tuple-element.32.x_ref), custom_call_target="tpu_custom_call" | custom-call | flops 8388608 | bytes 16777216 | tf_op jit(solution)/shard_map/flatten/pallas_call | solution.py:240
  59.1 3.1 %collective-permute-done.11.side_ref = f32[8,128]{1,0:T(8,128)S(1)} collective-permute-done((f32[8,128]{1,0:T(8,128)S(1)}, f32[8,128]{1,0:T(8,128)S(1)}, u32[]{:S(2)}, u32[]{:S(2)}) %collective-permute-start.11) | collective-permute-done | bytes 4128 | tf_op jit(solution)/shard_map/ppermute | solution.py:736
  62.2 1.8 %gram_to_send.1.after = f32[3,128,128]{2,1,0:T(8,128)S(1)} custom-call(s32[8,128]{1,0:T(8,128)S(1)} %scalars.1.info, f32[8,128]{1,0:T(8,128)S(1)} %add.15.after.own_ref, f32[8,128]{1,0:T(8,128)S(1)} %collective-permute-done.10.mate_ref, f32[8,128]{1,0:T(8,128)S(1)} %collective-permute-done.11.side_ref, bf16[2,64,128,256]{3,2,1,0:T(8,128)(2,1)S(1)} %flatten.1.d_ref), custom_call_target="tpu_custom_call" | custom-call | flops 1073741824 | bytes 4194304 | tf_op jit(solution)/shard_map/gram_to_send/pallas_call | solution.py:472
  64.0 3.0 %collective-permute-start.12 = (f32[3,128,128]{2,1,0:T(8,128)S(1)}, f32[3,128,128]{2,1,0:T(8,128)S(1)}, u32[]{:S(2)}, u32[]{:S(2)}) collective-permute-start(f32[3,128,128]{2,1,0:T(8,128)S(1)} %gram_to_send.1.after), channel_id=1, source_target_pairs={{0,1},{1,0},{2,3},{3,2},{4,5},{5,4},{6,7},{7,6},{8,9},{9,8},{10,11... | collective-permute-start | bytes 589832 | tf_op jit(solution)/shard_map/ppermute | solution.py:740
  67.0 1.9 %gram_to_keep.1 = (f32[3,128,128]{2,1,0:T(8,128)S(1)}, f32[3,2,128]{2,1,0:T(2,128)}) custom-call(s32[8,128]{1,0:T(8,128)S(1)} %scalars.1.info, f32[8,128]{1,0:T(8,128)S(1)} %add.15.after.own_ref, f32[8,128]{1,0:T(8,128)S(1)} %collective-permute-done.10.mate_ref, f32[8,128]{1,0:T(8,128)S(1)} %collective-permute-done.11.side_ref, ...), custom_call_target="tpu_custom_call" | custom-call | flops 1073741824 | bytes 4194304 | tf_op jit(solution)/shard_map/gram_to_keep/pallas_call | solution.py:472
  68.9 2.4 %collective-permute-done.12.got_ref = f32[3,128,128]{2,1,0:T(8,128)S(1)} collective-permute-done((f32[3,128,128]{2,1,0:T(8,128)S(1)}, f32[3,128,128]{2,1,0:T(8,128)S(1)}, u32[]{:S(2)}, u32[]{:S(2)}) %collective-permute-start.12) | collective-permute-done | bytes 196640 | tf_op jit(solution)/shard_map/ppermute | solution.py:740
  71.3 5.1 %root.1 = (f32[256,256]{1,0:T(8,128)S(1)}, f32[256,256]{1,0:T(8,128)S(1)}) custom-call(f32[3,128,128]{2,1,0:T(8,128)S(1)} %get-tuple-element.33.keep_ref, f32[3,128,128]{2,1,0:T(8,128)S(1)} %collective-permute-done.12.got_ref), custom_call_target="tpu_custom_call" | custom-call | flops 2214592512 | bytes 1048576 | tf_op jit(solution)/shard_map/root/pallas_call | solution.py:543
  76.6 1.5 %collective-permute-done.13.other_ref = f32[256,256]{1,0:T(8,128)S(1)} collective-permute-done((f32[256,256]{1,0:T(8,128)S(1)}, f32[256,256]{1,0:T(8,128)S(1)}, u32[]{:S(2)}, u32[]{:S(2)}) %collective-permute-start.13) | collective-permute-done | bytes 262176 | tf_op jit(solution)/shard_map/ppermute | solution.py:743
  78.1 5.3 %truncate.1.pack_ref.after = bf16[272,256]{1,0:T(8,128)(2,1)S(1)} custom-call(s32[8,128]{1,0:T(8,128)S(1)} %scalars.1.info, f32[4,4]{1,0:T(4,128)S(1)} %copy-done.3, f32[8,128]{1,0:T(8,128)S(1)} %add.15.after.own_ref, f32[8,128]{1,0:T(8,128)S(1)} %collective-permute-done.10.mate_ref, f32[256,256]{1,0:T(8,128)S(1)} %get-tuple-element.34.upper_ref, ...), custom_call_target="tpu_custom_call" | custom-call | flops 1342177280 | bytes 1572864 | tf_op jit(solution)/shard_map/truncate/pallas_call | solution.py:623
  83.4 3.0 %collective-permute-start.14 = (bf16[272,256]{1,0:T(8,128)(2,1)S(1)}, bf16[272,256]{1,0:T(8,128)(2,1)S(1)}, u32[]{:S(2)}, u32[]{:S(2)}) collective-permute-start(bf16[272,256]{1,0:T(8,128)(2,1)S(1)} %truncate.1.pack_ref.after), channel_id=1, source_target_pairs={{0,1},{1,0},{2,3},{3,2},{4,5},{5,4},{6,7},{7,6},{8,9},{9,8},{10,11... | collective-permute-start | bytes 417800 | tf_op jit(solution)/shard_map/ppermute | solution.py:745
  86.4 3.5 %update_own.1.begun_hbm = bf16[2,64,256,128]{3,2,1,0:T(8,128)(2,1)} custom-call(s32[8,128]{1,0:T(8,128)S(1)} %scalars.1.info, bf16[272,256]{1,0:T(8,128)(2,1)S(1)} %truncate.1.pack_ref.after, bf16[2,64,128,256]{3,2,1,0:T(8,128)(2,1)S(1)} %flatten.1.d_ref, bf16[272,256]{1,0:T(8,128)(2,1)S(1)} %truncate.1.pack_ref.after), custom_call_target="tpu_custom_call" | custom-call | flops 1073741824 | bytes 8388608 | tf_op jit(solution)/shard_map/update_own/pallas_call | solution.py:692
  89.9 0.8 collective-permute-done.14.got_ref
  90.7 3.5 %update_other.1 = (bf16[2,64,256,128]{3,2,1,0:T(8,128)(2,1)}, f32[2,128]{1,0:T(2,128)}) custom-call(s32[8,128]{1,0:T(8,128)S(1)} %scalars.1.info, bf16[272,256]{1,0:T(8,128)(2,1)S(1)} %truncate.1.pack_ref.after, bf16[272,256]{1,0:T(8,128)(2,1)S(1)} %collective-permute-done.14.got_ref, ...), custom_call_target="tpu_custom_call", output_to_operand_aliasing={{0}: (4, {})} | custom-call | flops 1073741824 | bytes 8388608 | tf_op jit(solution)/shard_map/update_other/pallas_call | solution.py:692
  (25 shorter events, 1.6 us)
Async XLA Ops:
  0.6 17.2 %copy-start.1 = (s32[128]{0:T(128)S(1)}, s32[128]{0:T(128)}, u32[]{:S(2)}) copy-start(s32[128]{0:T(128)} %ranks.1) | copy-start | bytes 1540
  0.6 17.2 %copy-start = (s32[128,3]{0,1:T(4,128)S(1)}, s32[128,3]{0,1:T(4,128)}, u32[]{:S(2)}) copy-start(s32[128,3]{0,1:T(4,128)} %param.6) | copy-start | bytes 4612
  5.3 5.2 %collective-permute-start = (f32[8,128]{1,0:T(8,128)S(1)}, f32[8,128]{1,0:T(8,128)S(1)}, u32[]{:S(2)}, u32[]{:S(2)}) collective-permute-start(f32[8,128]{1,0:T(8,128)S(1)} %get-tuple-element.21.after), channel_id=1, source_target_pairs={{0,1},{1,0},{2,3},{3,2},{4,5},{5,4},{6,7},{7,6},{8,9},{9,8},{10,11... | collective-permute-start | bytes 12296 | tf_op jit(solution)/shard_map/ppermute | solution.py:735
  10.5 8.0 %collective-permute-start.2 = (f32[8,128]{1,0:T(8,128)S(1)}, f32[8,128]{1,0:T(8,128)S(1)}, u32[]{:S(2)}, u32[]{:S(2)}) collective-permute-start(f32[8,128]{1,0:T(8,128)S(1)} %add.12.own_ref), channel_id=1, source_target_pairs={{0,2},{2,0},{4,6},{6,4},{8,10},{10,8},{12,14},{14,12},{16,18},{18,... | collective-permute-start | bytes 12296 | tf_op jit(solution)/shard_map/ppermute | solution.py:737
  10.5 11.2 %collective-permute-start.1 = (f32[8,128]{1,0:T(8,128)S(1)}, f32[8,128]{1,0:T(8,128)S(1)}, u32[]{:S(2)}, u32[]{:S(2)}) collective-permute-start(f32[8,128]{1,0:T(8,128)S(1)} %add.12.own_ref), channel_id=1, source_target_pairs={{2,4},{6,8},{10,12},{14,16},{18,20},{22,24},{26,28},{30,32},{34,36... | collective-permute-start | bytes 12296 | tf_op jit(solution)/shard_map/ppermute | solution.py:736
  22.1 5.1 %collective-permute-start.3 = (f32[8,128]{1,0:T(8,128)S(1)}, f32[8,128]{1,0:T(8,128)S(1)}, u32[]{:S(2)}, u32[]{:S(2)}) collective-permute-start(f32[8,128]{1,0:T(8,128)S(1)} %outer_round.3), channel_id=1, source_target_pairs={{0,1},{1,0},{2,3},{3,2},{4,5},{5,4},{6,7},{7,6},{8,9},{9,8},{10,11... | collective-permute-start | bytes 12296 | tf_op jit(solution)/shard_map/ppermute | solution.py:735
  27.2 3.0 %collective-permute-start.5 = (f32[8,128]{1,0:T(8,128)S(1)}, f32[8,128]{1,0:T(8,128)S(1)}, u32[]{:S(2)}, u32[]{:S(2)}) collective-permute-start(f32[8,128]{1,0:T(8,128)S(1)} %add.13.own_ref), channel_id=1, source_target_pairs={{0,2},{2,0},{4,6},{6,4},{8,10},{10,8},{12,14},{14,12},{16,18},{18,... | collective-permute-start | bytes 12296 | tf_op jit(solution)/shard_map/ppermute | solution.py:737
  27.2 7.9 %collective-permute-start.4 = (f32[8,128]{1,0:T(8,128)S(1)}, f32[8,128]{1,0:T(8,128)S(1)}, u32[]{:S(2)}, u32[]{:S(2)}) collective-permute-start(f32[8,128]{1,0:T(8,128)S(1)} %add.13.own_ref), channel_id=1, source_target_pairs={{2,4},{6,8},{10,12},{14,16},{18,20},{22,24},{26,28},{30,32},{34,36... | collective-permute-start | bytes 12296 | tf_op jit(solution)/shard_map/ppermute | solution.py:736
  35.5 5.1 %collective-permute-start.6 = (f32[8,128]{1,0:T(8,128)S(1)}, f32[8,128]{1,0:T(8,128)S(1)}, u32[]{:S(2)}, u32[]{:S(2)}) collective-permute-start(f32[8,128]{1,0:T(8,128)S(1)} %outer_round.4), channel_id=1, source_target_pairs={{0,1},{1,0},{2,3},{3,2},{4,5},{5,4},{6,7},{7,6},{8,9},{9,8},{10,11... | collective-permute-start | bytes 12296 | tf_op jit(solution)/shard_map/ppermute | solution.py:735
  40.7 2.5 %collective-permute-start.8 = (f32[8,128]{1,0:T(8,128)S(1)}, f32[8,128]{1,0:T(8,128)S(1)}, u32[]{:S(2)}, u32[]{:S(2)}) collective-permute-start(f32[8,128]{1,0:T(8,128)S(1)} %add.14.own_ref), channel_id=1, source_target_pairs={{0,2},{2,0},{4,6},{6,4},{8,10},{10,8},{12,14},{14,12},{16,18},{18,... | collective-permute-start | bytes 12296 | tf_op jit(solution)/shard_map/ppermute | solution.py:737
  40.7 7.9 %collective-permute-start.7 = (f32[8,128]{1,0:T(8,128)S(1)}, f32[8,128]{1,0:T(8,128)S(1)}, u32[]{:S(2)}, u32[]{:S(2)}) collective-permute-start(f32[8,128]{1,0:T(8,128)S(1)} %add.14.own_ref), channel_id=1, source_target_pairs={{2,4},{6,8},{10,12},{14,16},{18,20},{22,24},{26,28},{30,32},{34,36... | collective-permute-start | bytes 12296 | tf_op jit(solution)/shard_map/ppermute | solution.py:736
  49.0 5.1 %collective-permute-start.9 = (f32[8,128]{1,0:T(8,128)S(1)}, f32[8,128]{1,0:T(8,128)S(1)}, u32[]{:S(2)}, u32[]{:S(2)}) collective-permute-start(f32[8,128]{1,0:T(8,128)S(1)} %outer_round.5), channel_id=1, source_target_pairs={{0,1},{1,0},{2,3},{3,2},{4,5},{5,4},{6,7},{7,6},{8,9},{9,8},{10,11... | collective-permute-start | bytes 12296 | tf_op jit(solution)/shard_map/ppermute | solution.py:735
  54.1 8.0 %collective-permute-start.11 = (f32[8,128]{1,0:T(8,128)S(1)}, f32[8,128]{1,0:T(8,128)S(1)}, u32[]{:S(2)}, u32[]{:S(2)}) collective-permute-start(f32[8,128]{1,0:T(8,128)S(1)} %add.15.after.own_ref), channel_id=1, source_target_pairs={{2,4},{6,8},{10,12},{14,16},{18,20},{22,24},{26,28},{30,32},{34,36... | collective-permute-start | bytes 12296 | tf_op jit(solution)/shard_map/ppermute | solution.py:736
  56.6 5.6 %collective-permute-start.10 = (f32[8,128]{1,0:T(8,128)S(1)}, f32[8,128]{1,0:T(8,128)S(1)}, u32[]{:S(2)}, u32[]{:S(2)}) collective-permute-start(f32[8,128]{1,0:T(8,128)S(1)} %add.15.after.own_ref), channel_id=1, source_target_pairs={{0,2},{2,0},{4,6},{6,4},{8,10},{10,8},{12,14},{14,12},{16,18},{18,... | collective-permute-start | bytes 12296 | tf_op jit(solution)/shard_map/ppermute | solution.py:737
  64.0 14.1 %copy-start.2 = (f32[512,128]{1,0:T(8,128)S(1)}, f32[512,128]{1,0:T(8,128)}, u32[]{:S(2)}) copy-start(f32[512,128]{1,0:T(8,128)} %probes_ref.1) | copy-start | bytes 786436
  64.0 14.1 %copy-start.3 = (f32[4,4]{1,0:T(4,128)S(1)}, f32[4,4]{1,0:T(4,128)}, u32[]{:S(2)}) copy-start(f32[4,4]{1,0:T(4,128)} %gate.1) | copy-start | bytes 196
  64.0 7.3 %collective-permute-start.12 = (f32[3,128,128]{2,1,0:T(8,128)S(1)}, f32[3,128,128]{2,1,0:T(8,128)S(1)}, u32[]{:S(2)}, u32[]{:S(2)}) collective-permute-start(f32[3,128,128]{2,1,0:T(8,128)S(1)} %gram_to_send.1.after), channel_id=1, source_target_pairs={{0,1},{1,0},{2,3},{3,2},{4,5},{5,4},{6,7},{7,6},{8,9},{9,8},{10,11... | collective-permute-start | bytes 589832 | tf_op jit(solution)/shard_map/ppermute | solution.py:740
  76.3 1.8 %collective-permute-start.13 = (f32[256,256]{1,0:T(8,128)S(1)}, f32[256,256]{1,0:T(8,128)S(1)}, u32[]{:S(2)}, u32[]{:S(2)}) collective-permute-start(f32[256,256]{1,0:T(8,128)S(1)} %get-tuple-element.34.upper_ref), channel_id=1, source_target_pairs={{0,2},{2,0},{4,6},{6,4},{8,10},{10,8},{12,14},{14,12},{16,18},{18,... | collective-permute-start | bytes 786440 | tf_op jit(solution)/shard_map/ppermute | solution.py:743
  83.4 7.3 %collective-permute-start.14 = (bf16[272,256]{1,0:T(8,128)(2,1)S(1)}, bf16[272,256]{1,0:T(8,128)(2,1)S(1)}, u32[]{:S(2)}, u32[]{:S(2)}) collective-permute-start(bf16[272,256]{1,0:T(8,128)(2,1)S(1)} %truncate.1.pack_ref.after), channel_id=1, source_target_pairs={{0,1},{1,0},{2,3},{3,2},{4,5},{5,4},{6,7},{7,6},{8,9},{9,8},{10,11... | collective-permute-start | bytes 417800 | tf_op jit(solution)/shard_map/ppermute | solution.py:745

commit v4 on v3

--- a/solution.py
+++ b/solution.py
@@ -158,6 +158,22 @@
     )(after, near, ranks)
 
 
+def add_kernel(one_ref, two_ref, after, out_ref):
+    out_ref[...] = one_ref[...] + two_ref[...]
+
+
+def add_call(one, two, after):
+    return pl.pallas_call(
+        add_kernel,
+        in_specs=[vmem(), vmem(), anywhere()],
+        out_specs=vmem(),
+        out_shape=jax.ShapeDtypeStruct(one.shape, F32),
+        compiler_params=params(4),
+        cost_estimate=cost(one.size, 12 * one.size),
+        name="add",
+    )(one, two, after)
+
+
 def open_kernel(x_hbm, x_ref, s_ref, out_ref, scratch, sums_ref, total_ref, sems):
     members, rows, wide, bond = x_hbm.shape
     steps = sems.shape[0]
@@ -421,10 +437,10 @@
 
 def add_gram(info, member, weights, d_ref, out_ref, first_ref, gram):
     rows, bond = d_ref.shape[1:3]
-    block = 32
+    block = 64
     start = info[0, ROW] * rows
-    first_ref[...] = jnp.sqrt(down(weights[0]))
-    second = jnp.sqrt(down(weights[1]))
+    first_ref[...] = down(jnp.sqrt(weights[0]))
+    second = down(jnp.sqrt(weights[1]))
     gram[...] = jnp.zeros(gram.shape, F32)
 
     def body(step, carry):
@@ -504,7 +520,7 @@
     return down_index == across_index
 
 
-def root_pair(matrix):
+def root_sweeps(matrix):
     size = matrix.shape[0]
     diagonal = eye_mask(size)
     lift = jnp.where(diagonal, 1.5, 0.0).astype(F32)
@@ -514,13 +530,21 @@
     poly_parts = halves(poly)
     current = dot3(halves(current), poly_parts)
     partner = poly
+    yield None
     for _ in range(SWEEPS - 1):
         current_parts, partner_parts = (halves(current), halves(partner))
         poly_parts = halves(lift - 0.5 * dot3(partner_parts, current_parts))
         current = dot3(current_parts, poly_parts)
         partner = dot3(poly_parts, partner_parts)
+        yield None
     root_scale = jnp.sqrt(scale)
-    return (current * root_scale, partner / root_scale)
+    yield (current * root_scale, partner / root_scale)
+
+
+def root_pair(matrix):
+    for result in root_sweeps(matrix):
+        pass
+    return result
 
 
 def root_kernel(keep_ref, got_ref, upper_ref, inverse_ref):
@@ -599,18 +623,29 @@
     sampled_parts = halves(jnp.concatenate([sampled[:, :bond], sampled[:, bond:]], axis=0))
     inner = dot3(sampled_parts, sampled_parts, ((0,), (0,)))
     inner = inner + jnp.where(eye_mask(bond), 1.0 - mask, 0.0)
-    _, inner_inverse = root_pair(inner)
-    basis = dot3(sampled_parts, halves(inner_inverse))
-    basis = jnp.concatenate([basis[:wide], basis[wide:]], axis=1)
-    based = combined(
-        dot3(left_parts, halves(basis)),
-        lambda t, t_out, s, s_out: gate[2 * s_out + t_out, 2 * s + t],
-    )
+    sweeps = root_sweeps(inner)
+    next(sweeps)
+    based = dot3(left_parts, halves(sampled))
+    next(sweeps)
+    based = combined(based, lambda t, t_out, s, s_out: gate[2 * s_out + t_out, 2 * s + t])
+    next(sweeps)
+    next(sweeps)
     coeffs = dot3(right_parts, halves(based))
-    squares = jnp.sum(coeffs * coeffs, axis=0, keepdims=True)
-    new_bond = jnp.sqrt((squares[:, :bond] + squares[:, bond:]) / (2 * wide) + 1e-06)
-    target = jnp.where(odd, coeffs / jnp.concatenate([new_bond, new_bond], axis=1), basis)
-    change = dot3(halves(inverse_ref[...]), halves(target))
+    next(sweeps)
+    next(sweeps)
+    target = dot3(halves(inverse_ref[...]), halves(jnp.where(odd, coeffs, sampled)))
+    for result in sweeps:
+        pass
+    inner_inverse = result[1]
+    inner_parts = halves(inner_inverse)
+
+    def rooted(value):
+        return [dot3(halves(value[:, :bond]), inner_parts), dot3(halves(value[:, bond:]), inner_parts)]
+
+    squares = sum(jnp.sum(part * part, axis=0, keepdims=True) for part in rooted(coeffs))
+    new_bond = jnp.sqrt(squares / (2 * wide) + 1e-06)
+    divisor = jnp.where(odd, new_bond, 1.0)
+    change = jnp.concatenate([part / divisor for part in rooted(target)], axis=1)
     gated = info[0, GATED] == 1
     identity = eye_mask(wide).astype(F32)
     out_ref[:wide] = jnp.where(gated, change, identity).astype(BF16)
@@ -649,11 +684,13 @@
         def free():
             put(step).wait()
 
-        rows_in = d_ref[member, pl.ds(start, block)].reshape(block * bond, wide)
-        result = dot_of(rows_in, pack_ref[:wide])
+        change = pack_ref[:wide]
         for index in range(block):
+            if index % 4 == 0:
+                rows_in = d_ref[member, pl.ds(start + index, 4)].reshape(4 * bond, wide)
+                result = dot_of(rows_in, change)
             lane = scratch.at[index % scratch.shape[0]]
-            piece = result[index * bond : (index + 1) * bond]
+            piece = result[index % 4 * bond : (index % 4 + 1) * bond]
             lane[pl.ds(0, bond, 2), :] = piece[:, :bond]
             lane[pl.ds(1, bond, 2), :] = piece[:, bond:]
             held[slot, index] = lane[...].astype(BF16)
@@ -732,7 +769,8 @@
         if index > 0:
             begun = inner_call(info, own, mate, squares)
             part = outer_call(info, side, *begun)
-        own = part + lax.ppermute(part, "row", row_swap)
+        got = lax.ppermute(part, "row", row_swap)
+        own = part + got if index > 0 else add_call(part, got, info)
         side = lax.ppermute(own, "site", side_swap)
         mate = lax.ppermute(own, "site", core_swap)
     flat = flatten_call(own, x)

time: 94.6 us -> 92.8 us (0.981)
  Pallas kernels: 39.5 us -> 38.2 us
  waiting for transfers between devices: 20.3 us -> 19.1 us
where the time goes in v4:
time: 92.8 us; the launch traced here: 92.6 us
  Pallas kernels  38.2 us (41%)
  starting transfers between devices  34.4 us (37%)
  waiting for transfers between devices  19.1 us (21%)
  between operations  0.97 us (1%)
    ppermute x4, starting transfers between devices, shards(): side = lax.ppermute(own, 'site', side_swap)  16 us
    ppermute x4, starting transfers between devices, shards(): got = lax.ppermute(part, 'row', row_swap)  12 us
    pallas_call x3, Pallas kernels, inner_call(): pl.pallas_call(inner_kernel, in_specs=[vmem(), vmem(), vmem(), vmem()], o...  9.62 us
    ppermute x4, waiting for transfers between devices, shards(): got = lax.ppermute(part, 'row', row_swap)  7.93 us
    pallas_call x2, Pallas kernels, update_call(): pl.pallas_call(kernel, in_specs=in_specs, out_specs=[hbm(), hbm()] if wit...  6.71 us
    ppermute x4, waiting for transfers between devices, shards(): side = lax.ppermute(own, 'site', side_swap)  6.19 us
    pallas_call x1, Pallas kernels, root_call(): pl.pallas_call(root_kernel, in_specs=[vmem(), vmem()], out_specs=[vmem(),...  5.05 us
    pallas_call x1, Pallas kernels, open_call(): pl.pallas_call(open_kernel, in_specs=[hbm()], out_specs=[vmem(), vmem(),...  4.65 us
  transfers between devices with their start and end apart: 15, of which 10 were waited for; matrix products, arithmetic and copies ran while one was open for 0% of the time, Pallas kernels for 19%

profile of v4, /device:TPU:6, one launch (start us, length us, event | category | flops | bytes accessed | tf_op | source)
XLA Modules:
  0.0 92.6 jit_solution(2786947586235243694)
XLA Ops:
  0.7 4.6 %open.1 = (bf16[2,64,256,128]{3,2,1,0:T(8,128)(2,1)S(1)}, bf16[2,64,128,128]{3,2,1,0:T(8,128)(2,1)S(1)}, f32[8,128]{1,0:T(8,128)S(1)}) custom-call(bf16[2,64,256,128]{3,2,1,0:T(8,128)(2,1)} %bitcast.6), custom_call_target="tpu_custom_call" | custom-call | flops 16777216 | bytes 20971520 | tf_op jit(solution)/shard_map/open/pallas_call | solution.py:219
  5.3 3.3 %collective-permute-start = (f32[8,128]{1,0:T(8,128)S(1)}, f32[8,128]{1,0:T(8,128)S(1)}, u32[]{:S(2)}, u32[]{:S(2)}) collective-permute-start(f32[8,128]{1,0:T(8,128)S(1)} %get-tuple-element.21.after.one_ref), channel_id=1, source_target_pairs={{0,1},{1,0},{2,3},{3,2},{4,5},{5,4},{6,7},{7,6},{8,9},{9,8},{10,11... | collective-permute-start | bytes 12296 | tf_op jit(solution)/shard_map/ppermute | solution.py:772
  8.6 0.6 scalars.1.after.info
  9.2 1.3 %collective-permute-done.two_ref = f32[8,128]{1,0:T(8,128)S(1)} collective-permute-done((f32[8,128]{1,0:T(8,128)S(1)}, f32[8,128]{1,0:T(8,128)S(1)}, u32[]{:S(2)}, u32[]{:S(2)}) %collective-permute-start) | collective-permute-done | bytes 4128 | tf_op jit(solution)/shard_map/ppermute | solution.py:772
  10.5 7.3 %collective-permute-start.1 = (f32[8,128]{1,0:T(8,128)S(1)}, f32[8,128]{1,0:T(8,128)S(1)}, u32[]{:S(2)}, u32[]{:S(2)}) collective-permute-start(f32[8,128]{1,0:T(8,128)S(1)} %add.13.own_ref), channel_id=1, source_target_pairs={{2,4},{6,8},{10,12},{14,16},{18,20},{22,24},{26,28},{30,32},{34,36... | collective-permute-start | bytes 12296 | tf_op jit(solution)/shard_map/ppermute | solution.py:774
  17.8 3.2 %inner_round.3 = (f32[8,128]{1,0:T(8,128)S(1)}, f32[64,128]{1,0:T(8,128)S(1)}, f32[128,128]{1,0:T(8,128)S(1)}) custom-call(s32[8,128]{1,0:T(8,128)S(1)} %scalars.1.after.info, f32[8,128]{1,0:T(8,128)S(1)} %add.13.own_ref, f32[8,128]{1,0:T(8,128)S(1)} %collective-permute-done.2.mate_ref, bf16[2,64,128,128]{3,2,1,0:T(8,128)(2,1)S(1)} %get-tuple-element.22.s_ref), custom_call_target="tpu_custom_call" | custom-call | flops 8388608 | bytes 4194304 | tf_op jit(solution)/shard_map/inner_round/pallas_call | solution.py:410
  21.5 2.9 %collective-permute-start.3 = (f32[8,128]{1,0:T(8,128)S(1)}, f32[8,128]{1,0:T(8,128)S(1)}, u32[]{:S(2)}, u32[]{:S(2)}) collective-permute-start(f32[8,128]{1,0:T(8,128)S(1)} %outer_round.3), channel_id=1, source_target_pairs={{0,1},{1,0},{2,3},{3,2},{4,5},{5,4},{6,7},{7,6},{8,9},{9,8},{10,11... | collective-permute-start | bytes 12296 | tf_op jit(solution)/shard_map/ppermute | solution.py:772
  24.4 2.2 %collective-permute-done.3 = f32[8,128]{1,0:T(8,128)S(1)} collective-permute-done((f32[8,128]{1,0:T(8,128)S(1)}, f32[8,128]{1,0:T(8,128)S(1)}, u32[]{:S(2)}, u32[]{:S(2)}) %collective-permute-start.3) | collective-permute-done | bytes 4128 | tf_op jit(solution)/shard_map/ppermute | solution.py:772
  26.6 3.7 %collective-permute-start.4 = (f32[8,128]{1,0:T(8,128)S(1)}, f32[8,128]{1,0:T(8,128)S(1)}, u32[]{:S(2)}, u32[]{:S(2)}) collective-permute-start(f32[8,128]{1,0:T(8,128)S(1)} %add.10.own_ref), channel_id=1, source_target_pairs={{2,4},{6,8},{10,12},{14,16},{18,20},{22,24},{26,28},{30,32},{34,36... | collective-permute-start | bytes 12296 | tf_op jit(solution)/shard_map/ppermute | solution.py:774
  30.3 3.2 %inner_round.4 = (f32[8,128]{1,0:T(8,128)S(1)}, f32[64,128]{1,0:T(8,128)S(1)}, f32[128,128]{1,0:T(8,128)S(1)}) custom-call(s32[8,128]{1,0:T(8,128)S(1)} %scalars.1.after.info, f32[8,128]{1,0:T(8,128)S(1)} %add.10.own_ref, f32[8,128]{1,0:T(8,128)S(1)} %collective-permute-done.5.mate_ref, bf16[2,64,128,128]{3,2,1,0:T(8,128)(2,1)S(1)} %get-tuple-element.22.s_ref), custom_call_target="tpu_custom_call" | custom-call | flops 8388608 | bytes 4194304 | tf_op jit(solution)/shard_map/inner_round/pallas_call | solution.py:410
  33.5 1.0 %collective-permute-done.4.side_ref = f32[8,128]{1,0:T(8,128)S(1)} collective-permute-done((f32[8,128]{1,0:T(8,128)S(1)}, f32[8,128]{1,0:T(8,128)S(1)}, u32[]{:S(2)}, u32[]{:S(2)}) %collective-permute-start.4) | collective-permute-done | bytes 4128 | tf_op jit(solution)/shard_map/ppermute | solution.py:774
  34.9 2.9 %collective-permute-start.6 = (f32[8,128]{1,0:T(8,128)S(1)}, f32[8,128]{1,0:T(8,128)S(1)}, u32[]{:S(2)}, u32[]{:S(2)}) collective-permute-start(f32[8,128]{1,0:T(8,128)S(1)} %outer_round.4), channel_id=1, source_target_pairs={{0,1},{1,0},{2,3},{3,2},{4,5},{5,4},{6,7},{7,6},{8,9},{9,8},{10,11... | collective-permute-start | bytes 12296 | tf_op jit(solution)/shard_map/ppermute | solution.py:772
  37.8 2.2 %collective-permute-done.6 = f32[8,128]{1,0:T(8,128)S(1)} collective-permute-done((f32[8,128]{1,0:T(8,128)S(1)}, f32[8,128]{1,0:T(8,128)S(1)}, u32[]{:S(2)}, u32[]{:S(2)}) %collective-permute-start.6) | collective-permute-done | bytes 4128 | tf_op jit(solution)/shard_map/ppermute | solution.py:772
  40.0 2.6 %collective-permute-start.7 = (f32[8,128]{1,0:T(8,128)S(1)}, f32[8,128]{1,0:T(8,128)S(1)}, u32[]{:S(2)}, u32[]{:S(2)}) collective-permute-start(f32[8,128]{1,0:T(8,128)S(1)} %add.11.own_ref), channel_id=1, source_target_pairs={{2,4},{6,8},{10,12},{14,16},{18,20},{22,24},{26,28},{30,32},{34,36... | collective-permute-start | bytes 12296 | tf_op jit(solution)/shard_map/ppermute | solution.py:774
  42.7 3.2 %inner_round.5 = (f32[8,128]{1,0:T(8,128)S(1)}, f32[64,128]{1,0:T(8,128)S(1)}, f32[128,128]{1,0:T(8,128)S(1)}) custom-call(s32[8,128]{1,0:T(8,128)S(1)} %scalars.1.after.info, f32[8,128]{1,0:T(8,128)S(1)} %add.11.own_ref, f32[8,128]{1,0:T(8,128)S(1)} %collective-permute-done.8.mate_ref, bf16[2,64,128,128]{3,2,1,0:T(8,128)(2,1)S(1)} %get-tuple-element.22.s_ref), custom_call_target="tpu_custom_call" | custom-call | flops 8388608 | bytes 4194304 | tf_op jit(solution)/shard_map/inner_round/pallas_call | solution.py:410
  45.9 2.1 %collective-permute-done.7.side_ref = f32[8,128]{1,0:T(8,128)S(1)} collective-permute-done((f32[8,128]{1,0:T(8,128)S(1)}, f32[8,128]{1,0:T(8,128)S(1)}, u32[]{:S(2)}, u32[]{:S(2)}) %collective-permute-start.7) | collective-permute-done | bytes 4128 | tf_op jit(solution)/shard_map/ppermute | solution.py:774
  48.4 2.9 %collective-permute-start.9 = (f32[8,128]{1,0:T(8,128)S(1)}, f32[8,128]{1,0:T(8,128)S(1)}, u32[]{:S(2)}, u32[]{:S(2)}) collective-permute-start(f32[8,128]{1,0:T(8,128)S(1)} %outer_round.5), channel_id=1, source_target_pairs={{0,1},{1,0},{2,3},{3,2},{4,5},{5,4},{6,7},{7,6},{8,9},{9,8},{10,11... | collective-permute-start | bytes 12296 | tf_op jit(solution)/shard_map/ppermute | solution.py:772
  51.3 2.2 %collective-permute-done.9 = f32[8,128]{1,0:T(8,128)S(1)} collective-permute-done((f32[8,128]{1,0:T(8,128)S(1)}, f32[8,128]{1,0:T(8,128)S(1)}, u32[]{:S(2)}, u32[]{:S(2)}) %collective-permute-start.9) | collective-permute-done | bytes 4128 | tf_op jit(solution)/shard_map/ppermute | solution.py:772
  53.5 2.4 %collective-permute-start.11 = (f32[8,128]{1,0:T(8,128)S(1)}, f32[8,128]{1,0:T(8,128)S(1)}, u32[]{:S(2)}, u32[]{:S(2)}) collective-permute-start(f32[8,128]{1,0:T(8,128)S(1)} %add.12.after.own_ref), channel_id=1, source_target_pairs={{2,4},{6,8},{10,12},{14,16},{18,20},{22,24},{26,28},{30,32},{34,36... | collective-permute-start | bytes 12296 | tf_op jit(solution)/shard_map/ppermute | solution.py:774
  56.0 2.4 %flatten.1.d_ref = bf16[2,64,128,256]{3,2,1,0:T(8,128)(2,1)S(1)} custom-call(f32[8,128]{1,0:T(8,128)S(1)} %add.12.after.own_ref, bf16[2,64,256,128]{3,2,1,0:T(8,128)(2,1)S(1)} %get-tuple-element.32.x_ref), custom_call_target="tpu_custom_call" | custom-call | flops 8388608 | bytes 16777216 | tf_op jit(solution)/shard_map/flatten/pallas_call | solution.py:256
  58.5 3.1 %collective-permute-done.11.side_ref = f32[8,128]{1,0:T(8,128)S(1)} collective-permute-done((f32[8,128]{1,0:T(8,128)S(1)}, f32[8,128]{1,0:T(8,128)S(1)}, u32[]{:S(2)}, u32[]{:S(2)}) %collective-permute-start.11) | collective-permute-done | bytes 4128 | tf_op jit(solution)/shard_map/ppermute | solution.py:774
  61.5 1.8 %gram_to_send.1.after = f32[3,128,128]{2,1,0:T(8,128)S(1)} custom-call(s32[8,128]{1,0:T(8,128)S(1)} %scalars.1.after.info, f32[8,128]{1,0:T(8,128)S(1)} %add.12.after.own_ref, f32[8,128]{1,0:T(8,128)S(1)} %collective-permute-done.10.mate_ref, f32[8,128]{1,0:T(8,128)S(1)} %collective-permute-done.11.side_ref, bf16[2,64,128,256]{3,2,1,0:T(8,128)(2,1)S(1)} %flatten.1.d_ref), custom_call_target="tpu_custom_call" | custom-call | flops 1073741824 | bytes 4194304 | tf_op jit(solution)/shard_map/gram_to_send/pallas_call | solution.py:488
  63.3 3.2 %collective-permute-start.12 = (f32[3,128,128]{2,1,0:T(8,128)S(1)}, f32[3,128,128]{2,1,0:T(8,128)S(1)}, u32[]{:S(2)}, u32[]{:S(2)}) collective-permute-start(f32[3,128,128]{2,1,0:T(8,128)S(1)} %gram_to_send.1.after), channel_id=1, source_target_pairs={{0,1},{1,0},{2,3},{3,2},{4,5},{5,4},{6,7},{7,6},{8,9},{9,8},{10,11... | collective-permute-start | bytes 589832 | tf_op jit(solution)/shard_map/ppermute | solution.py:778
  66.5 1.8 %gram_to_keep.1 = (f32[3,128,128]{2,1,0:T(8,128)S(1)}, f32[3,2,128]{2,1,0:T(2,128)}) custom-call(s32[8,128]{1,0:T(8,128)S(1)} %scalars.1.after.info, f32[8,128]{1,0:T(8,128)S(1)} %add.12.after.own_ref, f32[8,128]{1,0:T(8,128)S(1)} %collective-permute-done.10.mate_ref, f32[8,128]{1,0:T(8,128)S(1)} %collective-permute-done.11.side_ref, ...), custom_call_target="tpu_custom_call" | custom-call | flops 1073741824 | bytes 4194304 | tf_op jit(solution)/shard_map/gram_to_keep/pallas_call | solution.py:488
  68.3 2.5 %collective-permute-done.12.got_ref = f32[3,128,128]{2,1,0:T(8,128)S(1)} collective-permute-done((f32[3,128,128]{2,1,0:T(8,128)S(1)}, f32[3,128,128]{2,1,0:T(8,128)S(1)}, u32[]{:S(2)}, u32[]{:S(2)}) %collective-permute-start.12) | collective-permute-done | bytes 196640 | tf_op jit(solution)/shard_map/ppermute | solution.py:778
  70.8 5.1 %root.1 = (f32[256,256]{1,0:T(8,128)S(1)}, f32[256,256]{1,0:T(8,128)S(1)}) custom-call(f32[3,128,128]{2,1,0:T(8,128)S(1)} %get-tuple-element.33.keep_ref, f32[3,128,128]{2,1,0:T(8,128)S(1)} %collective-permute-done.12.got_ref), custom_call_target="tpu_custom_call" | custom-call | flops 2214592512 | bytes 1048576 | tf_op jit(solution)/shard_map/root/pallas_call | solution.py:567
  75.9 1.5 %collective-permute-done.13.other_ref = f32[256,256]{1,0:T(8,128)S(1)} collective-permute-done((f32[256,256]{1,0:T(8,128)S(1)}, f32[256,256]{1,0:T(8,128)S(1)}, u32[]{:S(2)}, u32[]{:S(2)}) %collective-permute-start.13) | collective-permute-done | bytes 262176 | tf_op jit(solution)/shard_map/ppermute | solution.py:781
  77.4 4.3 %truncate.1.pack_ref.after = bf16[272,256]{1,0:T(8,128)(2,1)S(1)} custom-call(s32[8,128]{1,0:T(8,128)S(1)} %scalars.1.after.info, f32[4,4]{1,0:T(4,128)S(1)} %copy-done.3, f32[8,128]{1,0:T(8,128)S(1)} %add.12.after.own_ref, f32[8,128]{1,0:T(8,128)S(1)} %collective-permute-done.10.mate_ref, f32[256,256]{1,0:T(8,128)S(1)} %get-tuple-element.34.upper_ref, ...), custom_call_target="tpu_custom_call" | custom-call | flops 1342177280 | bytes 1572864 | tf_op jit(solution)/shard_map/truncate/pallas_call | solution.py:658
  81.8 3.0 %collective-permute-start.14 = (bf16[272,256]{1,0:T(8,128)(2,1)S(1)}, bf16[272,256]{1,0:T(8,128)(2,1)S(1)}, u32[]{:S(2)}, u32[]{:S(2)}) collective-permute-start(bf16[272,256]{1,0:T(8,128)(2,1)S(1)} %truncate.1.pack_ref.after), channel_id=1, source_target_pairs={{0,1},{1,0},{2,3},{3,2},{4,5},{5,4},{6,7},{7,6},{8,9},{9,8},{10,11... | collective-permute-start | bytes 417800 | tf_op jit(solution)/shard_map/ppermute | solution.py:783
  84.8 3.3 %update_own.1.begun_hbm = bf16[2,64,256,128]{3,2,1,0:T(8,128)(2,1)} custom-call(s32[8,128]{1,0:T(8,128)S(1)} %scalars.1.after.info, bf16[272,256]{1,0:T(8,128)(2,1)S(1)} %truncate.1.pack_ref.after, bf16[2,64,128,256]{3,2,1,0:T(8,128)(2,1)S(1)} %flatten.1.d_ref, bf16[272,256]{1,0:T(8,128)(2,1)S(1)} %truncate.1.pack_ref.after), custom_call_target="tpu_custom_call" | custom-call | flops 1073741824 | bytes 8388608 | tf_op jit(solution)/shard_map/update_own/pallas_call | solution.py:729
  88.1 1.0 %collective-permute-done.14.got_ref = bf16[272,256]{1,0:T(8,128)(2,1)S(1)} collective-permute-done((bf16[272,256]{1,0:T(8,128)(2,1)S(1)}, bf16[272,256]{1,0:T(8,128)(2,1)S(1)}, u32[]{:S(2)}, u32[]{:S(2)}) %collective-permute-start.14) | collective-permute-done | bytes 139296 | tf_op jit(solution)/shard_map/ppermute | solution.py:783
  89.1 3.4 %update_other.1 = (bf16[2,64,256,128]{3,2,1,0:T(8,128)(2,1)}, f32[2,128]{1,0:T(2,128)}) custom-call(s32[8,128]{1,0:T(8,128)S(1)} %scalars.1.after.info, bf16[272,256]{1,0:T(8,128)(2,1)S(1)} %truncate.1.pack_ref.after, bf16[272,256]{1,0:T(8,128)(2,1)S(1)} %collective-permute-done.14.got_ref, ...), custom_call_target="tpu_custom_call", output_to_operand_aliasing={{0}: (4, {})} | custom-call | flops 1073741824 | bytes 8388608 | tf_op jit(solution)/shard_map/update_other/pallas_call | solution.py:729
  (25 shorter events, 1.4 us)
Async XLA Ops:
  0.6 8.0 %copy-start.1 = (s32[128]{0:T(128)S(1)}, s32[128]{0:T(128)}, u32[]{:S(2)}) copy-start(s32[128]{0:T(128)} %ranks.1) | copy-start | bytes 1540
  0.6 7.9 %copy-start = (s32[128,3]{0,1:T(4,128)S(1)}, s32[128,3]{0,1:T(4,128)}, u32[]{:S(2)}) copy-start(s32[128,3]{0,1:T(4,128)} %param.6) | copy-start | bytes 4612
  5.3 5.2 %collective-permute-start = (f32[8,128]{1,0:T(8,128)S(1)}, f32[8,128]{1,0:T(8,128)S(1)}, u32[]{:S(2)}, u32[]{:S(2)}) collective-permute-start(f32[8,128]{1,0:T(8,128)S(1)} %get-tuple-element.21.after.one_ref), channel_id=1, source_target_pairs={{0,1},{1,0},{2,3},{3,2},{4,5},{5,4},{6,7},{7,6},{8,9},{9,8},{10,11... | collective-permute-start | bytes 12296 | tf_op jit(solution)/shard_map/ppermute | solution.py:772
  10.5 7.3 %collective-permute-start.2 = (f32[8,128]{1,0:T(8,128)S(1)}, f32[8,128]{1,0:T(8,128)S(1)}, u32[]{:S(2)}, u32[]{:S(2)}) collective-permute-start(f32[8,128]{1,0:T(8,128)S(1)} %add.13.own_ref), channel_id=1, source_target_pairs={{0,2},{2,0},{4,6},{6,4},{8,10},{10,8},{12,14},{14,12},{16,18},{18,... | collective-permute-start | bytes 12296 | tf_op jit(solution)/shard_map/ppermute | solution.py:775
  10.5 10.6 %collective-permute-start.1 = (f32[8,128]{1,0:T(8,128)S(1)}, f32[8,128]{1,0:T(8,128)S(1)}, u32[]{:S(2)}, u32[]{:S(2)}) collective-permute-start(f32[8,128]{1,0:T(8,128)S(1)} %add.13.own_ref), channel_id=1, source_target_pairs={{2,4},{6,8},{10,12},{14,16},{18,20},{22,24},{26,28},{30,32},{34,36... | collective-permute-start | bytes 12296 | tf_op jit(solution)/shard_map/ppermute | solution.py:774
  21.5 5.1 %collective-permute-start.3 = (f32[8,128]{1,0:T(8,128)S(1)}, f32[8,128]{1,0:T(8,128)S(1)}, u32[]{:S(2)}, u32[]{:S(2)}) collective-permute-start(f32[8,128]{1,0:T(8,128)S(1)} %outer_round.3), channel_id=1, source_target_pairs={{0,1},{1,0},{2,3},{3,2},{4,5},{5,4},{6,7},{7,6},{8,9},{9,8},{10,11... | collective-permute-start | bytes 12296 | tf_op jit(solution)/shard_map/ppermute | solution.py:772
  26.6 3.7 %collective-permute-start.5 = (f32[8,128]{1,0:T(8,128)S(1)}, f32[8,128]{1,0:T(8,128)S(1)}, u32[]{:S(2)}, u32[]{:S(2)}) collective-permute-start(f32[8,128]{1,0:T(8,128)S(1)} %add.10.own_ref), channel_id=1, source_target_pairs={{0,2},{2,0},{4,6},{6,4},{8,10},{10,8},{12,14},{14,12},{16,18},{18,... | collective-permute-start | bytes 12296 | tf_op jit(solution)/shard_map/ppermute | solution.py:775
  26.6 7.9 %collective-permute-start.4 = (f32[8,128]{1,0:T(8,128)S(1)}, f32[8,128]{1,0:T(8,128)S(1)}, u32[]{:S(2)}, u32[]{:S(2)}) collective-permute-start(f32[8,128]{1,0:T(8,128)S(1)} %add.10.own_ref), channel_id=1, source_target_pairs={{2,4},{6,8},{10,12},{14,16},{18,20},{22,24},{26,28},{30,32},{34,36... | collective-permute-start | bytes 12296 | tf_op jit(solution)/shard_map/ppermute | solution.py:774
  34.9 5.1 %collective-permute-start.6 = (f32[8,128]{1,0:T(8,128)S(1)}, f32[8,128]{1,0:T(8,128)S(1)}, u32[]{:S(2)}, u32[]{:S(2)}) collective-permute-start(f32[8,128]{1,0:T(8,128)S(1)} %outer_round.4), channel_id=1, source_target_pairs={{0,1},{1,0},{2,3},{3,2},{4,5},{5,4},{6,7},{7,6},{8,9},{9,8},{10,11... | collective-permute-start | bytes 12296 | tf_op jit(solution)/shard_map/ppermute | solution.py:772
  40.0 2.6 %collective-permute-start.8 = (f32[8,128]{1,0:T(8,128)S(1)}, f32[8,128]{1,0:T(8,128)S(1)}, u32[]{:S(2)}, u32[]{:S(2)}) collective-permute-start(f32[8,128]{1,0:T(8,128)S(1)} %add.11.own_ref), channel_id=1, source_target_pairs={{0,2},{2,0},{4,6},{6,4},{8,10},{10,8},{12,14},{14,12},{16,18},{18,... | collective-permute-start | bytes 12296 | tf_op jit(solution)/shard_map/ppermute | solution.py:775
  40.0 7.9 %collective-permute-start.7 = (f32[8,128]{1,0:T(8,128)S(1)}, f32[8,128]{1,0:T(8,128)S(1)}, u32[]{:S(2)}, u32[]{:S(2)}) collective-permute-start(f32[8,128]{1,0:T(8,128)S(1)} %add.11.own_ref), channel_id=1, source_target_pairs={{2,4},{6,8},{10,12},{14,16},{18,20},{22,24},{26,28},{30,32},{34,36... | collective-permute-start | bytes 12296 | tf_op jit(solution)/shard_map/ppermute | solution.py:774
  48.4 5.1 %collective-permute-start.9 = (f32[8,128]{1,0:T(8,128)S(1)}, f32[8,128]{1,0:T(8,128)S(1)}, u32[]{:S(2)}, u32[]{:S(2)}) collective-permute-start(f32[8,128]{1,0:T(8,128)S(1)} %outer_round.5), channel_id=1, source_target_pairs={{0,1},{1,0},{2,3},{3,2},{4,5},{5,4},{6,7},{7,6},{8,9},{9,8},{10,11... | collective-permute-start | bytes 12296 | tf_op jit(solution)/shard_map/ppermute | solution.py:772
  53.5 8.0 %collective-permute-start.11 = (f32[8,128]{1,0:T(8,128)S(1)}, f32[8,128]{1,0:T(8,128)S(1)}, u32[]{:S(2)}, u32[]{:S(2)}) collective-permute-start(f32[8,128]{1,0:T(8,128)S(1)} %add.12.after.own_ref), channel_id=1, source_target_pairs={{2,4},{6,8},{10,12},{14,16},{18,20},{22,24},{26,28},{30,32},{34,36... | collective-permute-start | bytes 12296 | tf_op jit(solution)/shard_map/ppermute | solution.py:774
  55.9 5.6 %collective-permute-start.10 = (f32[8,128]{1,0:T(8,128)S(1)}, f32[8,128]{1,0:T(8,128)S(1)}, u32[]{:S(2)}, u32[]{:S(2)}) collective-permute-start(f32[8,128]{1,0:T(8,128)S(1)} %add.12.after.own_ref), channel_id=1, source_target_pairs={{0,2},{2,0},{4,6},{6,4},{8,10},{10,8},{12,14},{14,12},{16,18},{18,... | collective-permute-start | bytes 12296 | tf_op jit(solution)/shard_map/ppermute | solution.py:775
  63.3 14.1 %copy-start.2 = (f32[512,128]{1,0:T(8,128)S(1)}, f32[512,128]{1,0:T(8,128)}, u32[]{:S(2)}) copy-start(f32[512,128]{1,0:T(8,128)} %probes_ref.1) | copy-start | bytes 786436
  63.3 14.1 %copy-start.3 = (f32[4,4]{1,0:T(4,128)S(1)}, f32[4,4]{1,0:T(4,128)}, u32[]{:S(2)}) copy-start(f32[4,4]{1,0:T(4,128)} %gate.1) | copy-start | bytes 196
  63.3 7.4 %collective-permute-start.12 = (f32[3,128,128]{2,1,0:T(8,128)S(1)}, f32[3,128,128]{2,1,0:T(8,128)S(1)}, u32[]{:S(2)}, u32[]{:S(2)}) collective-permute-start(f32[3,128,128]{2,1,0:T(8,128)S(1)} %gram_to_send.1.after), channel_id=1, source_target_pairs={{0,1},{1,0},{2,3},{3,2},{4,5},{5,4},{6,7},{7,6},{8,9},{9,8},{10,11... | collective-permute-start | bytes 589832 | tf_op jit(solution)/shard_map/ppermute | solution.py:778
  75.8 1.6 %collective-permute-start.13 = (f32[256,256]{1,0:T(8,128)S(1)}, f32[256,256]{1,0:T(8,128)S(1)}, u32[]{:S(2)}, u32[]{:S(2)}) collective-permute-start(f32[256,256]{1,0:T(8,128)S(1)} %get-tuple-element.34.upper_ref), channel_id=1, source_target_pairs={{0,2},{2,0},{4,6},{6,4},{8,10},{10,8},{12,14},{14,12},{16,18},{18,... | collective-permute-start | bytes 786440 | tf_op jit(solution)/shard_map/ppermute | solution.py:781
  81.8 7.3 %collective-permute-start.14 = (bf16[272,256]{1,0:T(8,128)(2,1)S(1)}, bf16[272,256]{1,0:T(8,128)(2,1)S(1)}, u32[]{:S(2)}, u32[]{:S(2)}) collective-permute-start(bf16[272,256]{1,0:T(8,128)(2,1)S(1)} %truncate.1.pack_ref.after), channel_id=1, source_target_pairs={{0,1},{1,0},{2,3},{3,2},{4,5},{5,4},{6,7},{7,6},{8,9},{9,8},{10,11... | collective-permute-start | bytes 417800 | tf_op jit(solution)/shard_map/ppermute | solution.py:783

commit v5 on v4

--- a/solution.py
+++ b/solution.py
@@ -12,7 +12,6 @@
 F32 = jnp.float32
 BF16 = jnp.bfloat16
 MB = 1 << 20
-highest = lax.Precision.HIGHEST
 
 CORE, ROW, MATE0, MATE1, FIRST, LAST, KEPT, RANK, GATED = range(9)
 
@@ -47,10 +46,6 @@
     return dot_of(left[0], right[0], dims) + (
         dot_of(left[0], right[1], dims) + dot_of(left[1], right[0], dims)
     )
-
-
-def dot_high(left, right, dims=((1,), (0,))):
-    return lax.dot_general(left, right, (dims, ((), ())), preferred_element_type=F32, precision=highest)
 
 
 def down(row):
@@ -214,7 +209,7 @@
 
 def open_call(x):
     members, rows, wide, bond = x.shape
-    block = 8
+    block = 16
     steps = members * rows // block
     return pl.pallas_call(
         open_kernel,
@@ -280,11 +275,11 @@
 
 
 def by_row(row, matrix):
-    return dot_high(jnp.broadcast_to(row, (8, row.shape[1])), matrix)[:1]
+    return dot3(halves(jnp.broadcast_to(row, (16, row.shape[1]))), halves(matrix))[:1]
 
 
 def by_column(row, matrix):
-    return dot_high(jnp.broadcast_to(row, (8, row.shape[1])), matrix, ((1,), (1,)))[:1]
+    return dot3(halves(jnp.broadcast_to(row, (16, row.shape[1]))), halves(matrix), ((1,), (1,)))[:1]
 
 
 def put_leg(out_ref, member, leg, row):
@@ -435,7 +430,7 @@
     )(info, side, part, mixed, other)
 
 
-def add_gram(info, member, weights, d_ref, out_ref, first_ref, gram):
+def add_gram(info, member, weights, d_ref, first_ref, gram):
     rows, bond = d_ref.shape[1:3]
     block = 64
     start = info[0, ROW] * rows
@@ -455,9 +450,6 @@
         return carry
 
     lax.fori_loop(0, rows // block, body, 0)
-    out_ref[0] = gram[:bond, :bond]
-    out_ref[1] = gram[:bond, bond:]
-    out_ref[2] = gram[bond:, bond:]
 
 
 def gram_weights(info, member, own_ref, mate_ref, side_ref):
@@ -468,19 +460,29 @@
 
 
 def send_kernel(info, own_ref, mate_ref, side_ref, d_ref, out_ref, first_ref, gram):
+    bond = d_ref.shape[2]
     member = 1 - info[0, KEPT]
     weights = gram_weights(info, member, own_ref, mate_ref, side_ref)
-    add_gram(info, member, weights, d_ref, out_ref, first_ref, gram)
+    add_gram(info, member, weights, d_ref, first_ref, gram)
+    corner, above, below = (gram[:bond, :bond], gram[:bond, bond:], gram[bond:, bond:])
+    out_ref[:bond] = jnp.where(below_diagonal(bond), below, corner)
+    out_ref[bond : 2 * bond] = above
+    diagonal = jnp.sum(jnp.where(eye_mask(bond), below, 0.0), axis=0, keepdims=True)
+    out_ref[2 * bond :] = jnp.broadcast_to(diagonal, (8, bond))
 
 
 def keep_kernel(info, own_ref, mate_ref, side_ref, d_ref, after, out_ref, msg_ref, first_ref, gram):
+    bond = d_ref.shape[2]
     member = info[0, KEPT]
     weights = gram_weights(info, member, own_ref, mate_ref, side_ref)
     own = normalized(own_ref)
     for place in range(2):
         for leg in range(3):
             msg_ref[leg, pl.ds(place, 1), :] = pick(own, place, leg)
-    add_gram(info, member, weights, d_ref, out_ref, first_ref, gram)
+    add_gram(info, member, weights, d_ref, first_ref, gram)
+    out_ref[0] = gram[:bond, :bond]
+    out_ref[1] = gram[:bond, bond:]
+    out_ref[2] = gram[bond:, bond:]
 
 
 def gram_call(kernel, name, extra_specs, out_specs, out_shape, flat, operands):
@@ -499,7 +501,7 @@
 
 def send_call(info, own, mate, side, flat):
     bond = flat.shape[2]
-    shape = jax.ShapeDtypeStruct((3, bond, bond), F32)
+    shape = jax.ShapeDtypeStruct((2 * bond + 8, bond), F32)
     operands = (info, own, mate, side, flat)
     return gram_call(send_kernel, "gram_to_send", [], vmem(), shape, flat, operands)
 
@@ -518,6 +520,11 @@
     down_index = lax.broadcasted_iota(jnp.int32, (size, size), 0)
     across_index = lax.broadcasted_iota(jnp.int32, (size, size), 1)
     return down_index == across_index
+
+
+def below_diagonal(size):
+    down_index = lax.broadcasted_iota(jnp.int32, (size, size), 0)
+    return down_index > lax.broadcasted_iota(jnp.int32, (size, size), 1)
 
 
 def root_sweeps(matrix):
@@ -548,9 +555,14 @@
 
 
 def root_kernel(keep_ref, got_ref, upper_ref, inverse_ref):
-    corner = keep_ref[0] + got_ref[0]
-    above = keep_ref[1] + got_ref[1]
-    below = keep_ref[2] + got_ref[2]
+    bond = keep_ref.shape[1]
+    merged = got_ref[:bond]
+    flipped = jnp.transpose(merged)
+    lower = below_diagonal(bond)
+    got_below = jnp.where(eye_mask(bond), got_ref[2 * bond : 2 * bond + 1], jnp.where(lower, merged, flipped))
+    corner = keep_ref[0] + jnp.where(lower, flipped, merged)
+    above = keep_ref[1] + got_ref[bond : 2 * bond]
+    below = keep_ref[2] + got_below
     matrix = jnp.concatenate(
         [
             jnp.concatenate([corner, above], axis=1),

time: 92.8 us -> 92.1 us (level)
  no operation moved by 1% of the time
where the time goes in v5:
time: 92.1 us; the launch traced here: 91.9 us
  Pallas kernels  38 us (41%)
  starting transfers between devices  34.3 us (37%)
  waiting for transfers between devices  18.6 us (20%)
  between operations  0.97 us (1%)
    ppermute x4, starting transfers between devices, shards(): side = lax.ppermute(own, 'site', side_swap)  15.9 us
    ppermute x4, starting transfers between devices, shards(): got = lax.ppermute(part, 'row', row_swap)  12 us
    pallas_call x3, Pallas kernels, inner_call(): pl.pallas_call(inner_kernel, in_specs=[vmem(), vmem(), vmem(), vmem()], o...  9.45 us
    ppermute x4, waiting for transfers between devices, shards(): got = lax.ppermute(part, 'row', row_swap)  7.91 us
    pallas_call x2, Pallas kernels, update_call(): pl.pallas_call(kernel, in_specs=in_specs, out_specs=[hbm(), hbm()] if wit...  6.71 us
    ppermute x4, waiting for transfers between devices, shards(): side = lax.ppermute(own, 'site', side_swap)  6.42 us
    pallas_call x1, Pallas kernels, root_call(): pl.pallas_call(root_kernel, in_specs=[vmem(), vmem()], out_specs=[vmem(),...  5.13 us
    pallas_call x1, Pallas kernels, open_call(): pl.pallas_call(open_kernel, in_specs=[hbm()], out_specs=[vmem(), vmem(),...  4.63 us
  transfers between devices with their start and end apart: 15, of which 10 were waited for; matrix products, arithmetic and copies ran while one was open for 0% of the time, Pallas kernels for 19%

profile of v5, /device:TPU:6, one launch (start us, length us, event | category | flops | bytes accessed | tf_op | source)
XLA Modules:
  0.0 91.9 jit_solution(12682418920481896652)
XLA Ops:
  0.7 4.6 %open.1 = (bf16[2,64,256,128]{3,2,1,0:T(8,128)(2,1)S(1)}, bf16[2,64,128,128]{3,2,1,0:T(8,128)(2,1)S(1)}, f32[8,128]{1,0:T(8,128)S(1)}) custom-call(bf16[2,64,256,128]{3,2,1,0:T(8,128)(2,1)} %bitcast.6), custom_call_target="tpu_custom_call" | custom-call | flops 16777216 | bytes 20971520 | tf_op jit(solution)/shard_map/open/pallas_call | solution.py:214
  5.3 3.3 %collective-permute-start = (f32[8,128]{1,0:T(8,128)S(1)}, f32[8,128]{1,0:T(8,128)S(1)}, u32[]{:S(2)}, u32[]{:S(2)}) collective-permute-start(f32[8,128]{1,0:T(8,128)S(1)} %get-tuple-element.21.after.one_ref), channel_id=1, source_target_pairs={{0,1},{1,0},{2,3},{3,2},{4,5},{5,4},{6,7},{7,6},{8,9},{9,8},{10,11... | collective-permute-start | bytes 12296 | tf_op jit(solution)/shard_map/ppermute | solution.py:784
  8.6 0.6 scalars.1.after.info
  9.2 1.3 %collective-permute-done.two_ref = f32[8,128]{1,0:T(8,128)S(1)} collective-permute-done((f32[8,128]{1,0:T(8,128)S(1)}, f32[8,128]{1,0:T(8,128)S(1)}, u32[]{:S(2)}, u32[]{:S(2)}) %collective-permute-start) | collective-permute-done | bytes 4128 | tf_op jit(solution)/shard_map/ppermute | solution.py:784
  10.5 7.3 %collective-permute-start.1 = (f32[8,128]{1,0:T(8,128)S(1)}, f32[8,128]{1,0:T(8,128)S(1)}, u32[]{:S(2)}, u32[]{:S(2)}) collective-permute-start(f32[8,128]{1,0:T(8,128)S(1)} %add.13.own_ref), channel_id=1, source_target_pairs={{2,4},{6,8},{10,12},{14,16},{18,20},{22,24},{26,28},{30,32},{34,36... | collective-permute-start | bytes 12296 | tf_op jit(solution)/shard_map/ppermute | solution.py:786
  17.8 3.1 %inner_round.3 = (f32[8,128]{1,0:T(8,128)S(1)}, f32[64,128]{1,0:T(8,128)S(1)}, f32[128,128]{1,0:T(8,128)S(1)}) custom-call(s32[8,128]{1,0:T(8,128)S(1)} %scalars.1.after.info, f32[8,128]{1,0:T(8,128)S(1)} %add.13.own_ref, f32[8,128]{1,0:T(8,128)S(1)} %collective-permute-done.2.mate_ref, bf16[2,64,128,128]{3,2,1,0:T(8,128)(2,1)S(1)} %get-tuple-element.22.s_ref), custom_call_target="tpu_custom_call" | custom-call | flops 8388608 | bytes 4194304 | tf_op jit(solution)/shard_map/inner_round/pallas_call | solution.py:405
  21.4 2.9 %collective-permute-start.3 = (f32[8,128]{1,0:T(8,128)S(1)}, f32[8,128]{1,0:T(8,128)S(1)}, u32[]{:S(2)}, u32[]{:S(2)}) collective-permute-start(f32[8,128]{1,0:T(8,128)S(1)} %outer_round.3), channel_id=1, source_target_pairs={{0,1},{1,0},{2,3},{3,2},{4,5},{5,4},{6,7},{7,6},{8,9},{9,8},{10,11... | collective-permute-start | bytes 12296 | tf_op jit(solution)/shard_map/ppermute | solution.py:784
  24.3 2.2 %collective-permute-done.3 = f32[8,128]{1,0:T(8,128)S(1)} collective-permute-done((f32[8,128]{1,0:T(8,128)S(1)}, f32[8,128]{1,0:T(8,128)S(1)}, u32[]{:S(2)}, u32[]{:S(2)}) %collective-permute-start.3) | collective-permute-done | bytes 4128 | tf_op jit(solution)/shard_map/ppermute | solution.py:784
  26.5 3.7 %collective-permute-start.4 = (f32[8,128]{1,0:T(8,128)S(1)}, f32[8,128]{1,0:T(8,128)S(1)}, u32[]{:S(2)}, u32[]{:S(2)}) collective-permute-start(f32[8,128]{1,0:T(8,128)S(1)} %add.10.own_ref), channel_id=1, source_target_pairs={{2,4},{6,8},{10,12},{14,16},{18,20},{22,24},{26,28},{30,32},{34,36... | collective-permute-start | bytes 12296 | tf_op jit(solution)/shard_map/ppermute | solution.py:786
  30.2 3.1 %inner_round.4 = (f32[8,128]{1,0:T(8,128)S(1)}, f32[64,128]{1,0:T(8,128)S(1)}, f32[128,128]{1,0:T(8,128)S(1)}) custom-call(s32[8,128]{1,0:T(8,128)S(1)} %scalars.1.after.info, f32[8,128]{1,0:T(8,128)S(1)} %add.10.own_ref, f32[8,128]{1,0:T(8,128)S(1)} %collective-permute-done.5.mate_ref, bf16[2,64,128,128]{3,2,1,0:T(8,128)(2,1)S(1)} %get-tuple-element.22.s_ref), custom_call_target="tpu_custom_call" | custom-call | flops 8388608 | bytes 4194304 | tf_op jit(solution)/shard_map/inner_round/pallas_call | solution.py:405
  33.3 1.1 %collective-permute-done.4.side_ref = f32[8,128]{1,0:T(8,128)S(1)} collective-permute-done((f32[8,128]{1,0:T(8,128)S(1)}, f32[8,128]{1,0:T(8,128)S(1)}, u32[]{:S(2)}, u32[]{:S(2)}) %collective-permute-start.4) | collective-permute-done | bytes 4128 | tf_op jit(solution)/shard_map/ppermute | solution.py:786
  34.8 2.9 %collective-permute-start.6 = (f32[8,128]{1,0:T(8,128)S(1)}, f32[8,128]{1,0:T(8,128)S(1)}, u32[]{:S(2)}, u32[]{:S(2)}) collective-permute-start(f32[8,128]{1,0:T(8,128)S(1)} %outer_round.4), channel_id=1, source_target_pairs={{0,1},{1,0},{2,3},{3,2},{4,5},{5,4},{6,7},{7,6},{8,9},{9,8},{10,11... | collective-permute-start | bytes 12296 | tf_op jit(solution)/shard_map/ppermute | solution.py:784
  37.7 2.2 %collective-permute-done.6 = f32[8,128]{1,0:T(8,128)S(1)} collective-permute-done((f32[8,128]{1,0:T(8,128)S(1)}, f32[8,128]{1,0:T(8,128)S(1)}, u32[]{:S(2)}, u32[]{:S(2)}) %collective-permute-start.6) | collective-permute-done | bytes 4128 | tf_op jit(solution)/shard_map/ppermute | solution.py:784
  40.0 2.6 %collective-permute-start.7 = (f32[8,128]{1,0:T(8,128)S(1)}, f32[8,128]{1,0:T(8,128)S(1)}, u32[]{:S(2)}, u32[]{:S(2)}) collective-permute-start(f32[8,128]{1,0:T(8,128)S(1)} %add.11.own_ref), channel_id=1, source_target_pairs={{2,4},{6,8},{10,12},{14,16},{18,20},{22,24},{26,28},{30,32},{34,36... | collective-permute-start | bytes 12296 | tf_op jit(solution)/shard_map/ppermute | solution.py:786
  42.5 3.1 %inner_round.5 = (f32[8,128]{1,0:T(8,128)S(1)}, f32[64,128]{1,0:T(8,128)S(1)}, f32[128,128]{1,0:T(8,128)S(1)}) custom-call(s32[8,128]{1,0:T(8,128)S(1)} %scalars.1.after.info, f32[8,128]{1,0:T(8,128)S(1)} %add.11.own_ref, f32[8,128]{1,0:T(8,128)S(1)} %collective-permute-done.8.mate_ref, bf16[2,64,128,128]{3,2,1,0:T(8,128)(2,1)S(1)} %get-tuple-element.22.s_ref), custom_call_target="tpu_custom_call" | custom-call | flops 8388608 | bytes 4194304 | tf_op jit(solution)/shard_map/inner_round/pallas_call | solution.py:405
  45.7 2.2 %collective-permute-done.7.side_ref = f32[8,128]{1,0:T(8,128)S(1)} collective-permute-done((f32[8,128]{1,0:T(8,128)S(1)}, f32[8,128]{1,0:T(8,128)S(1)}, u32[]{:S(2)}, u32[]{:S(2)}) %collective-permute-start.7) | collective-permute-done | bytes 4128 | tf_op jit(solution)/shard_map/ppermute | solution.py:786
  48.3 2.9 %collective-permute-start.9 = (f32[8,128]{1,0:T(8,128)S(1)}, f32[8,128]{1,0:T(8,128)S(1)}, u32[]{:S(2)}, u32[]{:S(2)}) collective-permute-start(f32[8,128]{1,0:T(8,128)S(1)} %outer_round.5), channel_id=1, source_target_pairs={{0,1},{1,0},{2,3},{3,2},{4,5},{5,4},{6,7},{7,6},{8,9},{9,8},{10,11... | collective-permute-start | bytes 12296 | tf_op jit(solution)/shard_map/ppermute | solution.py:784
  51.2 2.2 %collective-permute-done.9 = f32[8,128]{1,0:T(8,128)S(1)} collective-permute-done((f32[8,128]{1,0:T(8,128)S(1)}, f32[8,128]{1,0:T(8,128)S(1)}, u32[]{:S(2)}, u32[]{:S(2)}) %collective-permute-start.9) | collective-permute-done | bytes 4128 | tf_op jit(solution)/shard_map/ppermute | solution.py:784
  53.4 2.4 %collective-permute-start.11 = (f32[8,128]{1,0:T(8,128)S(1)}, f32[8,128]{1,0:T(8,128)S(1)}, u32[]{:S(2)}, u32[]{:S(2)}) collective-permute-start(f32[8,128]{1,0:T(8,128)S(1)} %add.12.after.own_ref), channel_id=1, source_target_pairs={{2,4},{6,8},{10,12},{14,16},{18,20},{22,24},{26,28},{30,32},{34,36... | collective-permute-start | bytes 12296 | tf_op jit(solution)/shard_map/ppermute | solution.py:786
  55.9 2.4 %flatten.1.d_ref = bf16[2,64,128,256]{3,2,1,0:T(8,128)(2,1)S(1)} custom-call(f32[8,128]{1,0:T(8,128)S(1)} %add.12.after.own_ref, bf16[2,64,256,128]{3,2,1,0:T(8,128)(2,1)S(1)} %get-tuple-element.32.x_ref), custom_call_target="tpu_custom_call" | custom-call | flops 8388608 | bytes 16777216 | tf_op jit(solution)/shard_map/flatten/pallas_call | solution.py:251
  58.3 3.1 %collective-permute-done.11.side_ref = f32[8,128]{1,0:T(8,128)S(1)} collective-permute-done((f32[8,128]{1,0:T(8,128)S(1)}, f32[8,128]{1,0:T(8,128)S(1)}, u32[]{:S(2)}, u32[]{:S(2)}) %collective-permute-start.11) | collective-permute-done | bytes 4128 | tf_op jit(solution)/shard_map/ppermute | solution.py:786
  61.4 1.8 %gram_to_send.1.after = f32[264,128]{1,0:T(8,128)S(1)} custom-call(s32[8,128]{1,0:T(8,128)S(1)} %scalars.1.after.info, f32[8,128]{1,0:T(8,128)S(1)} %add.12.after.own_ref, f32[8,128]{1,0:T(8,128)S(1)} %collective-permute-done.10.mate_ref, f32[8,128]{1,0:T(8,128)S(1)} %collective-permute-done.11.side_ref, bf16[2,64,128,256]{3,2,1,0:T(8,128)(2,1)S(1)} %flatten.1.d_ref), custom_call_target="tpu_custom_call" | custom-call | flops 1073741824 | bytes 4194304 | tf_op jit(solution)/shard_map/gram_to_send/pallas_call | solution.py:490
  63.2 3.2 %collective-permute-start.12 = (f32[264,128]{1,0:T(8,128)S(1)}, f32[264,128]{1,0:T(8,128)S(1)}, u32[]{:S(2)}, u32[]{:S(2)}) collective-permute-start(f32[264,128]{1,0:T(8,128)S(1)} %gram_to_send.1.after), channel_id=1, source_target_pairs={{0,1},{1,0},{2,3},{3,2},{4,5},{5,4},{6,7},{7,6},{8,9},{9,8},{10,11... | collective-permute-start | bytes 405512 | tf_op jit(solution)/shard_map/ppermute | solution.py:790
  66.4 1.8 %gram_to_keep.1 = (f32[3,128,128]{2,1,0:T(8,128)S(1)}, f32[3,2,128]{2,1,0:T(2,128)}) custom-call(s32[8,128]{1,0:T(8,128)S(1)} %scalars.1.after.info, f32[8,128]{1,0:T(8,128)S(1)} %add.12.after.own_ref, f32[8,128]{1,0:T(8,128)S(1)} %collective-permute-done.10.mate_ref, f32[8,128]{1,0:T(8,128)S(1)} %collective-permute-done.11.side_ref, ...), custom_call_target="tpu_custom_call" | custom-call | flops 1073741824 | bytes 4194304 | tf_op jit(solution)/shard_map/gram_to_keep/pallas_call | solution.py:490
  68.2 1.8 %collective-permute-done.12.got_ref = f32[264,128]{1,0:T(8,128)S(1)} collective-permute-done((f32[264,128]{1,0:T(8,128)S(1)}, f32[264,128]{1,0:T(8,128)S(1)}, u32[]{:S(2)}, u32[]{:S(2)}) %collective-permute-start.12) | collective-permute-done | bytes 135200 | tf_op jit(solution)/shard_map/ppermute | solution.py:790
  70.0 5.1 %root.1 = (f32[256,256]{1,0:T(8,128)S(1)}, f32[256,256]{1,0:T(8,128)S(1)}) custom-call(f32[3,128,128]{2,1,0:T(8,128)S(1)} %get-tuple-element.33.keep_ref, f32[264,128]{1,0:T(8,128)S(1)} %collective-permute-done.12.got_ref), custom_call_target="tpu_custom_call" | custom-call | flops 2214592512 | bytes 1048576 | tf_op jit(solution)/shard_map/root/pallas_call | solution.py:579
  75.2 1.5 %collective-permute-done.13.other_ref = f32[256,256]{1,0:T(8,128)S(1)} collective-permute-done((f32[256,256]{1,0:T(8,128)S(1)}, f32[256,256]{1,0:T(8,128)S(1)}, u32[]{:S(2)}, u32[]{:S(2)}) %collective-permute-start.13) | collective-permute-done | bytes 262176 | tf_op jit(solution)/shard_map/ppermute | solution.py:793
  76.8 4.3 %truncate.1.pack_ref.after = bf16[272,256]{1,0:T(8,128)(2,1)S(1)} custom-call(s32[8,128]{1,0:T(8,128)S(1)} %scalars.1.after.info, f32[4,4]{1,0:T(4,128)S(1)} %copy-done.3, f32[8,128]{1,0:T(8,128)S(1)} %add.12.after.own_ref, f32[8,128]{1,0:T(8,128)S(1)} %collective-permute-done.10.mate_ref, f32[256,256]{1,0:T(8,128)S(1)} %get-tuple-element.34.upper_ref, ...), custom_call_target="tpu_custom_call" | custom-call | flops 1342177280 | bytes 1572864 | tf_op jit(solution)/shard_map/truncate/pallas_call | solution.py:670
  81.1 3.0 %collective-permute-start.14 = (bf16[272,256]{1,0:T(8,128)(2,1)S(1)}, bf16[272,256]{1,0:T(8,128)(2,1)S(1)}, u32[]{:S(2)}, u32[]{:S(2)}) collective-permute-start(bf16[272,256]{1,0:T(8,128)(2,1)S(1)} %truncate.1.pack_ref.after), channel_id=1, source_target_pairs={{0,1},{1,0},{2,3},{3,2},{4,5},{5,4},{6,7},{7,6},{8,9},{9,8},{10,11... | collective-permute-start | bytes 417800 | tf_op jit(solution)/shard_map/ppermute | solution.py:795
  84.1 3.3 %update_own.1.begun_hbm = bf16[2,64,256,128]{3,2,1,0:T(8,128)(2,1)} custom-call(s32[8,128]{1,0:T(8,128)S(1)} %scalars.1.after.info, bf16[272,256]{1,0:T(8,128)(2,1)S(1)} %truncate.1.pack_ref.after, bf16[2,64,128,256]{3,2,1,0:T(8,128)(2,1)S(1)} %flatten.1.d_ref, bf16[272,256]{1,0:T(8,128)(2,1)S(1)} %truncate.1.pack_ref.after), custom_call_target="tpu_custom_call" | custom-call | flops 1073741824 | bytes 8388608 | tf_op jit(solution)/shard_map/update_own/pallas_call | solution.py:741
  87.5 0.9 %collective-permute-done.14.got_ref = bf16[272,256]{1,0:T(8,128)(2,1)S(1)} collective-permute-done((bf16[272,256]{1,0:T(8,128)(2,1)S(1)}, bf16[272,256]{1,0:T(8,128)(2,1)S(1)}, u32[]{:S(2)}, u32[]{:S(2)}) %collective-permute-start.14) | collective-permute-done | bytes 139296 | tf_op jit(solution)/shard_map/ppermute | solution.py:795
  88.4 3.4 %update_other.1 = (bf16[2,64,256,128]{3,2,1,0:T(8,128)(2,1)}, f32[2,128]{1,0:T(2,128)}) custom-call(s32[8,128]{1,0:T(8,128)S(1)} %scalars.1.after.info, bf16[272,256]{1,0:T(8,128)(2,1)S(1)} %truncate.1.pack_ref.after, bf16[272,256]{1,0:T(8,128)(2,1)S(1)} %collective-permute-done.14.got_ref, ...), custom_call_target="tpu_custom_call", output_to_operand_aliasing={{0}: (4, {})} | custom-call | flops 1073741824 | bytes 8388608 | tf_op jit(solution)/shard_map/update_other/pallas_call | solution.py:741
  (25 shorter events, 1.4 us)
Async XLA Ops:
  0.6 7.9 %copy-start.1 = (s32[128]{0:T(128)S(1)}, s32[128]{0:T(128)}, u32[]{:S(2)}) copy-start(s32[128]{0:T(128)} %ranks.1) | copy-start | bytes 1540
  0.6 7.9 %copy-start = (s32[128,3]{0,1:T(4,128)S(1)}, s32[128,3]{0,1:T(4,128)}, u32[]{:S(2)}) copy-start(s32[128,3]{0,1:T(4,128)} %param.6) | copy-start | bytes 4612
  5.3 5.2 %collective-permute-start = (f32[8,128]{1,0:T(8,128)S(1)}, f32[8,128]{1,0:T(8,128)S(1)}, u32[]{:S(2)}, u32[]{:S(2)}) collective-permute-start(f32[8,128]{1,0:T(8,128)S(1)} %get-tuple-element.21.after.one_ref), channel_id=1, source_target_pairs={{0,1},{1,0},{2,3},{3,2},{4,5},{5,4},{6,7},{7,6},{8,9},{9,8},{10,11... | collective-permute-start | bytes 12296 | tf_op jit(solution)/shard_map/ppermute | solution.py:784
  10.5 7.3 %collective-permute-start.2 = (f32[8,128]{1,0:T(8,128)S(1)}, f32[8,128]{1,0:T(8,128)S(1)}, u32[]{:S(2)}, u32[]{:S(2)}) collective-permute-start(f32[8,128]{1,0:T(8,128)S(1)} %add.13.own_ref), channel_id=1, source_target_pairs={{0,2},{2,0},{4,6},{6,4},{8,10},{10,8},{12,14},{14,12},{16,18},{18,... | collective-permute-start | bytes 12296 | tf_op jit(solution)/shard_map/ppermute | solution.py:787
  10.5 10.5 %collective-permute-start.1 = (f32[8,128]{1,0:T(8,128)S(1)}, f32[8,128]{1,0:T(8,128)S(1)}, u32[]{:S(2)}, u32[]{:S(2)}) collective-permute-start(f32[8,128]{1,0:T(8,128)S(1)} %add.13.own_ref), channel_id=1, source_target_pairs={{2,4},{6,8},{10,12},{14,16},{18,20},{22,24},{26,28},{30,32},{34,36... | collective-permute-start | bytes 12296 | tf_op jit(solution)/shard_map/ppermute | solution.py:786
  21.4 5.1 %collective-permute-start.3 = (f32[8,128]{1,0:T(8,128)S(1)}, f32[8,128]{1,0:T(8,128)S(1)}, u32[]{:S(2)}, u32[]{:S(2)}) collective-permute-start(f32[8,128]{1,0:T(8,128)S(1)} %outer_round.3), channel_id=1, source_target_pairs={{0,1},{1,0},{2,3},{3,2},{4,5},{5,4},{6,7},{7,6},{8,9},{9,8},{10,11... | collective-permute-start | bytes 12296 | tf_op jit(solution)/shard_map/ppermute | solution.py:784
  26.5 3.7 %collective-permute-start.5 = (f32[8,128]{1,0:T(8,128)S(1)}, f32[8,128]{1,0:T(8,128)S(1)}, u32[]{:S(2)}, u32[]{:S(2)}) collective-permute-start(f32[8,128]{1,0:T(8,128)S(1)} %add.10.own_ref), channel_id=1, source_target_pairs={{0,2},{2,0},{4,6},{6,4},{8,10},{10,8},{12,14},{14,12},{16,18},{18,... | collective-permute-start | bytes 12296 | tf_op jit(solution)/shard_map/ppermute | solution.py:787
  26.5 7.9 %collective-permute-start.4 = (f32[8,128]{1,0:T(8,128)S(1)}, f32[8,128]{1,0:T(8,128)S(1)}, u32[]{:S(2)}, u32[]{:S(2)}) collective-permute-start(f32[8,128]{1,0:T(8,128)S(1)} %add.10.own_ref), channel_id=1, source_target_pairs={{2,4},{6,8},{10,12},{14,16},{18,20},{22,24},{26,28},{30,32},{34,36... | collective-permute-start | bytes 12296 | tf_op jit(solution)/shard_map/ppermute | solution.py:786
  34.8 5.1 %collective-permute-start.6 = (f32[8,128]{1,0:T(8,128)S(1)}, f32[8,128]{1,0:T(8,128)S(1)}, u32[]{:S(2)}, u32[]{:S(2)}) collective-permute-start(f32[8,128]{1,0:T(8,128)S(1)} %outer_round.4), channel_id=1, source_target_pairs={{0,1},{1,0},{2,3},{3,2},{4,5},{5,4},{6,7},{7,6},{8,9},{9,8},{10,11... | collective-permute-start | bytes 12296 | tf_op jit(solution)/shard_map/ppermute | solution.py:784
  40.0 2.6 %collective-permute-start.8 = (f32[8,128]{1,0:T(8,128)S(1)}, f32[8,128]{1,0:T(8,128)S(1)}, u32[]{:S(2)}, u32[]{:S(2)}) collective-permute-start(f32[8,128]{1,0:T(8,128)S(1)} %add.11.own_ref), channel_id=1, source_target_pairs={{0,2},{2,0},{4,6},{6,4},{8,10},{10,8},{12,14},{14,12},{16,18},{18,... | collective-permute-start | bytes 12296 | tf_op jit(solution)/shard_map/ppermute | solution.py:787
  40.0 7.9 %collective-permute-start.7 = (f32[8,128]{1,0:T(8,128)S(1)}, f32[8,128]{1,0:T(8,128)S(1)}, u32[]{:S(2)}, u32[]{:S(2)}) collective-permute-start(f32[8,128]{1,0:T(8,128)S(1)} %add.11.own_ref), channel_id=1, source_target_pairs={{2,4},{6,8},{10,12},{14,16},{18,20},{22,24},{26,28},{30,32},{34,36... | collective-permute-start | bytes 12296 | tf_op jit(solution)/shard_map/ppermute | solution.py:786
  48.3 5.1 %collective-permute-start.9 = (f32[8,128]{1,0:T(8,128)S(1)}, f32[8,128]{1,0:T(8,128)S(1)}, u32[]{:S(2)}, u32[]{:S(2)}) collective-permute-start(f32[8,128]{1,0:T(8,128)S(1)} %outer_round.5), channel_id=1, source_target_pairs={{0,1},{1,0},{2,3},{3,2},{4,5},{5,4},{6,7},{7,6},{8,9},{9,8},{10,11... | collective-permute-start | bytes 12296 | tf_op jit(solution)/shard_map/ppermute | solution.py:784
  53.4 8.0 %collective-permute-start.11 = (f32[8,128]{1,0:T(8,128)S(1)}, f32[8,128]{1,0:T(8,128)S(1)}, u32[]{:S(2)}, u32[]{:S(2)}) collective-permute-start(f32[8,128]{1,0:T(8,128)S(1)} %add.12.after.own_ref), channel_id=1, source_target_pairs={{2,4},{6,8},{10,12},{14,16},{18,20},{22,24},{26,28},{30,32},{34,36... | collective-permute-start | bytes 12296 | tf_op jit(solution)/shard_map/ppermute | solution.py:786
  55.8 5.6 %collective-permute-start.10 = (f32[8,128]{1,0:T(8,128)S(1)}, f32[8,128]{1,0:T(8,128)S(1)}, u32[]{:S(2)}, u32[]{:S(2)}) collective-permute-start(f32[8,128]{1,0:T(8,128)S(1)} %add.12.after.own_ref), channel_id=1, source_target_pairs={{0,2},{2,0},{4,6},{6,4},{8,10},{10,8},{12,14},{14,12},{16,18},{18,... | collective-permute-start | bytes 12296 | tf_op jit(solution)/shard_map/ppermute | solution.py:787
  63.2 13.6 %copy-start.2 = (f32[512,128]{1,0:T(8,128)S(1)}, f32[512,128]{1,0:T(8,128)}, u32[]{:S(2)}) copy-start(f32[512,128]{1,0:T(8,128)} %probes_ref.1) | copy-start | bytes 786436
  63.2 13.5 %copy-start.3 = (f32[4,4]{1,0:T(4,128)S(1)}, f32[4,4]{1,0:T(4,128)}, u32[]{:S(2)}) copy-start(f32[4,4]{1,0:T(4,128)} %gate.1) | copy-start | bytes 196
  63.2 6.8 %collective-permute-start.12 = (f32[264,128]{1,0:T(8,128)S(1)}, f32[264,128]{1,0:T(8,128)S(1)}, u32[]{:S(2)}, u32[]{:S(2)}) collective-permute-start(f32[264,128]{1,0:T(8,128)S(1)} %gram_to_send.1.after), channel_id=1, source_target_pairs={{0,1},{1,0},{2,3},{3,2},{4,5},{5,4},{6,7},{7,6},{8,9},{9,8},{10,11... | collective-permute-start | bytes 405512 | tf_op jit(solution)/shard_map/ppermute | solution.py:790
  75.1 1.6 %collective-permute-start.13 = (f32[256,256]{1,0:T(8,128)S(1)}, f32[256,256]{1,0:T(8,128)S(1)}, u32[]{:S(2)}, u32[]{:S(2)}) collective-permute-start(f32[256,256]{1,0:T(8,128)S(1)} %get-tuple-element.34.upper_ref), channel_id=1, source_target_pairs={{0,2},{2,0},{4,6},{6,4},{8,10},{10,8},{12,14},{14,12},{16,18},{18,... | collective-permute-start | bytes 786440 | tf_op jit(solution)/shard_map/ppermute | solution.py:793
  81.1 7.3 %collective-permute-start.14 = (bf16[272,256]{1,0:T(8,128)(2,1)S(1)}, bf16[272,256]{1,0:T(8,128)(2,1)S(1)}, u32[]{:S(2)}, u32[]{:S(2)}) collective-permute-start(bf16[272,256]{1,0:T(8,128)(2,1)S(1)} %truncate.1.pack_ref.after), channel_id=1, source_target_pairs={{0,1},{1,0},{2,3},{3,2},{4,5},{5,4},{6,7},{7,6},{8,9},{9,8},{10,11... | collective-permute-start | bytes 417800 | tf_op jit(solution)/shard_map/ppermute | solution.py:795

commit v6 on v5

--- a/solution.py
+++ b/solution.py
@@ -684,22 +684,18 @@
     steps = rows // block
 
     def put(step):
-        slot = lax.rem(step, slots)
+        slot = step % slots
         target = out_hbm.at[member, pl.ds(step * block, block)]
         return pltpu.make_async_copy(held.at[slot], target, sems.at[slot])
 
-    def body(step, carry):
-        start = step * block
-        slot = lax.rem(step, slots)
-
-        @pl.when(step >= slots)
-        def free():
-            put(step).wait()
-
-        change = pack_ref[:wide]
+    change = pack_ref[:wide]
+    for step in range(steps):
+        slot = step % slots
+        if step >= slots:
+            put(step - slots).wait()
         for index in range(block):
             if index % 4 == 0:
-                rows_in = d_ref[member, pl.ds(start + index, 4)].reshape(4 * bond, wide)
+                rows_in = d_ref[member, pl.ds(step * block + index, 4)].reshape(4 * bond, wide)
                 result = dot_of(rows_in, change)
             lane = scratch.at[index % scratch.shape[0]]
             piece = result[index % 4 * bond : (index % 4 + 1) * bond]
@@ -707,9 +703,6 @@
             lane[pl.ds(1, bond, 2), :] = piece[:, bond:]
             held[slot, index] = lane[...].astype(BF16)
         put(step).start()
-        return carry
-
-    lax.fori_loop(0, steps, body, 0)
     for step in range(steps - slots, steps):
         put(step).wait()
 
@@ -735,7 +728,7 @@
 
 def update_call(kernel, name, in_specs, aliases, with_bonds, flat, operands):
     members, rows, bond, wide = flat.shape
-    block, slots = (16, 4)
+    block, slots = (8, 8)
     tensor = jax.ShapeDtypeStruct((members, rows, wide, bond), BF16)
     bonds = jax.ShapeDtypeStruct((members, bond), F32)
     return pl.pallas_call(

time: 92.1 us -> 91.5 us (level)
  Pallas kernels: 38 us -> 36.7 us
    pallas_call x2, Pallas kernels: 6.71 us -> 5.42 us  [update_call(): pl.pallas_call(kernel, in_specs=in_specs, out_specs=[hbm(), hbm()] if wit...]
where the time goes in v6:
time: 91.5 us; the launch traced here: 91.3 us
  Pallas kernels  36.7 us (40%)
  starting transfers between devices  34.3 us (37%)
  waiting for transfers between devices  19.2 us (21%)
  between operations  0.97 us (1%)
    ppermute x4, starting transfers between devices, shards(): side = lax.ppermute(own, 'site', side_swap)  15.9 us
    ppermute x4, starting transfers between devices, shards(): got = lax.ppermute(part, 'row', row_swap)  12 us
    pallas_call x3, Pallas kernels, inner_call(): pl.pallas_call(inner_kernel, in_specs=[vmem(), vmem(), vmem(), vmem()], o...  9.45 us
    ppermute x4, waiting for transfers between devices, shards(): got = lax.ppermute(part, 'row', row_swap)  7.91 us
    ppermute x4, waiting for transfers between devices, shards(): side = lax.ppermute(own, 'site', side_swap)  6.42 us
    pallas_call x2, Pallas kernels, update_call(): pl.pallas_call(kernel, in_specs=in_specs, out_specs=[hbm(), hbm()] if wit...  5.42 us
    pallas_call x1, Pallas kernels, root_call(): pl.pallas_call(root_kernel, in_specs=[vmem(), vmem()], out_specs=[vmem(),...  5.13 us
    pallas_call x1, Pallas kernels, open_call(): pl.pallas_call(open_kernel, in_specs=[hbm()], out_specs=[vmem(), vmem(),...  4.63 us
  transfers between devices with their start and end apart: 15, of which 10 were waited for; matrix products, arithmetic and copies ran while one was open for 0% of the time, Pallas kernels for 19%

profile of v6, /device:TPU:6, one launch (start us, length us, event | category | flops | bytes accessed | tf_op | source)
XLA Modules:
  0.0 91.3 jit_solution(16551511265136480392)
XLA Ops:
  0.7 4.6 %open.1 = (bf16[2,64,256,128]{3,2,1,0:T(8,128)(2,1)S(1)}, bf16[2,64,128,128]{3,2,1,0:T(8,128)(2,1)S(1)}, f32[8,128]{1,0:T(8,128)S(1)}) custom-call(bf16[2,64,256,128]{3,2,1,0:T(8,128)(2,1)} %bitcast.6), custom_call_target="tpu_custom_call" | custom-call | flops 16777216 | bytes 20971520 | tf_op jit(solution)/shard_map/open/pallas_call | solution.py:214
  5.3 3.3 %collective-permute-start = (f32[8,128]{1,0:T(8,128)S(1)}, f32[8,128]{1,0:T(8,128)S(1)}, u32[]{:S(2)}, u32[]{:S(2)}) collective-permute-start(f32[8,128]{1,0:T(8,128)S(1)} %get-tuple-element.21.after.one_ref), channel_id=1, source_target_pairs={{0,1},{1,0},{2,3},{3,2},{4,5},{5,4},{6,7},{7,6},{8,9},{9,8},{10,11... | collective-permute-start | bytes 12296 | tf_op jit(solution)/shard_map/ppermute | solution.py:777
  8.6 0.6 scalars.1.after.info
  9.2 1.3 %collective-permute-done.two_ref = f32[8,128]{1,0:T(8,128)S(1)} collective-permute-done((f32[8,128]{1,0:T(8,128)S(1)}, f32[8,128]{1,0:T(8,128)S(1)}, u32[]{:S(2)}, u32[]{:S(2)}) %collective-permute-start) | collective-permute-done | bytes 4128 | tf_op jit(solution)/shard_map/ppermute | solution.py:777
  10.5 7.3 %collective-permute-start.1 = (f32[8,128]{1,0:T(8,128)S(1)}, f32[8,128]{1,0:T(8,128)S(1)}, u32[]{:S(2)}, u32[]{:S(2)}) collective-permute-start(f32[8,128]{1,0:T(8,128)S(1)} %add.13.own_ref), channel_id=1, source_target_pairs={{2,4},{6,8},{10,12},{14,16},{18,20},{22,24},{26,28},{30,32},{34,36... | collective-permute-start | bytes 12296 | tf_op jit(solution)/shard_map/ppermute | solution.py:779
  17.8 3.1 %inner_round.3 = (f32[8,128]{1,0:T(8,128)S(1)}, f32[64,128]{1,0:T(8,128)S(1)}, f32[128,128]{1,0:T(8,128)S(1)}) custom-call(s32[8,128]{1,0:T(8,128)S(1)} %scalars.1.after.info, f32[8,128]{1,0:T(8,128)S(1)} %add.13.own_ref, f32[8,128]{1,0:T(8,128)S(1)} %collective-permute-done.2.mate_ref, bf16[2,64,128,128]{3,2,1,0:T(8,128)(2,1)S(1)} %get-tuple-element.22.s_ref), custom_call_target="tpu_custom_call" | custom-call | flops 8388608 | bytes 4194304 | tf_op jit(solution)/shard_map/inner_round/pallas_call | solution.py:405
  21.4 2.9 %collective-permute-start.3 = (f32[8,128]{1,0:T(8,128)S(1)}, f32[8,128]{1,0:T(8,128)S(1)}, u32[]{:S(2)}, u32[]{:S(2)}) collective-permute-start(f32[8,128]{1,0:T(8,128)S(1)} %outer_round.3), channel_id=1, source_target_pairs={{0,1},{1,0},{2,3},{3,2},{4,5},{5,4},{6,7},{7,6},{8,9},{9,8},{10,11... | collective-permute-start | bytes 12296 | tf_op jit(solution)/shard_map/ppermute | solution.py:777
  24.3 2.2 %collective-permute-done.3 = f32[8,128]{1,0:T(8,128)S(1)} collective-permute-done((f32[8,128]{1,0:T(8,128)S(1)}, f32[8,128]{1,0:T(8,128)S(1)}, u32[]{:S(2)}, u32[]{:S(2)}) %collective-permute-start.3) | collective-permute-done | bytes 4128 | tf_op jit(solution)/shard_map/ppermute | solution.py:777
  26.5 3.7 %collective-permute-start.4 = (f32[8,128]{1,0:T(8,128)S(1)}, f32[8,128]{1,0:T(8,128)S(1)}, u32[]{:S(2)}, u32[]{:S(2)}) collective-permute-start(f32[8,128]{1,0:T(8,128)S(1)} %add.10.own_ref), channel_id=1, source_target_pairs={{2,4},{6,8},{10,12},{14,16},{18,20},{22,24},{26,28},{30,32},{34,36... | collective-permute-start | bytes 12296 | tf_op jit(solution)/shard_map/ppermute | solution.py:779
  30.2 3.1 %inner_round.4 = (f32[8,128]{1,0:T(8,128)S(1)}, f32[64,128]{1,0:T(8,128)S(1)}, f32[128,128]{1,0:T(8,128)S(1)}) custom-call(s32[8,128]{1,0:T(8,128)S(1)} %scalars.1.after.info, f32[8,128]{1,0:T(8,128)S(1)} %add.10.own_ref, f32[8,128]{1,0:T(8,128)S(1)} %collective-permute-done.5.mate_ref, bf16[2,64,128,128]{3,2,1,0:T(8,128)(2,1)S(1)} %get-tuple-element.22.s_ref), custom_call_target="tpu_custom_call" | custom-call | flops 8388608 | bytes 4194304 | tf_op jit(solution)/shard_map/inner_round/pallas_call | solution.py:405
  33.3 1.1 %collective-permute-done.4.side_ref = f32[8,128]{1,0:T(8,128)S(1)} collective-permute-done((f32[8,128]{1,0:T(8,128)S(1)}, f32[8,128]{1,0:T(8,128)S(1)}, u32[]{:S(2)}, u32[]{:S(2)}) %collective-permute-start.4) | collective-permute-done | bytes 4128 | tf_op jit(solution)/shard_map/ppermute | solution.py:779
  34.8 2.9 %collective-permute-start.6 = (f32[8,128]{1,0:T(8,128)S(1)}, f32[8,128]{1,0:T(8,128)S(1)}, u32[]{:S(2)}, u32[]{:S(2)}) collective-permute-start(f32[8,128]{1,0:T(8,128)S(1)} %outer_round.4), channel_id=1, source_target_pairs={{0,1},{1,0},{2,3},{3,2},{4,5},{5,4},{6,7},{7,6},{8,9},{9,8},{10,11... | collective-permute-start | bytes 12296 | tf_op jit(solution)/shard_map/ppermute | solution.py:777
  37.7 2.2 %collective-permute-done.6 = f32[8,128]{1,0:T(8,128)S(1)} collective-permute-done((f32[8,128]{1,0:T(8,128)S(1)}, f32[8,128]{1,0:T(8,128)S(1)}, u32[]{:S(2)}, u32[]{:S(2)}) %collective-permute-start.6) | collective-permute-done | bytes 4128 | tf_op jit(solution)/shard_map/ppermute | solution.py:777
  40.0 2.6 %collective-permute-start.7 = (f32[8,128]{1,0:T(8,128)S(1)}, f32[8,128]{1,0:T(8,128)S(1)}, u32[]{:S(2)}, u32[]{:S(2)}) collective-permute-start(f32[8,128]{1,0:T(8,128)S(1)} %add.11.own_ref), channel_id=1, source_target_pairs={{2,4},{6,8},{10,12},{14,16},{18,20},{22,24},{26,28},{30,32},{34,36... | collective-permute-start | bytes 12296 | tf_op jit(solution)/shard_map/ppermute | solution.py:779
  42.5 3.1 %inner_round.5 = (f32[8,128]{1,0:T(8,128)S(1)}, f32[64,128]{1,0:T(8,128)S(1)}, f32[128,128]{1,0:T(8,128)S(1)}) custom-call(s32[8,128]{1,0:T(8,128)S(1)} %scalars.1.after.info, f32[8,128]{1,0:T(8,128)S(1)} %add.11.own_ref, f32[8,128]{1,0:T(8,128)S(1)} %collective-permute-done.8.mate_ref, bf16[2,64,128,128]{3,2,1,0:T(8,128)(2,1)S(1)} %get-tuple-element.22.s_ref), custom_call_target="tpu_custom_call" | custom-call | flops 8388608 | bytes 4194304 | tf_op jit(solution)/shard_map/inner_round/pallas_call | solution.py:405
  45.7 2.2 %collective-permute-done.7.side_ref = f32[8,128]{1,0:T(8,128)S(1)} collective-permute-done((f32[8,128]{1,0:T(8,128)S(1)}, f32[8,128]{1,0:T(8,128)S(1)}, u32[]{:S(2)}, u32[]{:S(2)}) %collective-permute-start.7) | collective-permute-done | bytes 4128 | tf_op jit(solution)/shard_map/ppermute | solution.py:779
  48.3 2.9 %collective-permute-start.9 = (f32[8,128]{1,0:T(8,128)S(1)}, f32[8,128]{1,0:T(8,128)S(1)}, u32[]{:S(2)}, u32[]{:S(2)}) collective-permute-start(f32[8,128]{1,0:T(8,128)S(1)} %outer_round.5), channel_id=1, source_target_pairs={{0,1},{1,0},{2,3},{3,2},{4,5},{5,4},{6,7},{7,6},{8,9},{9,8},{10,11... | collective-permute-start | bytes 12296 | tf_op jit(solution)/shard_map/ppermute | solution.py:777
  51.2 2.2 %collective-permute-done.9 = f32[8,128]{1,0:T(8,128)S(1)} collective-permute-done((f32[8,128]{1,0:T(8,128)S(1)}, f32[8,128]{1,0:T(8,128)S(1)}, u32[]{:S(2)}, u32[]{:S(2)}) %collective-permute-start.9) | collective-permute-done | bytes 4128 | tf_op jit(solution)/shard_map/ppermute | solution.py:777
  53.4 2.4 %collective-permute-start.11 = (f32[8,128]{1,0:T(8,128)S(1)}, f32[8,128]{1,0:T(8,128)S(1)}, u32[]{:S(2)}, u32[]{:S(2)}) collective-permute-start(f32[8,128]{1,0:T(8,128)S(1)} %add.12.after.own_ref), channel_id=1, source_target_pairs={{2,4},{6,8},{10,12},{14,16},{18,20},{22,24},{26,28},{30,32},{34,36... | collective-permute-start | bytes 12296 | tf_op jit(solution)/shard_map/ppermute | solution.py:779
  55.9 2.4 %flatten.1.d_ref = bf16[2,64,128,256]{3,2,1,0:T(8,128)(2,1)S(1)} custom-call(f32[8,128]{1,0:T(8,128)S(1)} %add.12.after.own_ref, bf16[2,64,256,128]{3,2,1,0:T(8,128)(2,1)S(1)} %get-tuple-element.32.x_ref), custom_call_target="tpu_custom_call" | custom-call | flops 8388608 | bytes 16777216 | tf_op jit(solution)/shard_map/flatten/pallas_call | solution.py:251
  58.3 3.1 %collective-permute-done.11.side_ref = f32[8,128]{1,0:T(8,128)S(1)} collective-permute-done((f32[8,128]{1,0:T(8,128)S(1)}, f32[8,128]{1,0:T(8,128)S(1)}, u32[]{:S(2)}, u32[]{:S(2)}) %collective-permute-start.11) | collective-permute-done | bytes 4128 | tf_op jit(solution)/shard_map/ppermute | solution.py:779
  61.4 1.8 %gram_to_send.1.after = f32[264,128]{1,0:T(8,128)S(1)} custom-call(s32[8,128]{1,0:T(8,128)S(1)} %scalars.1.after.info, f32[8,128]{1,0:T(8,128)S(1)} %add.12.after.own_ref, f32[8,128]{1,0:T(8,128)S(1)} %collective-permute-done.10.mate_ref, f32[8,128]{1,0:T(8,128)S(1)} %collective-permute-done.11.side_ref, bf16[2,64,128,256]{3,2,1,0:T(8,128)(2,1)S(1)} %flatten.1.d_ref), custom_call_target="tpu_custom_call" | custom-call | flops 1073741824 | bytes 4194304 | tf_op jit(solution)/shard_map/gram_to_send/pallas_call | solution.py:490
  63.2 3.2 %collective-permute-start.12 = (f32[264,128]{1,0:T(8,128)S(1)}, f32[264,128]{1,0:T(8,128)S(1)}, u32[]{:S(2)}, u32[]{:S(2)}) collective-permute-start(f32[264,128]{1,0:T(8,128)S(1)} %gram_to_send.1.after), channel_id=1, source_target_pairs={{0,1},{1,0},{2,3},{3,2},{4,5},{5,4},{6,7},{7,6},{8,9},{9,8},{10,11... | collective-permute-start | bytes 405512 | tf_op jit(solution)/shard_map/ppermute | solution.py:783
  66.4 1.8 %gram_to_keep.1 = (f32[3,128,128]{2,1,0:T(8,128)S(1)}, f32[3,2,128]{2,1,0:T(2,128)}) custom-call(s32[8,128]{1,0:T(8,128)S(1)} %scalars.1.after.info, f32[8,128]{1,0:T(8,128)S(1)} %add.12.after.own_ref, f32[8,128]{1,0:T(8,128)S(1)} %collective-permute-done.10.mate_ref, f32[8,128]{1,0:T(8,128)S(1)} %collective-permute-done.11.side_ref, ...), custom_call_target="tpu_custom_call" | custom-call | flops 1073741824 | bytes 4194304 | tf_op jit(solution)/shard_map/gram_to_keep/pallas_call | solution.py:490
  68.2 1.8 %collective-permute-done.12.got_ref = f32[264,128]{1,0:T(8,128)S(1)} collective-permute-done((f32[264,128]{1,0:T(8,128)S(1)}, f32[264,128]{1,0:T(8,128)S(1)}, u32[]{:S(2)}, u32[]{:S(2)}) %collective-permute-start.12) | collective-permute-done | bytes 135200 | tf_op jit(solution)/shard_map/ppermute | solution.py:783
  70.0 5.1 %root.1 = (f32[256,256]{1,0:T(8,128)S(1)}, f32[256,256]{1,0:T(8,128)S(1)}) custom-call(f32[3,128,128]{2,1,0:T(8,128)S(1)} %get-tuple-element.33.keep_ref, f32[264,128]{1,0:T(8,128)S(1)} %collective-permute-done.12.got_ref), custom_call_target="tpu_custom_call" | custom-call | flops 2214592512 | bytes 1048576 | tf_op jit(solution)/shard_map/root/pallas_call | solution.py:579
  75.2 1.5 %collective-permute-done.13.other_ref = f32[256,256]{1,0:T(8,128)S(1)} collective-permute-done((f32[256,256]{1,0:T(8,128)S(1)}, f32[256,256]{1,0:T(8,128)S(1)}, u32[]{:S(2)}, u32[]{:S(2)}) %collective-permute-start.13) | collective-permute-done | bytes 262176 | tf_op jit(solution)/shard_map/ppermute | solution.py:786
  76.8 4.3 %truncate.1.pack_ref.after = bf16[272,256]{1,0:T(8,128)(2,1)S(1)} custom-call(s32[8,128]{1,0:T(8,128)S(1)} %scalars.1.after.info, f32[4,4]{1,0:T(4,128)S(1)} %copy-done.3, f32[8,128]{1,0:T(8,128)S(1)} %add.12.after.own_ref, f32[8,128]{1,0:T(8,128)S(1)} %collective-permute-done.10.mate_ref, f32[256,256]{1,0:T(8,128)S(1)} %get-tuple-element.34.upper_ref, ...), custom_call_target="tpu_custom_call" | custom-call | flops 1342177280 | bytes 1572864 | tf_op jit(solution)/shard_map/truncate/pallas_call | solution.py:670
  81.1 3.0 %collective-permute-start.14 = (bf16[272,256]{1,0:T(8,128)(2,1)S(1)}, bf16[272,256]{1,0:T(8,128)(2,1)S(1)}, u32[]{:S(2)}, u32[]{:S(2)}) collective-permute-start(bf16[272,256]{1,0:T(8,128)(2,1)S(1)} %truncate.1.pack_ref.after), channel_id=1, source_target_pairs={{0,1},{1,0},{2,3},{3,2},{4,5},{5,4},{6,7},{7,6},{8,9},{9,8},{10,11... | collective-permute-start | bytes 417800 | tf_op jit(solution)/shard_map/ppermute | solution.py:788
  84.1 2.7 %update_own.1.begun_hbm = bf16[2,64,256,128]{3,2,1,0:T(8,128)(2,1)} custom-call(s32[8,128]{1,0:T(8,128)S(1)} %scalars.1.after.info, bf16[272,256]{1,0:T(8,128)(2,1)S(1)} %truncate.1.pack_ref.after, bf16[2,64,128,256]{3,2,1,0:T(8,128)(2,1)S(1)} %flatten.1.d_ref, bf16[272,256]{1,0:T(8,128)(2,1)S(1)} %truncate.1.pack_ref.after), custom_call_target="tpu_custom_call" | custom-call | flops 1073741824 | bytes 8388608 | tf_op jit(solution)/shard_map/update_own/pallas_call | solution.py:734
  86.8 1.6 %collective-permute-done.14.got_ref = bf16[272,256]{1,0:T(8,128)(2,1)S(1)} collective-permute-done((bf16[272,256]{1,0:T(8,128)(2,1)S(1)}, bf16[272,256]{1,0:T(8,128)(2,1)S(1)}, u32[]{:S(2)}, u32[]{:S(2)}) %collective-permute-start.14) | collective-permute-done | bytes 139296 | tf_op jit(solution)/shard_map/ppermute | solution.py:788
  88.4 2.7 %update_other.1 = (bf16[2,64,256,128]{3,2,1,0:T(8,128)(2,1)}, f32[2,128]{1,0:T(2,128)}) custom-call(s32[8,128]{1,0:T(8,128)S(1)} %scalars.1.after.info, bf16[272,256]{1,0:T(8,128)(2,1)S(1)} %truncate.1.pack_ref.after, bf16[272,256]{1,0:T(8,128)(2,1)S(1)} %collective-permute-done.14.got_ref, ...), custom_call_target="tpu_custom_call", output_to_operand_aliasing={{0}: (4, {})} | custom-call | flops 1073741824 | bytes 8388608 | tf_op jit(solution)/shard_map/update_other/pallas_call | solution.py:734
  (25 shorter events, 1.4 us)
Async XLA Ops:
  0.6 7.9 %copy-start.1 = (s32[128]{0:T(128)S(1)}, s32[128]{0:T(128)}, u32[]{:S(2)}) copy-start(s32[128]{0:T(128)} %ranks.1) | copy-start | bytes 1540
  0.6 7.9 %copy-start = (s32[128,3]{0,1:T(4,128)S(1)}, s32[128,3]{0,1:T(4,128)}, u32[]{:S(2)}) copy-start(s32[128,3]{0,1:T(4,128)} %param.6) | copy-start | bytes 4612
  5.3 5.2 %collective-permute-start = (f32[8,128]{1,0:T(8,128)S(1)}, f32[8,128]{1,0:T(8,128)S(1)}, u32[]{:S(2)}, u32[]{:S(2)}) collective-permute-start(f32[8,128]{1,0:T(8,128)S(1)} %get-tuple-element.21.after.one_ref), channel_id=1, source_target_pairs={{0,1},{1,0},{2,3},{3,2},{4,5},{5,4},{6,7},{7,6},{8,9},{9,8},{10,11... | collective-permute-start | bytes 12296 | tf_op jit(solution)/shard_map/ppermute | solution.py:777
  10.5 7.3 %collective-permute-start.2 = (f32[8,128]{1,0:T(8,128)S(1)}, f32[8,128]{1,0:T(8,128)S(1)}, u32[]{:S(2)}, u32[]{:S(2)}) collective-permute-start(f32[8,128]{1,0:T(8,128)S(1)} %add.13.own_ref), channel_id=1, source_target_pairs={{0,2},{2,0},{4,6},{6,4},{8,10},{10,8},{12,14},{14,12},{16,18},{18,... | collective-permute-start | bytes 12296 | tf_op jit(solution)/shard_map/ppermute | solution.py:780
  10.5 10.5 %collective-permute-start.1 = (f32[8,128]{1,0:T(8,128)S(1)}, f32[8,128]{1,0:T(8,128)S(1)}, u32[]{:S(2)}, u32[]{:S(2)}) collective-permute-start(f32[8,128]{1,0:T(8,128)S(1)} %add.13.own_ref), channel_id=1, source_target_pairs={{2,4},{6,8},{10,12},{14,16},{18,20},{22,24},{26,28},{30,32},{34,36... | collective-permute-start | bytes 12296 | tf_op jit(solution)/shard_map/ppermute | solution.py:779
  21.4 5.1 %collective-permute-start.3 = (f32[8,128]{1,0:T(8,128)S(1)}, f32[8,128]{1,0:T(8,128)S(1)}, u32[]{:S(2)}, u32[]{:S(2)}) collective-permute-start(f32[8,128]{1,0:T(8,128)S(1)} %outer_round.3), channel_id=1, source_target_pairs={{0,1},{1,0},{2,3},{3,2},{4,5},{5,4},{6,7},{7,6},{8,9},{9,8},{10,11... | collective-permute-start | bytes 12296 | tf_op jit(solution)/shard_map/ppermute | solution.py:777
  26.5 3.7 %collective-permute-start.5 = (f32[8,128]{1,0:T(8,128)S(1)}, f32[8,128]{1,0:T(8,128)S(1)}, u32[]{:S(2)}, u32[]{:S(2)}) collective-permute-start(f32[8,128]{1,0:T(8,128)S(1)} %add.10.own_ref), channel_id=1, source_target_pairs={{0,2},{2,0},{4,6},{6,4},{8,10},{10,8},{12,14},{14,12},{16,18},{18,... | collective-permute-start | bytes 12296 | tf_op jit(solution)/shard_map/ppermute | solution.py:780
  26.5 7.9 %collective-permute-start.4 = (f32[8,128]{1,0:T(8,128)S(1)}, f32[8,128]{1,0:T(8,128)S(1)}, u32[]{:S(2)}, u32[]{:S(2)}) collective-permute-start(f32[8,128]{1,0:T(8,128)S(1)} %add.10.own_ref), channel_id=1, source_target_pairs={{2,4},{6,8},{10,12},{14,16},{18,20},{22,24},{26,28},{30,32},{34,36... | collective-permute-start | bytes 12296 | tf_op jit(solution)/shard_map/ppermute | solution.py:779
  34.8 5.1 %collective-permute-start.6 = (f32[8,128]{1,0:T(8,128)S(1)}, f32[8,128]{1,0:T(8,128)S(1)}, u32[]{:S(2)}, u32[]{:S(2)}) collective-permute-start(f32[8,128]{1,0:T(8,128)S(1)} %outer_round.4), channel_id=1, source_target_pairs={{0,1},{1,0},{2,3},{3,2},{4,5},{5,4},{6,7},{7,6},{8,9},{9,8},{10,11... | collective-permute-start | bytes 12296 | tf_op jit(solution)/shard_map/ppermute | solution.py:777
  40.0 2.6 %collective-permute-start.8 = (f32[8,128]{1,0:T(8,128)S(1)}, f32[8,128]{1,0:T(8,128)S(1)}, u32[]{:S(2)}, u32[]{:S(2)}) collective-permute-start(f32[8,128]{1,0:T(8,128)S(1)} %add.11.own_ref), channel_id=1, source_target_pairs={{0,2},{2,0},{4,6},{6,4},{8,10},{10,8},{12,14},{14,12},{16,18},{18,... | collective-permute-start | bytes 12296 | tf_op jit(solution)/shard_map/ppermute | solution.py:780
  40.0 7.9 %collective-permute-start.7 = (f32[8,128]{1,0:T(8,128)S(1)}, f32[8,128]{1,0:T(8,128)S(1)}, u32[]{:S(2)}, u32[]{:S(2)}) collective-permute-start(f32[8,128]{1,0:T(8,128)S(1)} %add.11.own_ref), channel_id=1, source_target_pairs={{2,4},{6,8},{10,12},{14,16},{18,20},{22,24},{26,28},{30,32},{34,36... | collective-permute-start | bytes 12296 | tf_op jit(solution)/shard_map/ppermute | solution.py:779
  48.3 5.1 %collective-permute-start.9 = (f32[8,128]{1,0:T(8,128)S(1)}, f32[8,128]{1,0:T(8,128)S(1)}, u32[]{:S(2)}, u32[]{:S(2)}) collective-permute-start(f32[8,128]{1,0:T(8,128)S(1)} %outer_round.5), channel_id=1, source_target_pairs={{0,1},{1,0},{2,3},{3,2},{4,5},{5,4},{6,7},{7,6},{8,9},{9,8},{10,11... | collective-permute-start | bytes 12296 | tf_op jit(solution)/shard_map/ppermute | solution.py:777
  53.4 8.0 %collective-permute-start.11 = (f32[8,128]{1,0:T(8,128)S(1)}, f32[8,128]{1,0:T(8,128)S(1)}, u32[]{:S(2)}, u32[]{:S(2)}) collective-permute-start(f32[8,128]{1,0:T(8,128)S(1)} %add.12.after.own_ref), channel_id=1, source_target_pairs={{2,4},{6,8},{10,12},{14,16},{18,20},{22,24},{26,28},{30,32},{34,36... | collective-permute-start | bytes 12296 | tf_op jit(solution)/shard_map/ppermute | solution.py:779
  55.8 5.6 %collective-permute-start.10 = (f32[8,128]{1,0:T(8,128)S(1)}, f32[8,128]{1,0:T(8,128)S(1)}, u32[]{:S(2)}, u32[]{:S(2)}) collective-permute-start(f32[8,128]{1,0:T(8,128)S(1)} %add.12.after.own_ref), channel_id=1, source_target_pairs={{0,2},{2,0},{4,6},{6,4},{8,10},{10,8},{12,14},{14,12},{16,18},{18,... | collective-permute-start | bytes 12296 | tf_op jit(solution)/shard_map/ppermute | solution.py:780
  63.2 13.6 %copy-start.2 = (f32[512,128]{1,0:T(8,128)S(1)}, f32[512,128]{1,0:T(8,128)}, u32[]{:S(2)}) copy-start(f32[512,128]{1,0:T(8,128)} %probes_ref.1) | copy-start | bytes 786436
  63.2 13.5 %copy-start.3 = (f32[4,4]{1,0:T(4,128)S(1)}, f32[4,4]{1,0:T(4,128)}, u32[]{:S(2)}) copy-start(f32[4,4]{1,0:T(4,128)} %gate.1) | copy-start | bytes 196
  63.2 6.8 %collective-permute-start.12 = (f32[264,128]{1,0:T(8,128)S(1)}, f32[264,128]{1,0:T(8,128)S(1)}, u32[]{:S(2)}, u32[]{:S(2)}) collective-permute-start(f32[264,128]{1,0:T(8,128)S(1)} %gram_to_send.1.after), channel_id=1, source_target_pairs={{0,1},{1,0},{2,3},{3,2},{4,5},{5,4},{6,7},{7,6},{8,9},{9,8},{10,11... | collective-permute-start | bytes 405512 | tf_op jit(solution)/shard_map/ppermute | solution.py:783
  75.1 1.6 %collective-permute-start.13 = (f32[256,256]{1,0:T(8,128)S(1)}, f32[256,256]{1,0:T(8,128)S(1)}, u32[]{:S(2)}, u32[]{:S(2)}) collective-permute-start(f32[256,256]{1,0:T(8,128)S(1)} %get-tuple-element.34.upper_ref), channel_id=1, source_target_pairs={{0,2},{2,0},{4,6},{6,4},{8,10},{10,8},{12,14},{14,12},{16,18},{18,... | collective-permute-start | bytes 786440 | tf_op jit(solution)/shard_map/ppermute | solution.py:786
  81.1 7.3 %collective-permute-start.14 = (bf16[272,256]{1,0:T(8,128)(2,1)S(1)}, bf16[272,256]{1,0:T(8,128)(2,1)S(1)}, u32[]{:S(2)}, u32[]{:S(2)}) collective-permute-start(bf16[272,256]{1,0:T(8,128)(2,1)S(1)} %truncate.1.pack_ref.after), channel_id=1, source_target_pairs={{0,1},{1,0},{2,3},{3,2},{4,5},{5,4},{6,7},{7,6},{8,9},{9,8},{10,11... | collective-permute-start | bytes 417800 | tf_op jit(solution)/shard_map/ppermute | solution.py:788

commit v7 on v6

--- a/solution.py
+++ b/solution.py
@@ -169,7 +169,7 @@
     )(one, two, after)
 
 
-def open_kernel(x_hbm, x_ref, s_ref, out_ref, scratch, sums_ref, total_ref, sems):
+def open_kernel(x_hbm, x_ref, s_ref, out_ref, pairs_ref, sums_ref, total_ref, sems):
     members, rows, wide, bond = x_hbm.shape
     steps = sems.shape[0]
     per = steps // members
@@ -182,20 +182,22 @@
     for step in range(steps):
         fetch(step).start()
     total_ref[...] = jnp.zeros(total_ref.shape, F32)
+    down_index = lax.broadcasted_iota(jnp.int32, (bond, wide), 0)
+    across_index = lax.broadcasted_iota(jnp.int32, (bond, wide), 1)
+    pairs_ref[...] = (across_index // 2 == down_index).astype(F32).astype(BF16)
 
     def body(step, carry):
         fetch(step).wait()
         member, start = (step // per, lax.rem(step, per) * block)
         total = total_ref[member]
-        for index in range(block):
-            lane = scratch.at[index % scratch.shape[0]]
-            lane[...] = x_ref[member, start + index].astype(F32)
-            even = lane[pl.ds(0, bond, 2), :]
-            odd = lane[pl.ds(1, bond, 2), :]
-            square = even * even + odd * odd
-            s_ref[member, start + index] = square.astype(BF16)
-            sums_ref[member, start + index] = jnp.sum(square.reshape(bond // 8, 8, bond), axis=0)
-            total = total + square
+        for index in range(0, block, 2):
+            places = [start + index, start + index + 1]
+            both = jnp.concatenate([x_ref[member, place] for place in places], axis=1)
+            both = dot_of(pairs_ref[...], both * both)
+            for place, square in zip(places, (both[:, :bond], both[:, bond:])):
+                s_ref[member, place] = square.astype(BF16)
+                sums_ref[member, place] = jnp.sum(square.reshape(bond // 8, 8, bond), axis=0)
+                total = total + square
         total_ref[member] = total
         return carry
 
@@ -221,7 +223,7 @@
             jax.ShapeDtypeStruct((8, bond), F32),
         ],
         scratch_shapes=[
-            pltpu.VMEM((4, wide, bond), F32),
+            pltpu.VMEM((bond, wide), BF16),
             pltpu.VMEM((members, rows, 8, bond), F32),
             pltpu.VMEM((members, bond, bond), F32),
             pltpu.SemaphoreType.DMA((steps,)),
@@ -396,8 +398,10 @@
     @pl.when(info[0, CORE] == 0)
     def as_first():
         half = halved(info[0, ROW], far)
-        put_leg(out_ref, 0, 1, by_row(half, mixed_ref[...]))
-        put_leg(out_ref, 0, 2, by_row(half, other_ref[:rows]))
+        both = by_row(half, jnp.concatenate([mixed_ref[...], other_ref[:rows]], axis=1))
+        bond = mixed_ref.shape[1]
+        put_leg(out_ref, 0, 1, both[:, :bond])
+        put_leg(out_ref, 0, 2, both[:, bond:])
 
 
 def inner_call(info, own, mate, squares):

time: 91.5 us -> 91.2 us (level)
  no operation moved by 1% of the time
where the time goes in v7:
time: 91.2 us; the launch traced here: 91 us
  Pallas kernels  36.5 us (40%)
  starting transfers between devices  34.3 us (38%)
  waiting for transfers between devices  19.2 us (21%)
  between operations  0.97 us (1%)
    ppermute x4, starting transfers between devices, shards(): side = lax.ppermute(own, 'site', side_swap)  16 us
    ppermute x4, starting transfers between devices, shards(): got = lax.ppermute(part, 'row', row_swap)  12 us
    pallas_call x3, Pallas kernels, inner_call(): pl.pallas_call(inner_kernel, in_specs=[vmem(), vmem(), vmem(), vmem()], o...  9.45 us
    ppermute x4, waiting for transfers between devices, shards(): got = lax.ppermute(part, 'row', row_swap)  7.94 us
    ppermute x4, waiting for transfers between devices, shards(): side = lax.ppermute(own, 'site', side_swap)  6.35 us
    pallas_call x2, Pallas kernels, update_call(): pl.pallas_call(kernel, in_specs=in_specs, out_specs=[hbm(), hbm()] if wit...  5.42 us
    pallas_call x1, Pallas kernels, root_call(): pl.pallas_call(root_kernel, in_specs=[vmem(), vmem()], out_specs=[vmem(),...  5.13 us
    pallas_call x1, Pallas kernels, open_call(): pl.pallas_call(open_kernel, in_specs=[hbm()], out_specs=[vmem(), vmem(),...  4.41 us
  transfers between devices with their start and end apart: 15, of which 10 were waited for; matrix products, arithmetic and copies ran while one was open for 0% of the time, Pallas kernels for 19%

profile of v7, /device:TPU:6, one launch (start us, length us, event | category | flops | bytes accessed | tf_op | source)
XLA Modules:
  0.0 91.0 jit_solution(17040235162058124671)
XLA Ops:
  0.7 4.4 %open.1 = (bf16[2,64,256,128]{3,2,1,0:T(8,128)(2,1)S(1)}, bf16[2,64,128,128]{3,2,1,0:T(8,128)(2,1)S(1)}, f32[8,128]{1,0:T(8,128)S(1)}) custom-call(bf16[2,64,256,128]{3,2,1,0:T(8,128)(2,1)} %bitcast.6), custom_call_target="tpu_custom_call" | custom-call | flops 16777216 | bytes 20971520 | tf_op jit(solution)/shard_map/open/pallas_call | solution.py:216
  5.1 3.3 %collective-permute-start = (f32[8,128]{1,0:T(8,128)S(1)}, f32[8,128]{1,0:T(8,128)S(1)}, u32[]{:S(2)}, u32[]{:S(2)}) collective-permute-start(f32[8,128]{1,0:T(8,128)S(1)} %get-tuple-element.21.after.one_ref), channel_id=1, source_target_pairs={{0,1},{1,0},{2,3},{3,2},{4,5},{5,4},{6,7},{7,6},{8,9},{9,8},{10,11... | collective-permute-start | bytes 12296 | tf_op jit(solution)/shard_map/ppermute | solution.py:781
  8.4 0.6 scalars.1.after.info
  9.0 1.3 %collective-permute-done.two_ref = f32[8,128]{1,0:T(8,128)S(1)} collective-permute-done((f32[8,128]{1,0:T(8,128)S(1)}, f32[8,128]{1,0:T(8,128)S(1)}, u32[]{:S(2)}, u32[]{:S(2)}) %collective-permute-start) | collective-permute-done | bytes 4128 | tf_op jit(solution)/shard_map/ppermute | solution.py:781
  10.3 7.3 %collective-permute-start.1 = (f32[8,128]{1,0:T(8,128)S(1)}, f32[8,128]{1,0:T(8,128)S(1)}, u32[]{:S(2)}, u32[]{:S(2)}) collective-permute-start(f32[8,128]{1,0:T(8,128)S(1)} %add.13.own_ref), channel_id=1, source_target_pairs={{2,4},{6,8},{10,12},{14,16},{18,20},{22,24},{26,28},{30,32},{34,36... | collective-permute-start | bytes 12296 | tf_op jit(solution)/shard_map/ppermute | solution.py:783
  17.6 3.1 %inner_round.3 = (f32[8,128]{1,0:T(8,128)S(1)}, f32[64,128]{1,0:T(8,128)S(1)}, f32[128,128]{1,0:T(8,128)S(1)}) custom-call(s32[8,128]{1,0:T(8,128)S(1)} %scalars.1.after.info, f32[8,128]{1,0:T(8,128)S(1)} %add.13.own_ref, f32[8,128]{1,0:T(8,128)S(1)} %collective-permute-done.2.mate_ref, bf16[2,64,128,128]{3,2,1,0:T(8,128)(2,1)S(1)} %get-tuple-element.22.s_ref), custom_call_target="tpu_custom_call" | custom-call | flops 8388608 | bytes 4194304 | tf_op jit(solution)/shard_map/inner_round/pallas_call | solution.py:409
  21.2 2.9 %collective-permute-start.3 = (f32[8,128]{1,0:T(8,128)S(1)}, f32[8,128]{1,0:T(8,128)S(1)}, u32[]{:S(2)}, u32[]{:S(2)}) collective-permute-start(f32[8,128]{1,0:T(8,128)S(1)} %outer_round.3), channel_id=1, source_target_pairs={{0,1},{1,0},{2,3},{3,2},{4,5},{5,4},{6,7},{7,6},{8,9},{9,8},{10,11... | collective-permute-start | bytes 12296 | tf_op jit(solution)/shard_map/ppermute | solution.py:781
  24.1 2.2 %collective-permute-done.3 = f32[8,128]{1,0:T(8,128)S(1)} collective-permute-done((f32[8,128]{1,0:T(8,128)S(1)}, f32[8,128]{1,0:T(8,128)S(1)}, u32[]{:S(2)}, u32[]{:S(2)}) %collective-permute-start.3) | collective-permute-done | bytes 4128 | tf_op jit(solution)/shard_map/ppermute | solution.py:781
  26.3 3.7 %collective-permute-start.4 = (f32[8,128]{1,0:T(8,128)S(1)}, f32[8,128]{1,0:T(8,128)S(1)}, u32[]{:S(2)}, u32[]{:S(2)}) collective-permute-start(f32[8,128]{1,0:T(8,128)S(1)} %add.10.own_ref), channel_id=1, source_target_pairs={{2,4},{6,8},{10,12},{14,16},{18,20},{22,24},{26,28},{30,32},{34,36... | collective-permute-start | bytes 12296 | tf_op jit(solution)/shard_map/ppermute | solution.py:783
  30.0 3.1 %inner_round.4 = (f32[8,128]{1,0:T(8,128)S(1)}, f32[64,128]{1,0:T(8,128)S(1)}, f32[128,128]{1,0:T(8,128)S(1)}) custom-call(s32[8,128]{1,0:T(8,128)S(1)} %scalars.1.after.info, f32[8,128]{1,0:T(8,128)S(1)} %add.10.own_ref, f32[8,128]{1,0:T(8,128)S(1)} %collective-permute-done.5.mate_ref, bf16[2,64,128,128]{3,2,1,0:T(8,128)(2,1)S(1)} %get-tuple-element.22.s_ref), custom_call_target="tpu_custom_call" | custom-call | flops 8388608 | bytes 4194304 | tf_op jit(solution)/shard_map/inner_round/pallas_call | solution.py:409
  33.1 1.1 %collective-permute-done.4.side_ref = f32[8,128]{1,0:T(8,128)S(1)} collective-permute-done((f32[8,128]{1,0:T(8,128)S(1)}, f32[8,128]{1,0:T(8,128)S(1)}, u32[]{:S(2)}, u32[]{:S(2)}) %collective-permute-start.4) | collective-permute-done | bytes 4128 | tf_op jit(solution)/shard_map/ppermute | solution.py:783
  34.6 2.9 %collective-permute-start.6 = (f32[8,128]{1,0:T(8,128)S(1)}, f32[8,128]{1,0:T(8,128)S(1)}, u32[]{:S(2)}, u32[]{:S(2)}) collective-permute-start(f32[8,128]{1,0:T(8,128)S(1)} %outer_round.4), channel_id=1, source_target_pairs={{0,1},{1,0},{2,3},{3,2},{4,5},{5,4},{6,7},{7,6},{8,9},{9,8},{10,11... | collective-permute-start | bytes 12296 | tf_op jit(solution)/shard_map/ppermute | solution.py:781
  37.5 2.2 %collective-permute-done.6 = f32[8,128]{1,0:T(8,128)S(1)} collective-permute-done((f32[8,128]{1,0:T(8,128)S(1)}, f32[8,128]{1,0:T(8,128)S(1)}, u32[]{:S(2)}, u32[]{:S(2)}) %collective-permute-start.6) | collective-permute-done | bytes 4128 | tf_op jit(solution)/shard_map/ppermute | solution.py:781
  39.7 2.6 %collective-permute-start.7 = (f32[8,128]{1,0:T(8,128)S(1)}, f32[8,128]{1,0:T(8,128)S(1)}, u32[]{:S(2)}, u32[]{:S(2)}) collective-permute-start(f32[8,128]{1,0:T(8,128)S(1)} %add.11.own_ref), channel_id=1, source_target_pairs={{2,4},{6,8},{10,12},{14,16},{18,20},{22,24},{26,28},{30,32},{34,36... | collective-permute-start | bytes 12296 | tf_op jit(solution)/shard_map/ppermute | solution.py:783
  42.3 3.1 %inner_round.5 = (f32[8,128]{1,0:T(8,128)S(1)}, f32[64,128]{1,0:T(8,128)S(1)}, f32[128,128]{1,0:T(8,128)S(1)}) custom-call(s32[8,128]{1,0:T(8,128)S(1)} %scalars.1.after.info, f32[8,128]{1,0:T(8,128)S(1)} %add.11.own_ref, f32[8,128]{1,0:T(8,128)S(1)} %collective-permute-done.8.mate_ref, bf16[2,64,128,128]{3,2,1,0:T(8,128)(2,1)S(1)} %get-tuple-element.22.s_ref), custom_call_target="tpu_custom_call" | custom-call | flops 8388608 | bytes 4194304 | tf_op jit(solution)/shard_map/inner_round/pallas_call | solution.py:409
  45.5 2.1 %collective-permute-done.7.side_ref = f32[8,128]{1,0:T(8,128)S(1)} collective-permute-done((f32[8,128]{1,0:T(8,128)S(1)}, f32[8,128]{1,0:T(8,128)S(1)}, u32[]{:S(2)}, u32[]{:S(2)}) %collective-permute-start.7) | collective-permute-done | bytes 4128 | tf_op jit(solution)/shard_map/ppermute | solution.py:783
  48.0 2.9 %collective-permute-start.9 = (f32[8,128]{1,0:T(8,128)S(1)}, f32[8,128]{1,0:T(8,128)S(1)}, u32[]{:S(2)}, u32[]{:S(2)}) collective-permute-start(f32[8,128]{1,0:T(8,128)S(1)} %outer_round.5), channel_id=1, source_target_pairs={{0,1},{1,0},{2,3},{3,2},{4,5},{5,4},{6,7},{7,6},{8,9},{9,8},{10,11... | collective-permute-start | bytes 12296 | tf_op jit(solution)/shard_map/ppermute | solution.py:781
  50.9 2.2 %collective-permute-done.9 = f32[8,128]{1,0:T(8,128)S(1)} collective-permute-done((f32[8,128]{1,0:T(8,128)S(1)}, f32[8,128]{1,0:T(8,128)S(1)}, u32[]{:S(2)}, u32[]{:S(2)}) %collective-permute-start.9) | collective-permute-done | bytes 4128 | tf_op jit(solution)/shard_map/ppermute | solution.py:781
  53.1 2.4 %collective-permute-start.11 = (f32[8,128]{1,0:T(8,128)S(1)}, f32[8,128]{1,0:T(8,128)S(1)}, u32[]{:S(2)}, u32[]{:S(2)}) collective-permute-start(f32[8,128]{1,0:T(8,128)S(1)} %add.12.after.own_ref), channel_id=1, source_target_pairs={{2,4},{6,8},{10,12},{14,16},{18,20},{22,24},{26,28},{30,32},{34,36... | collective-permute-start | bytes 12296 | tf_op jit(solution)/shard_map/ppermute | solution.py:783
  55.6 2.4 %flatten.1.d_ref = bf16[2,64,128,256]{3,2,1,0:T(8,128)(2,1)S(1)} custom-call(f32[8,128]{1,0:T(8,128)S(1)} %add.12.after.own_ref, bf16[2,64,256,128]{3,2,1,0:T(8,128)(2,1)S(1)} %get-tuple-element.32.x_ref), custom_call_target="tpu_custom_call" | custom-call | flops 8388608 | bytes 16777216 | tf_op jit(solution)/shard_map/flatten/pallas_call | solution.py:253
  58.0 3.1 %collective-permute-done.11.side_ref = f32[8,128]{1,0:T(8,128)S(1)} collective-permute-done((f32[8,128]{1,0:T(8,128)S(1)}, f32[8,128]{1,0:T(8,128)S(1)}, u32[]{:S(2)}, u32[]{:S(2)}) %collective-permute-start.11) | collective-permute-done | bytes 4128 | tf_op jit(solution)/shard_map/ppermute | solution.py:783
  61.1 1.8 %gram_to_send.1.after = f32[264,128]{1,0:T(8,128)S(1)} custom-call(s32[8,128]{1,0:T(8,128)S(1)} %scalars.1.after.info, f32[8,128]{1,0:T(8,128)S(1)} %add.12.after.own_ref, f32[8,128]{1,0:T(8,128)S(1)} %collective-permute-done.10.mate_ref, f32[8,128]{1,0:T(8,128)S(1)} %collective-permute-done.11.side_ref, bf16[2,64,128,256]{3,2,1,0:T(8,128)(2,1)S(1)} %flatten.1.d_ref), custom_call_target="tpu_custom_call" | custom-call | flops 1073741824 | bytes 4194304 | tf_op jit(solution)/shard_map/gram_to_send/pallas_call | solution.py:494
  62.9 3.2 %collective-permute-start.12 = (f32[264,128]{1,0:T(8,128)S(1)}, f32[264,128]{1,0:T(8,128)S(1)}, u32[]{:S(2)}, u32[]{:S(2)}) collective-permute-start(f32[264,128]{1,0:T(8,128)S(1)} %gram_to_send.1.after), channel_id=1, source_target_pairs={{0,1},{1,0},{2,3},{3,2},{4,5},{5,4},{6,7},{7,6},{8,9},{9,8},{10,11... | collective-permute-start | bytes 405512 | tf_op jit(solution)/shard_map/ppermute | solution.py:787
  66.1 1.8 %gram_to_keep.1 = (f32[3,128,128]{2,1,0:T(8,128)S(1)}, f32[3,2,128]{2,1,0:T(2,128)}) custom-call(s32[8,128]{1,0:T(8,128)S(1)} %scalars.1.after.info, f32[8,128]{1,0:T(8,128)S(1)} %add.12.after.own_ref, f32[8,128]{1,0:T(8,128)S(1)} %collective-permute-done.10.mate_ref, f32[8,128]{1,0:T(8,128)S(1)} %collective-permute-done.11.side_ref, ...), custom_call_target="tpu_custom_call" | custom-call | flops 1073741824 | bytes 4194304 | tf_op jit(solution)/shard_map/gram_to_keep/pallas_call | solution.py:494
  67.9 1.8 %collective-permute-done.12.got_ref = f32[264,128]{1,0:T(8,128)S(1)} collective-permute-done((f32[264,128]{1,0:T(8,128)S(1)}, f32[264,128]{1,0:T(8,128)S(1)}, u32[]{:S(2)}, u32[]{:S(2)}) %collective-permute-start.12) | collective-permute-done | bytes 135200 | tf_op jit(solution)/shard_map/ppermute | solution.py:787
  69.7 5.1 %root.1 = (f32[256,256]{1,0:T(8,128)S(1)}, f32[256,256]{1,0:T(8,128)S(1)}) custom-call(f32[3,128,128]{2,1,0:T(8,128)S(1)} %get-tuple-element.33.keep_ref, f32[264,128]{1,0:T(8,128)S(1)} %collective-permute-done.12.got_ref), custom_call_target="tpu_custom_call" | custom-call | flops 2214592512 | bytes 1048576 | tf_op jit(solution)/shard_map/root/pallas_call | solution.py:583
  75.0 1.5 %collective-permute-done.13.other_ref = f32[256,256]{1,0:T(8,128)S(1)} collective-permute-done((f32[256,256]{1,0:T(8,128)S(1)}, f32[256,256]{1,0:T(8,128)S(1)}, u32[]{:S(2)}, u32[]{:S(2)}) %collective-permute-start.13) | collective-permute-done | bytes 262176 | tf_op jit(solution)/shard_map/ppermute | solution.py:790
  76.5 4.3 %truncate.1.pack_ref.after = bf16[272,256]{1,0:T(8,128)(2,1)S(1)} custom-call(s32[8,128]{1,0:T(8,128)S(1)} %scalars.1.after.info, f32[4,4]{1,0:T(4,128)S(1)} %copy-done.3, f32[8,128]{1,0:T(8,128)S(1)} %add.12.after.own_ref, f32[8,128]{1,0:T(8,128)S(1)} %collective-permute-done.10.mate_ref, f32[256,256]{1,0:T(8,128)S(1)} %get-tuple-element.34.upper_ref, ...), custom_call_target="tpu_custom_call" | custom-call | flops 1342177280 | bytes 1572864 | tf_op jit(solution)/shard_map/truncate/pallas_call | solution.py:674
  80.8 3.0 %collective-permute-start.14 = (bf16[272,256]{1,0:T(8,128)(2,1)S(1)}, bf16[272,256]{1,0:T(8,128)(2,1)S(1)}, u32[]{:S(2)}, u32[]{:S(2)}) collective-permute-start(bf16[272,256]{1,0:T(8,128)(2,1)S(1)} %truncate.1.pack_ref.after), channel_id=1, source_target_pairs={{0,1},{1,0},{2,3},{3,2},{4,5},{5,4},{6,7},{7,6},{8,9},{9,8},{10,11... | collective-permute-start | bytes 417800 | tf_op jit(solution)/shard_map/ppermute | solution.py:792
  83.8 2.7 %update_own.1.begun_hbm = bf16[2,64,256,128]{3,2,1,0:T(8,128)(2,1)} custom-call(s32[8,128]{1,0:T(8,128)S(1)} %scalars.1.after.info, bf16[272,256]{1,0:T(8,128)(2,1)S(1)} %truncate.1.pack_ref.after, bf16[2,64,128,256]{3,2,1,0:T(8,128)(2,1)S(1)} %flatten.1.d_ref, bf16[272,256]{1,0:T(8,128)(2,1)S(1)} %truncate.1.pack_ref.after), custom_call_target="tpu_custom_call" | custom-call | flops 1073741824 | bytes 8388608 | tf_op jit(solution)/shard_map/update_own/pallas_call | solution.py:738
  86.5 1.6 %collective-permute-done.14.got_ref = bf16[272,256]{1,0:T(8,128)(2,1)S(1)} collective-permute-done((bf16[272,256]{1,0:T(8,128)(2,1)S(1)}, bf16[272,256]{1,0:T(8,128)(2,1)S(1)}, u32[]{:S(2)}, u32[]{:S(2)}) %collective-permute-start.14) | collective-permute-done | bytes 139296 | tf_op jit(solution)/shard_map/ppermute | solution.py:792
  88.1 2.7 %update_other.1 = (bf16[2,64,256,128]{3,2,1,0:T(8,128)(2,1)}, f32[2,128]{1,0:T(2,128)}) custom-call(s32[8,128]{1,0:T(8,128)S(1)} %scalars.1.after.info, bf16[272,256]{1,0:T(8,128)(2,1)S(1)} %truncate.1.pack_ref.after, bf16[272,256]{1,0:T(8,128)(2,1)S(1)} %collective-permute-done.14.got_ref, ...), custom_call_target="tpu_custom_call", output_to_operand_aliasing={{0}: (4, {})} | custom-call | flops 1073741824 | bytes 8388608 | tf_op jit(solution)/shard_map/update_other/pallas_call | solution.py:738
  (25 shorter events, 1.3 us)
Async XLA Ops:
  0.6 7.7 %copy-start.1 = (s32[128]{0:T(128)S(1)}, s32[128]{0:T(128)}, u32[]{:S(2)}) copy-start(s32[128]{0:T(128)} %ranks.1) | copy-start | bytes 1540
  0.6 7.7 %copy-start = (s32[128,3]{0,1:T(4,128)S(1)}, s32[128,3]{0,1:T(4,128)}, u32[]{:S(2)}) copy-start(s32[128,3]{0,1:T(4,128)} %param.6) | copy-start | bytes 4612
  5.1 5.2 %collective-permute-start = (f32[8,128]{1,0:T(8,128)S(1)}, f32[8,128]{1,0:T(8,128)S(1)}, u32[]{:S(2)}, u32[]{:S(2)}) collective-permute-start(f32[8,128]{1,0:T(8,128)S(1)} %get-tuple-element.21.after.one_ref), channel_id=1, source_target_pairs={{0,1},{1,0},{2,3},{3,2},{4,5},{5,4},{6,7},{7,6},{8,9},{9,8},{10,11... | collective-permute-start | bytes 12296 | tf_op jit(solution)/shard_map/ppermute | solution.py:781
  10.3 7.3 %collective-permute-start.2 = (f32[8,128]{1,0:T(8,128)S(1)}, f32[8,128]{1,0:T(8,128)S(1)}, u32[]{:S(2)}, u32[]{:S(2)}) collective-permute-start(f32[8,128]{1,0:T(8,128)S(1)} %add.13.own_ref), channel_id=1, source_target_pairs={{0,2},{2,0},{4,6},{6,4},{8,10},{10,8},{12,14},{14,12},{16,18},{18,... | collective-permute-start | bytes 12296 | tf_op jit(solution)/shard_map/ppermute | solution.py:784
  10.3 10.5 %collective-permute-start.1 = (f32[8,128]{1,0:T(8,128)S(1)}, f32[8,128]{1,0:T(8,128)S(1)}, u32[]{:S(2)}, u32[]{:S(2)}) collective-permute-start(f32[8,128]{1,0:T(8,128)S(1)} %add.13.own_ref), channel_id=1, source_target_pairs={{2,4},{6,8},{10,12},{14,16},{18,20},{22,24},{26,28},{30,32},{34,36... | collective-permute-start | bytes 12296 | tf_op jit(solution)/shard_map/ppermute | solution.py:783
  21.2 5.1 %collective-permute-start.3 = (f32[8,128]{1,0:T(8,128)S(1)}, f32[8,128]{1,0:T(8,128)S(1)}, u32[]{:S(2)}, u32[]{:S(2)}) collective-permute-start(f32[8,128]{1,0:T(8,128)S(1)} %outer_round.3), channel_id=1, source_target_pairs={{0,1},{1,0},{2,3},{3,2},{4,5},{5,4},{6,7},{7,6},{8,9},{9,8},{10,11... | collective-permute-start | bytes 12296 | tf_op jit(solution)/shard_map/ppermute | solution.py:781
  26.3 3.7 %collective-permute-start.5 = (f32[8,128]{1,0:T(8,128)S(1)}, f32[8,128]{1,0:T(8,128)S(1)}, u32[]{:S(2)}, u32[]{:S(2)}) collective-permute-start(f32[8,128]{1,0:T(8,128)S(1)} %add.10.own_ref), channel_id=1, source_target_pairs={{0,2},{2,0},{4,6},{6,4},{8,10},{10,8},{12,14},{14,12},{16,18},{18,... | collective-permute-start | bytes 12296 | tf_op jit(solution)/shard_map/ppermute | solution.py:784
  26.3 7.9 %collective-permute-start.4 = (f32[8,128]{1,0:T(8,128)S(1)}, f32[8,128]{1,0:T(8,128)S(1)}, u32[]{:S(2)}, u32[]{:S(2)}) collective-permute-start(f32[8,128]{1,0:T(8,128)S(1)} %add.10.own_ref), channel_id=1, source_target_pairs={{2,4},{6,8},{10,12},{14,16},{18,20},{22,24},{26,28},{30,32},{34,36... | collective-permute-start | bytes 12296 | tf_op jit(solution)/shard_map/ppermute | solution.py:783
  34.6 5.1 %collective-permute-start.6 = (f32[8,128]{1,0:T(8,128)S(1)}, f32[8,128]{1,0:T(8,128)S(1)}, u32[]{:S(2)}, u32[]{:S(2)}) collective-permute-start(f32[8,128]{1,0:T(8,128)S(1)} %outer_round.4), channel_id=1, source_target_pairs={{0,1},{1,0},{2,3},{3,2},{4,5},{5,4},{6,7},{7,6},{8,9},{9,8},{10,11... | collective-permute-start | bytes 12296 | tf_op jit(solution)/shard_map/ppermute | solution.py:781
  39.7 2.6 %collective-permute-start.8 = (f32[8,128]{1,0:T(8,128)S(1)}, f32[8,128]{1,0:T(8,128)S(1)}, u32[]{:S(2)}, u32[]{:S(2)}) collective-permute-start(f32[8,128]{1,0:T(8,128)S(1)} %add.11.own_ref), channel_id=1, source_target_pairs={{0,2},{2,0},{4,6},{6,4},{8,10},{10,8},{12,14},{14,12},{16,18},{18,... | collective-permute-start | bytes 12296 | tf_op jit(solution)/shard_map/ppermute | solution.py:784
  39.7 7.9 %collective-permute-start.7 = (f32[8,128]{1,0:T(8,128)S(1)}, f32[8,128]{1,0:T(8,128)S(1)}, u32[]{:S(2)}, u32[]{:S(2)}) collective-permute-start(f32[8,128]{1,0:T(8,128)S(1)} %add.11.own_ref), channel_id=1, source_target_pairs={{2,4},{6,8},{10,12},{14,16},{18,20},{22,24},{26,28},{30,32},{34,36... | collective-permute-start | bytes 12296 | tf_op jit(solution)/shard_map/ppermute | solution.py:783
  48.0 5.1 %collective-permute-start.9 = (f32[8,128]{1,0:T(8,128)S(1)}, f32[8,128]{1,0:T(8,128)S(1)}, u32[]{:S(2)}, u32[]{:S(2)}) collective-permute-start(f32[8,128]{1,0:T(8,128)S(1)} %outer_round.5), channel_id=1, source_target_pairs={{0,1},{1,0},{2,3},{3,2},{4,5},{5,4},{6,7},{7,6},{8,9},{9,8},{10,11... | collective-permute-start | bytes 12296 | tf_op jit(solution)/shard_map/ppermute | solution.py:781
  53.1 8.0 %collective-permute-start.11 = (f32[8,128]{1,0:T(8,128)S(1)}, f32[8,128]{1,0:T(8,128)S(1)}, u32[]{:S(2)}, u32[]{:S(2)}) collective-permute-start(f32[8,128]{1,0:T(8,128)S(1)} %add.12.after.own_ref), channel_id=1, source_target_pairs={{2,4},{6,8},{10,12},{14,16},{18,20},{22,24},{26,28},{30,32},{34,36... | collective-permute-start | bytes 12296 | tf_op jit(solution)/shard_map/ppermute | solution.py:783
  55.5 5.6 %collective-permute-start.10 = (f32[8,128]{1,0:T(8,128)S(1)}, f32[8,128]{1,0:T(8,128)S(1)}, u32[]{:S(2)}, u32[]{:S(2)}) collective-permute-start(f32[8,128]{1,0:T(8,128)S(1)} %add.12.after.own_ref), channel_id=1, source_target_pairs={{0,2},{2,0},{4,6},{6,4},{8,10},{10,8},{12,14},{14,12},{16,18},{18,... | collective-permute-start | bytes 12296 | tf_op jit(solution)/shard_map/ppermute | solution.py:784
  62.9 13.6 %copy-start.2 = (f32[512,128]{1,0:T(8,128)S(1)}, f32[512,128]{1,0:T(8,128)}, u32[]{:S(2)}) copy-start(f32[512,128]{1,0:T(8,128)} %probes_ref.1) | copy-start | bytes 786436
  62.9 13.5 %copy-start.3 = (f32[4,4]{1,0:T(4,128)S(1)}, f32[4,4]{1,0:T(4,128)}, u32[]{:S(2)}) copy-start(f32[4,4]{1,0:T(4,128)} %gate.1) | copy-start | bytes 196
  62.9 6.8 %collective-permute-start.12 = (f32[264,128]{1,0:T(8,128)S(1)}, f32[264,128]{1,0:T(8,128)S(1)}, u32[]{:S(2)}, u32[]{:S(2)}) collective-permute-start(f32[264,128]{1,0:T(8,128)S(1)} %gram_to_send.1.after), channel_id=1, source_target_pairs={{0,1},{1,0},{2,3},{3,2},{4,5},{5,4},{6,7},{7,6},{8,9},{9,8},{10,11... | collective-permute-start | bytes 405512 | tf_op jit(solution)/shard_map/ppermute | solution.py:787
  74.9 1.6 %collective-permute-start.13 = (f32[256,256]{1,0:T(8,128)S(1)}, f32[256,256]{1,0:T(8,128)S(1)}, u32[]{:S(2)}, u32[]{:S(2)}) collective-permute-start(f32[256,256]{1,0:T(8,128)S(1)} %get-tuple-element.34.upper_ref), channel_id=1, source_target_pairs={{0,2},{2,0},{4,6},{6,4},{8,10},{10,8},{12,14},{14,12},{16,18},{18,... | collective-permute-start | bytes 786440 | tf_op jit(solution)/shard_map/ppermute | solution.py:790
  80.8 7.3 %collective-permute-start.14 = (bf16[272,256]{1,0:T(8,128)(2,1)S(1)}, bf16[272,256]{1,0:T(8,128)(2,1)S(1)}, u32[]{:S(2)}, u32[]{:S(2)}) collective-permute-start(bf16[272,256]{1,0:T(8,128)(2,1)S(1)} %truncate.1.pack_ref.after), channel_id=1, source_target_pairs={{0,1},{1,0},{2,3},{3,2},{4,5},{5,4},{6,7},{7,6},{8,9},{9,8},{10,11... | collective-permute-start | bytes 417800 | tf_op jit(solution)/shard_map/ppermute | solution.py:792
